TPU v7x, 128 devices: a whole 4x4x4 slice. The times are simulated.
128 devices in a mesh: ctx: 16 (over z, x), exp: 4 (over y), dp: 2 (over core).
Axes of the slice: x: 4, y: 4, z: 4, core: 2. Of those that a mesh axis runs over, the one named last changes fastest.
Arguments:
- mixer_in: bfloat16 [2, 4096, 4096], P('dp', 'ctx', 'exp'), may hold values from -6 to 6
- gate_in: bfloat16 [2, 4096, 4096], P('dp', 'ctx', 'exp'), may hold values from -6 to 6
- state_write: bfloat16 [2, 4096, 4, 128], P('dp', 'ctx', 'exp'), may hold values from -0.5 to 0.5
- state_read: bfloat16 [2, 4096, 4, 128], P('dp', 'ctx', 'exp'), may hold values from -0.5 to 0.5
- decay_rate: float32 [2, 64, 4096], P('dp', 'exp', 'ctx'), may hold values from 0 to 1, as said below
- skip_gain: float32 [64], P('exp'), may hold values from 0.5 to 1.5
- norm_gain: float32 [4096], P('exp'), may hold values from 0.5 to 1.5
- start_state: float32 [2, 64, 64, 128], P('dp', 'exp'), may hold values from -12 to 12
- out_weight: bfloat16 [4096, 4096], P('exp'), may hold values from -0.09375 to 0.09375
- residual: bfloat16 [2, 4096, 4096], P('dp', ('ctx', 'exp')), may hold values from -6 to 6
- router_weight: bfloat16 [4096, 8], replicated, may hold values from -0.09375 to 0.09375
- chosen: int32 [2, 4096, 2], P('dp', ('ctx', 'exp')), may hold values from 0 to 7, as said below
- slot_index: int32 [2, 4096, 2], P('dp', ('ctx', 'exp')), may hold values from -1 to 13, as said below
- spill_index: int32 [2, 4096, 2], P('dp', ('ctx', 'exp')), may hold values from -1 to 15, as said below
- gate_weight: bfloat16 [8, 4096, 8192], P(('exp', 'dp'), None, 'ctx'), may hold values from -0.09375 to 0.09375
- up_weight: bfloat16 [8, 4096, 8192], P(('exp', 'dp'), None, 'ctx'), may hold values from -0.09375 to 0.09375
- down_weight: bfloat16 [8, 4096, 8192], P(('exp', 'dp'), None, 'ctx'), may hold values from -0.125 to 0.125
Outputs:
- layer_out: bfloat16 [2, 4096, 4096], P('dp', ('ctx', 'exp'))
Inputs may be any that keep to these rules, and one draw needn't show every extreme that they name: `decay_rate`: positive. `chosen`: two different experts per token. `slot_index`: the rank of the assignment among the assignments of the same device to the same expert, in the order of affinity, where that rank is below 14; -1 otherwise; distinct per device and expert. `spill_index`: -1 where slot_index is 0 or more or the assignment is dropped; else target expert * 2 + a row below 2, distinct per device and target.
All inputs are finite; a program needn't handle non-finite values.
Results may differ from a plain program's by a relative error of at most 0.03.
Values may be sent and summed in bfloat16 or wider, within the bound.
A program may use at most 192 MiB of HBM per device.

v0:
```python
import jax
import jax.numpy as jnp
from jax import lax
from jax.sharding import PartitionSpec as P

D = 4096
EXPERTS = 8
CAP = 14
SPILL = 2
BLOCK = 16


def entering_2(value, axis, combine, identity):
    length, here = (lax.axis_size(axis), lax.axis_index(axis))
    everything = jax.tree.map(
        lambda part, kind: lax.all_gather(part.astype(kind), axis),
        value,
        (jnp.bfloat16, jnp.bfloat16),
    )
    start = jax.tree.map(
        lambda part, zero: jnp.broadcast_to(jnp.asarray(zero, part.dtype), part.shape),
        value,
        identity,
    )

    def hop(k, before):
        reached = k < here
        new = combine(
            before, jax.tree.map(lambda part, own: part[k].astype(own.dtype), everything, value)
        )
        return jax.tree.map(lambda a, b: jnp.where(reached, a, b), new, before)

    return lax.fori_loop(0, length, hop, start)


def chain_combine(earlier, later):
    return (earlier[0] * later[0], later[0][:, None, None] * earlier[1] + later[1])


def ffn_rows(flat_rows, gate_w, up_w, down_w):
    gate_val = jnp.dot(flat_rows, gate_w, preferred_element_type=jnp.float32)
    up_val = jnp.dot(flat_rows, up_w, preferred_element_type=jnp.float32)
    activated = (jax.nn.silu(gate_val) * up_val).astype(jnp.bfloat16)
    return lax.dot_general(
        activated, down_w, (((1,), (1,)), ((), ())), preferred_element_type=jnp.float32
    )


def shards(
    mixer_in,
    gate_in,
    state_write,
    state_read,
    decay_rate,
    skip_gain,
    norm_gain,
    start_state,
    out_weight,
    residual,
    router_weight,
    chosen,
    slot_index,
    spill_index,
    gate_weight,
    up_weight,
    down_weight,
):
    exact = lax.Precision.HIGHEST
    length = mixer_in.shape[1]
    head_count = skip_gain.shape[0]
    inner_width = mixer_in.shape[2]
    head_size = inner_width // head_count
    inputs = mixer_in[0].astype(jnp.float32).reshape(length, head_count, head_size)
    write_rows = state_write[0, :, 0].astype(jnp.float32)
    read_rows = state_read[0, :, 0].astype(jnp.float32)
    levels = jnp.cumsum(decay_rate[0], axis=1)
    locations = jnp.arange(length)
    causal = locations[:, None] >= locations[None, :]
    span_levels = levels[:, :, None] - levels[:, None, :]
    decay_pairs = jnp.where(causal[None], jnp.exp(-jnp.where(causal[None], span_levels, 0.0)), 0.0)
    intersections = jnp.dot(read_rows, write_rows.T, precision=exact)
    within = jnp.einsum("hts,shp->thp", decay_pairs * intersections[None], inputs, precision=exact)
    to_end = jnp.exp(levels - levels[:, -1:])
    local_state = jnp.einsum("hs,shp,sn->hpn", to_end, inputs, write_rows, precision=exact)
    totals = jnp.exp(-levels[:, -1])
    before_decay, before_state = entering_2(
        (totals, local_state),
        "ctx",
        chain_combine,
        (jnp.ones_like(totals), jnp.zeros_like(local_state)),
    )
    entering = before_decay[:, None, None] * start_state[0] + before_state
    carried = (
        jnp.einsum("tn,hpn->thp", read_rows, entering, precision=exact)
        * jnp.exp(-levels).T[:, :, None]
    )
    head_out = within + carried + skip_gain[None, :, None] * inputs
    gated_out = head_out.reshape(length, inner_width) * jax.nn.silu(gate_in[0].astype(jnp.float32))
    normed = (
        gated_out
        * lax.rsqrt(jnp.mean(gated_out * gated_out, axis=1, keepdims=True) + 1e-05)
        * norm_gain
    ).astype(jnp.bfloat16)
    mixer_out = lax.psum_scatter(
        jnp.dot(normed, out_weight, preferred_element_type=jnp.float32).astype(jnp.bfloat16),
        "exp",
        scatter_dimension=0,
        tiled=True,
    ).astype(jnp.float32)
    hidden = (residual[0].astype(jnp.float32) + mixer_out).astype(jnp.bfloat16)
    logits = jnp.dot(hidden, router_weight, preferred_element_type=jnp.float32)
    expert_ids = chosen[0]
    matches = expert_ids[:, :, None] == jnp.arange(EXPERTS)[None, None, :]
    picked = jnp.sum(jnp.where(matches, logits[:, None, :], 0.0), axis=2)
    shares = jax.nn.sigmoid(picked - picked[:, ::-1])
    slot_ids = slot_index[0]
    spill_ids = spill_index[0]
    target_row = jnp.where(
        slot_ids >= 0,
        expert_ids * BLOCK + slot_ids,
        jnp.where(spill_ids >= 0, spill_ids // SPILL * BLOCK + CAP + spill_ids % SPILL, -1),
    )
    onehot = target_row[:, :, None] == jnp.arange(EXPERTS * BLOCK)[None, None, :]
    placing = jnp.sum(onehot, axis=1).astype(jnp.bfloat16)
    outgoing = lax.dot_general(
        placing, hidden, (((0,), (0,)), ((), ())), preferred_element_type=jnp.float32
    )
    outgoing = outgoing.astype(jnp.bfloat16).reshape(EXPERTS, BLOCK, D)
    own_gate = gate_weight[0]
    own_up = up_weight[0]
    own_down = down_weight[0]

    def experts_round(buffer):
        arrived = lax.all_to_all(buffer, ("exp", "dp"), split_axis=0, concat_axis=0, tiled=True)
        part_rows = lax.all_gather(arrived, "ctx", axis=0, tiled=True)
        flat_rows = part_rows.reshape(-1, part_rows.shape[-1])
        partial_value = ffn_rows(flat_rows, own_gate, own_up, own_down).reshape(part_rows.shape)
        summed = lax.psum_scatter(
            partial_value.astype(jnp.bfloat16), "ctx", scatter_dimension=0, tiled=True
        )
        return lax.all_to_all(summed, ("exp", "dp"), split_axis=0, concat_axis=0, tiled=True)

    returned = jnp.concatenate(
        (experts_round(outgoing[:, :CAP]), experts_round(outgoing[:, CAP:])), axis=1
    )
    weighting = jnp.sum(jnp.where(onehot, shares[:, :, None], 0.0), axis=1)
    expert_sum = jnp.dot(
        weighting, returned.reshape(EXPERTS * BLOCK, D).astype(jnp.float32), precision=exact
    )
    return (hidden.astype(jnp.float32) + expert_sum).astype(jnp.bfloat16)[None]


def solution(mesh):
    placed = (
        P("dp", "ctx", "exp"),
        P("dp", "ctx", "exp"),
        P("dp", "ctx", "exp", None),
        P("dp", "ctx", "exp", None),
        P("dp", "exp", "ctx"),
        P("exp"),
        P("exp"),
        P("dp", "exp", None, None),
        P("exp", None),
        P("dp", ("ctx", "exp"), None),
        P(),
        P("dp", ("ctx", "exp"), None),
        P("dp", ("ctx", "exp"), None),
        P("dp", ("ctx", "exp"), None),
        P(("exp", "dp"), None, "ctx"),
        P(("exp", "dp"), None, "ctx"),
        P(("exp", "dp"), None, "ctx"),
    )
    return jax.shard_map(
        shards, mesh=mesh, in_specs=placed, out_specs=P("dp", ("ctx", "exp"), None), check_vma=False
    )
```

profile of v0, /device:TPU:1, one launch (start us, length us, event | category | flops | bytes accessed | tf_op | source)
XLA Modules:
  0.0 616.7 jit_solution(900796972803478497)
XLA Ops:
  6.5 0.8 reshape.195
  7.3 0.6 reduce-window.6
  7.9 0.2 slice_reduce_fusion
  8.2 0.2 slice_reduce_fusion.1
  8.5 1.2 copy.83
  9.7 2.2 convolution_convert_fusion.4
  12.0 1.4 fusion.71
  14.0 0.2 fusion.64
  14.2 0.2 dynamic-update-slice
  14.4 35.3 %all-reduce = bf16[256]{0:T(256)(128)(2,1)S(1)} all-reduce(bf16[256]{0:T(256)(128)(2,1)S(1)} %dynamic-update-slice), channel_id=2, replica_groups=mesh['ctx'=16,'exp'=4,'dp'=2] {'ctx'}, use_global_device_ids=true, to_apply=%add | all-reduce | flops 256 | bytes 1024
  49.8 1.2 copy.85
  51.1 1.0 fusion.60
  52.2 4.6 fusion.28
  56.7 10.4 %all-gather.10.cloned.1.call-done = bf16[256,64,128]{2,1,0:T(8,128)(2,1)} async-done(((bf16[16,64,128]{2,1,0:T(8,128)(2,1)}), bf16[256,64,128]{2,1,0:T(8,128)(2,1)}) %all-gather.10.cloned.1.call-update) | async-done | bytes 4194320 | tf_op jit(solution)/shard_map/all_gather | solution.py:16
  67.1 18.2 %while.16 = (s32[]{:T(128)}, f32[16]{0:T(128)S(1)}, f32[16,64,128]{2,1,0:T(8,128)S(1)}, s32[]{:T(128)}, bf16[16,16]{1,0:T(8,128)(2,1)S(1)}, /*index=5*/bf16[16,16,64,128]{3,2,1,0:T(8,128)(2,1)}, s32[]{:T(128)}, s32[]{:T(128)}) while((s32[]{:T(128)}, f32[16]{0:T(128)S(1)}, f32[16,64,128]{2,1,0:T(8,128)S(1)}, s32[]{:T(128)}, ...), condition=%wide.region_3.4_spmd.clone, body=%wide.region_2.3_spmd.clone.sunk | while | flops 655428 | bytes 1311123 | solution.py:33
  67.1 1.1 fusion.82
  68.2 1.1 fusion.82
  69.4 1.1 fusion.82
  70.5 1.1 fusion.82
  71.7 1.1 fusion.82
  72.8 1.1 fusion.82
  74.0 1.1 fusion.82
  75.1 1.1 fusion.82
  76.2 1.1 fusion.82
  77.4 1.1 fusion.82
  78.5 1.1 fusion.82
  79.7 1.1 fusion.82
  80.8 1.1 fusion.82
  81.9 1.1 fusion.82
  83.1 1.1 fusion.82
  84.2 1.1 fusion.82
  85.3 2.3 multiply_reduce_fusion
  87.6 0.3 copy.84
  88.0 7.5 %convolution_convert_fusion.1 = bf16[256,4096]{1,0:T(8,128)(2,1)} fusion(bf16[1024,4096]{1,0:T(8,128)(2,1)} %param.27, f32[256,1024]{1,0:T(8,128)S(1)} %copy.84, f32[1024]{0:T(1024)S(1)} %copy-done.11, f32[256]{0:T(256)S(1)} %add_rsqrt_fusion, bf16[1,256,1024]{2,1,0:T(8,128)(2,1)} %param.20), kind=kOutput, calls=%fused_computation.6 | convolution fusion | flops 2150891520 | bytes 12063744 | tf_op jit(solution)/shard_map/dot_general | solution.py:105
  95.8 29.1 %reduce-scatter.4.cloned.1.call-done = bf16[64,4096]{1,0:T(8,128)(2,1)} async-done(((bf16[256,4096]{1,0:T(8,128)(2,1)}), bf16[64,4096]{1,0:T(8,128)(2,1)}) %reduce-scatter.4.cloned.1.call-update) | async-done | bytes 524304 | tf_op jit(solution)/shard_map/reduce_scatter | solution.py:104
  124.9 1.5 convolution_convert_fusion.3
  126.6 9.0 %all_to_all.20 = bf16[8,2,4096]{2,1,0:T(2,128)(2,1)} all-to-all(bf16[8,2,4096]{2,1,0:T(2,128)(2,1)S(1)} %slice.24), channel_id=1, replica_groups=mesh['ctx'=16,'exp'=4,'dp'=2] {'exp','dp'}, dimensions={0} | all-to-all | bytes 262144 | tf_op jit(solution)/shard_map/all_to_all | solution.py:134
  135.6 18.3 %all_to_all.21 = bf16[8,14,4096]{2,1,0:T(8,128)(2,1)S(1)} all-to-all(bf16[8,14,4096]{2,1,0:T(8,128)(2,1)S(1)} %bitcast.152), channel_id=1, replica_groups=mesh['ctx'=16,'exp'=4,'dp'=2] {'exp','dp'}, dimensions={0} | all-to-all | bytes 1835008 | tf_op jit(solution)/shard_map/all_to_all | solution.py:134
  154.0 1.4 copy.86
  155.4 0.2 all-reduce.6.cloned.1.call-start
  155.7 23.9 %all-gather.8.cloned.1.call-done = bf16[128,2,4096]{2,1,0:T(2,128)(2,1)} async-done(((bf16[8,2,4096]{2,1,0:T(2,128)(2,1)}), bf16[128,2,4096]{2,1,0:T(2,128)(2,1)}) %all-gather.8.cloned.1.call-update) | async-done | bytes 2097168 | tf_op jit(solution)/shard_map/all_gather | solution.py:135
  179.5 2.7 reshape.201
  182.3 3.6 fusion.9
  185.9 1.3 fusion.37
  187.3 4.8 convolution_convert_fusion.2
  192.1 90.7 %all-gather.6.cloned.1.call-done = bf16[128,14,4096]{2,0,1:T(8,128)(2,1)} async-done(((bf16[8,14,4096]{2,0,1:T(8,128)(2,1)}), bf16[128,14,4096]{2,0,1:T(8,128)(2,1)}) %all-gather.6.cloned.1.call-update) | async-done | bytes 14680080 | tf_op jit(solution)/shard_map/all_gather | solution.py:135
  282.8 17.4 %copy.87 = bf16[128,14,4096]{2,1,0:T(8,128)(2,1)} copy(bf16[128,14,4096]{2,0,1:T(8,128)(2,1)} %all-gather.6.cloned.1.call-done) | data formatting | bytes 29360128 | tf_op jit(solution)/shard_map/all_gather | solution.py:135
  300.3 18.0 %reshape.200 = bf16[1792,4096]{1,0:T(8,128)(2,1)} reshape(bf16[128,14,4096]{2,1,0:T(8,128)(2,1)} %copy.87) | data formatting | bytes 29360128 | tf_op jit(solution)/shard_map/reshape | solution.py:136
  318.3 12.4 %fusion.11 = f32[1792,512]{1,0:T(8,128)S(1)} fusion(bf16[1792,4096]{1,0:T(8,128)(2,1)} %reshape.200, bf16[1,4096,512]{2,1,0:T(8,128)(2,1)} %param.33), kind=kOutput, calls=%fused_computation.20 | convolution fusion | flops 7516192768 | bytes 22544384 | tf_op jit(solution)/shard_map/dot_general | solution.py:41
  330.8 9.2 %multiply_convert_fusion = bf16[1792,512]{1,0:T(8,128)(2,1)} fusion(f32[1792,512]{1,0:T(8,128)S(1)} %fusion.11, bf16[1792,4096]{1,0:T(8,128)(2,1)S(1)} %copy-done.2, bf16[1,4096,512]{2,1,0:T(8,128)(2,1)S(1)} %copy-done.10), kind=kOutput, calls=%fused_computation.29 | convolution fusion | flops 7521697792 | bytes 24379392 | tf_op jit(solution)/shard_map/dot_general | solution.py:42
  340.0 2.5 dot_general.68
  342.5 13.5 %convolution_convert_fusion = bf16[128,14,4096]{2,0,1:T(8,128)(2,1)} fusion(bf16[1,4096,512]{2,1,0:T(8,128)(2,1)} %param.35, bf16[128,14,512]{2,1,0:T(8,128)(2,1)S(1)} %dot_general.68), kind=kOutput, calls=%fused_computation.5 | convolution fusion | flops 7523532800 | bytes 20709376 | tf_op jit(solution)/shard_map/dot_general | solution.py:44
  356.8 220.0 %all-reduce.6.cloned.1.call-done = (bf16[128,2,4096]{2,0,1:T(8,128)(2,1)}, bf16[128,14,4096]{2,0,1:T(8,128)(2,1)}) async-done(((bf16[128,2,4096]{2,0,1:T(8,128)(2,1)}, bf16[128,14,4096]{2,0,1:T(8,128)(2,1)}), (bf16[128,2,4096]{2,0,1:T(8,128)(2,1)}, bf16[128,14,4096]{2,0,1:T(8,128)(2,1)})) %all-reduce.6.cloned.1.call-update) | async-done | bytes 16777232
  576.7 0.9 constant_dynamic-slice_fusion
  577.7 0.8 copy.91
  578.4 5.3 all-to-all-start.3
  583.8 1.2 constant_dynamic-slice_fusion.1
  585.0 1.5 copy.89
  586.5 2.5 all-to-all-done.3
  589.0 4.3 all-to-all-start.1
  593.4 0.2 fusion.69
  593.8 14.7 %all-to-all-done.1 = bf16[8,14,4096]{2,1,0:T(8,128)(2,1)S(1)} async-done(((bf16[8,14,4096]{2,1,0:T(8,128)(2,1)}), bf16[8,14,4096]{2,1,0:T(8,128)(2,1)S(1)}, u32[]{:S(2)}, u32[]{:S(2)}) %all-to-all-start.1) | async-done | bytes 917536 | tf_op jit(solution)/shard_map/all_to_all | solution.py:141
  608.5 0.3 pad_maximum_fusion
  608.8 1.4 fusion.2
  (70 shorter events, 1.4 us)
Async XLA Ops:
  6.5 44.6 %copy-start = (bf16[1,256,1,128]{3,1,2,0:T(8,128)(2,1)S(1)}, bf16[1,256,1,128]{3,1,2,0:T(8,128)(2,1)}, u32[]{:S(2)}) copy-start(bf16[1,256,1,128]{3,1,2,0:T(8,128)(2,1)} %param.22) | copy-start | bytes 196612
  6.5 60.6 %all-gather.10.cloned.1.call-start = ((), (), s32[]{:S(2)}) async-start(), calls=%async_computation.8 | async-start | bytes 4456448 | tf_op jit(solution)/shard_map/all_gather | solution.py:16
  11.9 113.0 %reduce-scatter.4.cloned.1.call-start = ((), (), s32[]{:S(2)}) async-start(), calls=%async_computation.5 | async-start | bytes 2621440 | tf_op jit(solution)/shard_map/reduce_scatter | solution.py:104
  56.7 28.6 %copy-start.12 = (f32[16]{0:T(128)S(1)}, f32[16]{0:T(128)}, u32[]{:S(2)}) copy-start(f32[16]{0:T(128)} %param.24) | copy-start | bytes 196
  85.3 2.7 copy-start.11
  88.0 7.7 %copy-start.6 = (s32[1,64,2]{1,2,0:T(2,128)S(1)}, s32[1,64,2]{1,2,0:T(2,128)}, u32[]{:S(2)}) copy-start(s32[1,64,2]{1,2,0:T(2,128)} %param.30) | copy-start | bytes 1540
  88.0 7.7 %copy-start.7 = (s32[1,64,2]{1,2,0:T(2,128)S(1)}, s32[1,64,2]{1,2,0:T(2,128)}, u32[]{:S(2)}) copy-start(s32[1,64,2]{1,2,0:T(2,128)} %param.32) | copy-start | bytes 1540
  88.0 7.7 %copy-start.8 = (s32[1,64,2]{1,2,0:T(2,128)S(1)}, s32[1,64,2]{1,2,0:T(2,128)}, u32[]{:S(2)}) copy-start(s32[1,64,2]{1,2,0:T(2,128)} %param.31) | copy-start | bytes 1540
  88.0 36.9 %copy-start.3 = (bf16[1,64,4096]{2,1,0:T(8,128)(2,1)S(1)}, bf16[1,64,4096]{2,1,0:T(8,128)(2,1)}, u32[]{:S(2)}) copy-start(bf16[1,64,4096]{2,1,0:T(8,128)(2,1)} %param.28) | copy-start | bytes 1572868
  95.6 83.9 %all-gather.8.cloned.1.call-start = ((), (), s32[]{:S(2)}) async-start(), calls=%async_computation.7 | async-start | bytes 2228224 | tf_op jit(solution)/shard_map/all_gather | solution.py:135
  135.6 147.3 %all-gather.6.cloned.1.call-start = ((), (), s32[]{:S(2)}) async-start(), calls=%async_computation.6 | async-start | bytes 15597568 | tf_op jit(solution)/shard_map/all_gather | solution.py:135
  155.4 421.3 %all-reduce.6.cloned.1.call-start = ((), (), s32[]{:S(2)}) async-start(), calls=%async_computation.9 | async-start | bytes 33554432
  182.3 3.6 copy-start.9
  318.3 12.5 %copy-start.2 = (bf16[1792,4096]{1,0:T(8,128)(2,1)S(1)}, bf16[1792,4096]{1,0:T(8,128)(2,1)}, u32[]{:S(2)}) copy-start(bf16[1792,4096]{1,0:T(8,128)(2,1)} %reshape.200) | copy-start | bytes 44040196
  318.3 12.5 %copy-start.10 = (bf16[1,4096,512]{2,1,0:T(8,128)(2,1)S(1)}, bf16[1,4096,512]{2,1,0:T(8,128)(2,1)}, u32[]{:S(2)}) copy-start(bf16[1,4096,512]{2,1,0:T(8,128)(2,1)} %param.34) | copy-start | bytes 12582916
  356.1 237.3 %copy-start.4 = (bf16[64,4096]{1,0:T(8,128)(2,1)S(1)}, bf16[64,4096]{1,0:T(8,128)(2,1)}, u32[]{:S(2)}) copy-start(bf16[64,4096]{1,0:T(8,128)(2,1)} %reduce-scatter.4.cloned.1.call-done) | copy-start | bytes 1572868
  356.1 237.3 %copy-start.5 = (bf16[4096,8]{0,1:T(8,128)(2,1)S(1)}, bf16[4096,8]{0,1:T(8,128)(2,1)}, u32[]{:S(2)}) copy-start(bf16[4096,8]{0,1:T(8,128)(2,1)} %param.29) | copy-start | bytes 196612
  578.4 10.6 %all-to-all-start.3 = ((bf16[8,2,4096]{2,1,0:T(2,128)(2,1)}), bf16[8,2,4096]{2,1,0:T(2,128)(2,1)S(1)}, u32[]{:S(2)}, u32[]{:S(2)}) async-start(bf16[8,2,4096]{2,1,0:T(2,128)(2,1)} %copy.91), calls=%async_computation.4 | async-start | bytes 262144 | tf_op jit(solution)/shard_map/all_to_all | solution.py:141
  585.0 25.2 %copy-start.1 = (bf16[1,256,1,128]{3,1,2,0:T(8,128)(2,1)S(1)}, bf16[1,256,1,128]{3,1,2,0:T(8,128)(2,1)}, u32[]{:S(2)}) copy-start(bf16[1,256,1,128]{3,1,2,0:T(8,128)(2,1)} %param.22) | copy-start | bytes 196612
  589.0 19.4 %all-to-all-start.1 = ((bf16[8,14,4096]{2,1,0:T(8,128)(2,1)}), bf16[8,14,4096]{2,1,0:T(8,128)(2,1)S(1)}, u32[]{:S(2)}, u32[]{:S(2)}) async-start(bf16[8,14,4096]{2,1,0:T(8,128)(2,1)} %copy.89), calls=%async_computation.2 | async-start | bytes 2097152 | tf_op jit(solution)/shard_map/all_to_all | solution.py:141
Sparse Core Ops, SparseCore 0:
  12.1 54.9 all-gather.9
  95.7 29.1 reduce-scatter.3
  135.7 43.8 all-gather.7
  181.8 101.0 all-gather.5
  356.2 220.5 all-reduce.5
where the time goes:
time: 619 us; the launch traced here: 617 us
  waiting for transfers between devices  391 us (63%)
  matrix products  65.6 us (11%)
  blocking collectives  62.6 us (10%)
  local copies, waits for them, and re-layouts  52.6 us (8%)
  other arithmetic  19.3 us (3%)
  between operations  14.8 us (2%)
  starting transfers between devices  10 us (2%)
    unnamed x6, waiting for transfers between devices  220 us
    all_gather x2, waiting for transfers between devices, experts_round(): part_rows = lax.all_gather(arrived, 'ctx', axis=0, tiled=True)  115 us
    unnamed x1, blocking collectives  35.3 us
    reduce_scatter x1, waiting for transfers between devices, shards(): lax.psum_scatter(jnp.dot(normed, out_weight, preferred_element_type=jnp.f...  29.1 us
    all_to_all x2, blocking collectives, experts_round(): lax.all_to_all(buffer, ('exp', 'dp'), split_axis=0, concat_axis=0, tiled=...  27.3 us
    reshape x2, local copies, waits for them, and re-layouts, experts_round(): flat_rows = part_rows.reshape(-1, part_rows.shape[-1])  20.8 us
    dot_general x2, matrix products, ffn_rows(): lax.dot_general(activated, down_w, (((1,), (1,)), ((), ())), preferred_el...  18.3 us
    select_n x32, other arithmetic, hop(): return jax.tree.map(lambda a, b: jnp.where(reached, a, b), new, before)  17.8 us
  transfers between devices with their start and end apart: 7, of which 7 were waited for; matrix products, arithmetic and copies ran while one was open for 4% of the time, Pallas kernels for 0%

commit v1 on v0

--- a/solution.py
+++ b/solution.py
@@ -1,6 +1,8 @@
 import jax
 import jax.numpy as jnp
 from jax import lax
+from jax.experimental import pallas as pl
+from jax.experimental.pallas import tpu as pltpu
 from jax.sharding import PartitionSpec as P
 
 D = 4096
@@ -8,6 +10,376 @@
 CAP = 14
 SPILL = 2
 BLOCK = 16
+SIDE = 4
+ROWS = EXPERTS * BLOCK
+WIDTH = 512
+PAIRS = D // WIDTH // 2
+HALF = ROWS // 2
+MESH = pl.DeviceIdType.MESH
+
+
+def experts_kernel(
+    rows_ref,
+    gate_ref,
+    up_ref,
+    down_ref,
+    out_ref,
+    xg,
+    acc,
+    act,
+    w_gate,
+    w_up,
+    w_down,
+    part,
+    line,
+    ag_send,
+    ag_recv,
+    rs_send,
+    rs_recv,
+    load_sem,
+    own_sem,
+):
+    here = lax.axis_index("ctx")
+    my = {"x": lax.rem(here, SIDE), "z": lax.div(here, SIDE)}
+
+    def around(axis, step):
+        return lax.rem(my[axis] + step + SIDE, SIDE)
+
+    def neighbour(axis, step):
+        other = around(axis, step)
+        if axis == "x":
+            return {"ctx": my["z"] * SIDE + other}
+        return {"ctx": other * SIDE + my["x"]}
+
+    def along(axis, ref, place, at):
+        if axis == "z":
+            return ref.at[place, at]
+        return ref.at[at, place]
+
+    loads = [
+        pltpu.make_async_copy(src, dst, load_sem.at[i])
+        for i, (src, dst) in enumerate(((gate_ref, w_gate), (up_ref, w_up), (down_ref, w_down)))
+    ]
+    for load in loads:
+        load.start()
+    own = [
+        pltpu.make_async_copy(
+            rows_ref.at[:, pl.ds(k * WIDTH, WIDTH)], xg.at[k, my["z"], my["x"]], own_sem.at[k]
+        )
+        for k in range(2 * PAIRS)
+    ]
+    for copy in own:
+        copy.start()
+
+    barrier = pltpu.get_barrier_semaphore()
+    for axis in ("x", "z"):
+        for step in (1, -1):
+            pl.semaphore_signal(
+                barrier, inc=1, device_id=neighbour(axis, step), device_id_type=MESH
+            )
+    pl.semaphore_wait(barrier, 4)
+    for copy in own:
+        copy.wait()
+
+    every = pl.ds(0, SIDE)
+    halves = {1: pl.ds(0, SIDE // 2), -1: pl.ds(SIDE // 2, SIDE // 2)}
+    half_rows = {1: pl.ds(0, HALF), -1: pl.ds(HALF, HALF)}
+    axes = (("x", "z"), ("z", "x"))
+    slot = {1: 0, -1: 1}
+
+    def ag_copy(j, t, step, d, landing):
+        near, far = axes[t]
+        chunk = xg.at[2 * j + t]
+        back = -d if landing else 0
+        if step == 0:
+            ref, to = along(near, chunk, around(near, back), my[far]), near
+        elif step == 1:
+            ref = along(near, chunk, around(near, -2 * d if landing else -d), my[far])
+            ref, to = ref.at[half_rows[d]], near
+        elif step == 2:
+            ref, to = along(far, chunk, around(far, back), every), far
+        else:
+            ref = along(far, chunk, around(far, -2 * d if landing else -d), halves[d])
+            to = far
+        m = step * 2 + slot[d]
+        return pltpu.make_async_remote_copy(
+            src_ref=ref,
+            dst_ref=ref,
+            send_sem=ag_send.at[j, t, m],
+            recv_sem=ag_recv.at[j, t, m],
+            device_id=neighbour(to, d),
+            device_id_type=MESH,
+        )
+
+    def ag_start(j, step):
+        for t in range(2):
+            for d in (1, -1):
+                ag_copy(j, t, step, d, False).start()
+
+    def ag_arrive(j, step):
+        for t in range(2):
+            for d in (1, -1):
+                ag_copy(j, t, step, d, True).wait_recv()
+
+    def ag_sent(j):
+        for step in range(4):
+            for t in range(2):
+                for d in (1, -1):
+                    ag_copy(j, t, step, d, False).wait_send()
+
+    def gate_up(j, first):
+        @pl.loop(0, SIDE * SIDE // 2)
+        def _(b):
+            zz, x0 = lax.div(b, 2), lax.rem(b, 2) * 2
+            rows = pl.ds(pl.multiple_of(b * 2 * ROWS, 2 * ROWS), 2 * ROWS)
+            for n, weight in enumerate((w_gate, w_up)):
+                total = None
+                for t in range(2):
+                    k = 2 * j + t
+                    left = xg[k, zz, pl.ds(x0, 2)].reshape(2 * ROWS, WIDTH)
+                    right = weight[pl.ds(pl.multiple_of(k * WIDTH, WIDTH), WIDTH), :]
+                    term = jnp.dot(left, right, preferred_element_type=jnp.float32)
+                    total = term if total is None else total + term
+                if first:
+                    acc[n, rows, :] = total
+                else:
+                    acc[n, rows, :] += total
+
+    ag_start(0, 0)
+    ag_arrive(0, 0)
+    ag_start(0, 1)
+    ag_arrive(0, 1)
+    ag_start(0, 2)
+    for load in loads:
+        load.wait()
+
+    def ag_round(j, first):
+        last = j == PAIRS - 1 if isinstance(j, int) else False
+        if not last:
+            ag_start(j + 1, 0)
+        if not first:
+            if isinstance(j, int) and j == 1:
+                gate_up(0, True)
+            else:
+                gate_up(j - 1, False)
+        if not last:
+            ag_arrive(j + 1, 0)
+            ag_start(j + 1, 1)
+        ag_arrive(j, 2)
+        if not first:
+            ag_sent(j - 1)
+        ag_start(j, 3)
+        if not last:
+            ag_arrive(j + 1, 1)
+            ag_start(j + 1, 2)
+        ag_arrive(j, 3)
+
+    ag_round(0, True)
+    ag_round(1, False)
+
+    @pl.loop(2, PAIRS - 1)
+    def _(j):
+        ag_round(j, False)
+
+    ag_round(PAIRS - 1, False)
+    gate_up(PAIRS - 1, False)
+
+    @pl.loop(0, SIDE * SIDE)
+    def _(b):
+        rows = pl.ds(pl.multiple_of(b * ROWS, ROWS), ROWS)
+        gate_val = acc[0, rows, :]
+        act[rows, :] = (gate_val / (1.0 + jnp.exp(-gate_val)) * acc[1, rows, :]).astype(jnp.bfloat16)
+
+    ag_sent(PAIRS - 1)
+
+    def rs_copy(j, t, step, d):
+        near, far = axes[t]
+        p = part.at[lax.rem(j, 2), t]
+        room = xg.at[2 * j + t]
+        if step == 0:
+            src = along(far, p, around(far, 2), halves[d])
+            dst, to = room.at[0, halves[d]], far
+        elif step == 1:
+            src = along(far, p, around(far, d), every)
+            dst, to = room.at[1 + slot[d]], far
+        elif step == 2:
+            src = line.at[lax.rem(j, 2), t, around(near, 2), half_rows[d]]
+            dst, to = room.at[3, 0, half_rows[d]], near
+        else:
+            src = line.at[lax.rem(j, 2), t, around(near, d)]
+            dst, to = room.at[3, 1 + slot[d]], near
+        m = step * 2 + slot[d]
+        return pltpu.make_async_remote_copy(
+            src_ref=src,
+            dst_ref=dst,
+            send_sem=rs_send.at[j, t, m],
+            recv_sem=rs_recv.at[j, t, m],
+            device_id=neighbour(to, d),
+            device_id_type=MESH,
+        )
+
+    def rs_start(j, step, t):
+        for d in (1, -1):
+            rs_copy(j, t, step, d).start()
+
+    def rs_arrive(j, step, t):
+        for d in (1, -1):
+            rs_copy(j, t, step, d).wait_recv()
+
+    def rs_sent(j):
+        for step in range(4):
+            for t in range(2):
+                for d in (1, -1):
+                    rs_copy(j, t, step, d).wait_send()
+
+    def down(j):
+        @pl.loop(0, SIDE * SIDE // 2)
+        def _(b):
+            zz, x0 = lax.div(b, 2), lax.rem(b, 2) * 2
+            rows = pl.ds(pl.multiple_of(b * 2 * ROWS, 2 * ROWS), 2 * ROWS)
+            for t in range(2):
+                k = 2 * j + t
+                right = w_down[pl.ds(pl.multiple_of(k * WIDTH, WIDTH), WIDTH), :]
+                term = lax.dot_general(
+                    act[rows, :], right, (((1,), (1,)), ((), ())), preferred_element_type=jnp.float32
+                )
+                part[lax.rem(j, 2), t, zz, pl.ds(x0, 2)] = term.astype(jnp.bfloat16).reshape(
+                    2, ROWS, WIDTH
+                )
+
+    f32 = jnp.float32
+
+    def add_first(j, t):
+        far, near = axes[t][1], axes[t][0]
+        s = lax.rem(j, 2)
+        for d in (1, -1):
+            base = 0 if d == 1 else SIDE // 2
+            place = around(far, d)
+
+            @pl.loop(0, SIDE // 2)
+            def _(i):
+                at = (place, base + i) if far == "z" else (base + i, place)
+                part[s, t, at[0], at[1]] = (
+                    part[s, t, at[0], at[1]].astype(f32) + xg[2 * j + t, 0, base + i].astype(f32)
+                ).astype(jnp.bfloat16)
+
+    def add_line(j, t):
+        far = axes[t][1]
+        s = lax.rem(j, 2)
+
+        @pl.loop(0, SIDE)
+        def _(i):
+            at = (my[far], i) if far == "z" else (i, my[far])
+            line[s, t, i] = (
+                part[s, t, at[0], at[1]].astype(f32)
+                + xg[2 * j + t, 1, i].astype(f32)
+                + xg[2 * j + t, 2, i].astype(f32)
+            ).astype(jnp.bfloat16)
+
+    def add_second(j, t):
+        near = axes[t][0]
+        s = lax.rem(j, 2)
+        for d in (1, -1):
+            at = around(near, d)
+            line[s, t, at, half_rows[d]] = (
+                line[s, t, at, half_rows[d]].astype(f32)
+                + xg[2 * j + t, 3, 0, half_rows[d]].astype(f32)
+            ).astype(jnp.bfloat16)
+
+    def add_last(j, t):
+        near = axes[t][0]
+        s = lax.rem(j, 2)
+        total = (
+            line[s, t, my[near]].astype(f32)
+            + xg[2 * j + t, 3, 1].astype(f32)
+            + xg[2 * j + t, 3, 2].astype(f32)
+        )
+        start = (2 * j + t) * WIDTH
+        out_ref[:, pl.ds(pl.multiple_of(start, WIDTH), WIDTH)] = total.astype(jnp.bfloat16)
+
+    def rs_second(j):
+        for t in range(2):
+            rs_arrive(j, 1, t)
+            add_line(j, t)
+            rs_start(j, 2, t)
+
+    def rs_third(j):
+        for t in range(2):
+            rs_arrive(j, 2, t)
+            add_second(j, t)
+            rs_start(j, 3, t)
+
+    def rs_begin(j):
+        for t in range(2):
+            rs_arrive(j, 0, t)
+            add_first(j, t)
+            rs_start(j, 1, t)
+
+    def rs_end(j):
+        for t in range(2):
+            rs_arrive(j, 3, t)
+            add_last(j, t)
+        rs_sent(j)
+
+    def both(j):
+        for t in range(2):
+            rs_start(j, 0, t)
+
+    down(0)
+    both(0)
+    down(1)
+    rs_begin(0)
+    both(1)
+
+    @pl.loop(0, PAIRS - 1)
+    def _(j):
+        rs_second(j)
+        rs_begin(j + 1)
+        rs_third(j)
+        rs_end(j)
+
+        @pl.when(j + 2 < PAIRS)
+        def _():
+            down(j + 2)
+            both(j + 2)
+
+    rs_second(PAIRS - 1)
+    rs_third(PAIRS - 1)
+    rs_end(PAIRS - 1)
+
+
+def experts(rows, gate_w, up_w, down_w):
+    hidden = gate_w.shape[1]
+    bf16 = jnp.bfloat16
+    any_space = pl.BlockSpec(memory_space=pl.ANY)
+    return pl.pallas_call(
+        experts_kernel,
+        out_shape=jax.ShapeDtypeStruct((ROWS, D), bf16),
+        in_specs=[any_space] * 4,
+        out_specs=pl.BlockSpec(memory_space=pltpu.VMEM),
+        scratch_shapes=[
+            pltpu.VMEM((2 * PAIRS, SIDE, SIDE, ROWS, WIDTH), bf16),
+            pltpu.VMEM((2, SIDE * SIDE * ROWS, hidden), jnp.float32),
+            pltpu.VMEM((SIDE * SIDE * ROWS, hidden), bf16),
+            pltpu.VMEM((D, hidden), bf16),
+            pltpu.VMEM((D, hidden), bf16),
+            pltpu.VMEM((D, hidden), bf16),
+            pltpu.VMEM((2, 2, SIDE, SIDE, ROWS, WIDTH), bf16),
+            pltpu.VMEM((2, 2, SIDE, ROWS, WIDTH), bf16),
+            pltpu.SemaphoreType.DMA((PAIRS, 2, 8)),
+            pltpu.SemaphoreType.DMA((PAIRS, 2, 8)),
+            pltpu.SemaphoreType.DMA((PAIRS, 2, 8)),
+            pltpu.SemaphoreType.DMA((PAIRS, 2, 8)),
+            pltpu.SemaphoreType.DMA((3,)),
+            pltpu.SemaphoreType.DMA((2 * PAIRS,)),
+        ],
+        compiler_params=pltpu.CompilerParams(
+            collective_id=0, has_side_effects=True, vmem_limit_bytes=60 << 20
+        ),
+        cost_estimate=pl.CostEstimate(
+            flops=6 * 2048 * D * 512, bytes_accessed=14 << 20, transcendentals=1 << 20
+        ),
+    )(rows, gate_w, up_w, down_w)
 
 
 def entering_2(value, axis, combine, identity):
@@ -35,15 +407,6 @@
 
 def chain_combine(earlier, later):
     return (earlier[0] * later[0], later[0][:, None, None] * earlier[1] + later[1])
-
-
-def ffn_rows(flat_rows, gate_w, up_w, down_w):
-    gate_val = jnp.dot(flat_rows, gate_w, preferred_element_type=jnp.float32)
-    up_val = jnp.dot(flat_rows, up_w, preferred_element_type=jnp.float32)
-    activated = (jax.nn.silu(gate_val) * up_val).astype(jnp.bfloat16)
-    return lax.dot_general(
-        activated, down_w, (((1,), (1,)), ((), ())), preferred_element_type=jnp.float32
-    )
 
 
 def shards(
@@ -130,18 +493,10 @@
     own_up = up_weight[0]
     own_down = down_weight[0]
 
-    def experts_round(buffer):
-        arrived = lax.all_to_all(buffer, ("exp", "dp"), split_axis=0, concat_axis=0, tiled=True)
-        part_rows = lax.all_gather(arrived, "ctx", axis=0, tiled=True)
-        flat_rows = part_rows.reshape(-1, part_rows.shape[-1])
-        partial_value = ffn_rows(flat_rows, own_gate, own_up, own_down).reshape(part_rows.shape)
-        summed = lax.psum_scatter(
-            partial_value.astype(jnp.bfloat16), "ctx", scatter_dimension=0, tiled=True
-        )
-        return lax.all_to_all(summed, ("exp", "dp"), split_axis=0, concat_axis=0, tiled=True)
-
-    returned = jnp.concatenate(
-        (experts_round(outgoing[:, :CAP]), experts_round(outgoing[:, CAP:])), axis=1
+    arrived = lax.all_to_all(outgoing, ("exp", "dp"), split_axis=0, concat_axis=0, tiled=True)
+    summed = experts(arrived.reshape(ROWS, D), own_gate, own_up, own_down)
+    returned = lax.all_to_all(
+        summed.reshape(EXPERTS, BLOCK, D), ("exp", "dp"), split_axis=0, concat_axis=0, tiled=True
     )
     weighting = jnp.sum(jnp.where(onehot, shares[:, :, None], 0.0), axis=1)
     expert_sum = jnp.dot(

time: 619 us -> 386 us (0.62)
  waiting for transfers between devices: 391 us -> 54.4 us
  Pallas kernels: 0 us -> 201 us
  local copies, waits for them, and re-layouts: 52.6 us -> 5.6 us
  matrix products: 65.6 us -> 20.8 us
  blocking collectives: 62.6 us -> 54.2 us
    unnamed x6 -> x2, waiting for transfers between devices: 220 us -> 0.03 us
    pallas_call x0 -> x1, Pallas kernels: none -> 201 us  [experts(): pl.pallas_call(experts_kernel, out_shape=jax.ShapeDtypeStruct((ROWS, D),...]
    all_gather x2 -> x0, waiting for transfers between devices: 115 us -> none  [experts_round(): part_rows = lax.all_gather(arrived, 'ctx', axis=0, tiled=True)]
    dot_general x6 -> x0, matrix products: 44.9 us -> none  [the longest x2 18.3 us: ffn_rows(): lax.dot_general(activated, down_w, (((1,), (1,)), ((), ())), preferred_el...]
    reshape x4 -> x2, local copies, waits for them, and re-layouts: 21.5 us -> 0.77 us  [the longest x2 20.8 us: experts_round(): flat_rows = part_rows.reshape(-1, part_rows.shape[-1])]
    all_gather x1 -> x0, local copies, waits for them, and re-layouts: 17.4 us -> none  [experts_round(): part_rows = lax.all_gather(arrived, 'ctx', axis=0, tiled=True)]
    all_to_all x2 -> x1, blocking collectives: 27.3 us -> 18.8 us  [shards(): lax.all_to_all(outgoing, ('exp', 'dp'), split_axis=0, concat_axis=0, tile...]
    all_to_all x2 -> x1, starting transfers between devices: 9.66 us -> 15.2 us  [shards(): lax.all_to_all(summed.reshape(EXPERTS, BLOCK, D), ('exp', 'dp'), split_ax...]
  transfers between devices with their start and end apart: 7 -> 3, of which waited for: 7 -> 3; matrix products, arithmetic and copies ran while one was open for 4% -> 2% of each run, Pallas kernels for 0% -> 0%
where the time goes in v1:
time: 386 us; the launch traced here: 385 us
  Pallas kernels  201 us (52%)
  waiting for transfers between devices  54.4 us (14%)
  blocking collectives  54.2 us (14%)
  matrix products  20.8 us (5%)
  other arithmetic  19.1 us (5%)
  starting transfers between devices  15.2 us (4%)
  between operations  14.3 us (4%)
  local copies, waits for them, and re-layouts  5.6 us (1%)
    pallas_call x1, Pallas kernels, experts(): pl.pallas_call(experts_kernel, out_shape=jax.ShapeDtypeStruct((ROWS, D),...  201 us
    unnamed x1, blocking collectives  35.4 us
    reduce_scatter x1, waiting for transfers between devices, shards(): lax.psum_scatter(jnp.dot(normed, out_weight, preferred_element_type=jnp.f...  29.3 us
    all_to_all x1, blocking collectives, shards(): lax.all_to_all(outgoing, ('exp', 'dp'), split_axis=0, concat_axis=0, tile...  18.8 us
    select_n x32, other arithmetic, hop(): return jax.tree.map(lambda a, b: jnp.where(reached, a, b), new, before)  17.8 us
    all_to_all x1, starting transfers between devices, shards(): lax.all_to_all(summed.reshape(EXPERTS, BLOCK, D), ('exp', 'dp'), split_ax...  15.2 us
    all_to_all x1, waiting for transfers between devices, shards(): lax.all_to_all(summed.reshape(EXPERTS, BLOCK, D), ('exp', 'dp'), split_ax...  14.7 us
    all_gather x1, waiting for transfers between devices, entering_2(): lax.all_gather(part.astype(kind), axis)  10.4 us
  transfers between devices with their start and end apart: 3, of which 3 were waited for; matrix products, arithmetic and copies ran while one was open for 2% of the time, Pallas kernels for 0%

profile of v1, /device:TPU:1, one launch (start us, length us, event | category | flops | bytes accessed | tf_op | source)
XLA Modules:
  0.0 385.1 jit_solution(4524381491499340067)
XLA Ops:
  6.5 0.0 copy-start
  6.5 0.0 all-gather.4.cloned.1.call-start
  6.5 0.8 reshape.191
  7.3 0.6 reduce-window.6
  7.9 0.2 slice_reduce_fusion
  8.1 0.1 copy_bitcast_fusion
  8.2 0.2 slice_reduce_fusion.1
  8.4 0.1 exponential_bitcast_fusion
  8.5 1.2 copy.55
  9.7 2.2 convolution_convert_fusion.2
  11.9 0.0 all-gather.4.cloned.1.call-update
  11.9 0.0 reduce-scatter.2.cloned.1.call-start
  12.0 1.3 dynamic-slice
  13.9 0.2 fusion.44
  14.1 0.2 dynamic-update-slice
  14.3 35.4 %all-reduce = bf16[256]{0:T(256)(128)(2,1)S(1)} all-reduce(bf16[256]{0:T(256)(128)(2,1)S(1)} %dynamic-update-slice), channel_id=2, replica_groups=mesh['ctx'=16,'exp'=4,'dp'=2] {'ctx'}, use_global_device_ids=true, to_apply=%add | all-reduce | flops 256 | bytes 1024
  49.7 0.1 reshape.204
  49.8 1.2 copy.57
  51.1 0.0 copy-done
  51.1 1.0 fusion.40
  52.1 4.6 %fusion.15 = f32[256,16,64]{0,2,1:T(8,128)} fusion(bf16[256,16,64]{0,2,1:T(8,128)(2,1)S(1)} %bitcast.127, f32[256,256]{1,0:T(8,128)S(1)} %fusion.40, f32[16,256]{1,0:T(8,128)S(1)} %copy_bitcast_fusion, pred[256,256]{1,0:T(8,128)(4,1)S(1)} %iota_compare_fusion), kind=kOutput, calls=%fused_computation.23 | convolution fusion | flops 810549248 | bytes 1916928 | tf_op jit(solution)/shard_map/hts,shp->thp/dot_general | solution.py:445
  56.7 10.4 %all-gather.4.cloned.1.call-done = bf16[256,64,128]{2,1,0:T(8,128)(2,1)} async-done(((bf16[16,64,128]{2,1,0:T(8,128)(2,1)}), bf16[256,64,128]{2,1,0:T(8,128)(2,1)}) %all-gather.4.cloned.1.call-update) | async-done | bytes 4194320 | tf_op jit(solution)/shard_map/all_gather | solution.py:388
  67.1 18.2 %while.16 = (s32[]{:T(128)}, f32[16]{0:T(128)S(1)}, f32[16,64,128]{2,1,0:T(8,128)S(1)}, s32[]{:T(128)}, bf16[16,16]{1,0:T(8,128)(2,1)S(1)}, /*index=5*/bf16[16,16,64,128]{3,2,1,0:T(8,128)(2,1)}, s32[]{:T(128)}, s32[]{:T(128)}) while((s32[]{:T(128)}, f32[16]{0:T(128)S(1)}, f32[16,64,128]{2,1,0:T(8,128)S(1)}, s32[]{:T(128)}, ...), condition=%wide.region_3.4_spmd.clone, body=%wide.region_2.3_spmd.clone.sunk | while | flops 655428 | bytes 1311123 | solution.py:405
  67.1 1.1 fusion.57
  68.3 1.1 fusion.57
  69.4 1.1 fusion.57
  70.6 1.1 fusion.57
  71.7 1.1 fusion.57
  72.8 1.1 fusion.57
  74.0 1.1 fusion.57
  75.1 1.1 fusion.57
  76.3 1.1 fusion.57
  77.4 1.1 fusion.57
  78.5 1.1 fusion.57
  79.7 1.1 fusion.57
  80.8 1.1 fusion.57
  82.0 1.1 fusion.57
  83.1 1.1 fusion.57
  84.2 1.1 fusion.57
  85.3 0.0 copy-done.8
  85.4 0.0 copy-start.7
  85.4 2.3 multiply_reduce_fusion
  87.7 0.3 copy.56
  88.0 0.0 copy-done.7
  88.0 0.0 copy-start.4
  88.0 0.0 copy-start.5
  88.0 0.0 copy-start.6
  88.1 0.0 copy-start.1
  88.1 7.6 %convolution_convert_fusion = bf16[256,4096]{1,0:T(8,128)(2,1)} fusion(bf16[1024,4096]{1,0:T(8,128)(2,1)} %param.27, f32[256,1024]{1,0:T(8,128)S(1)} %copy.56, f32[1024]{0:T(1024)S(1)} %copy-done.7, f32[256]{0:T(256)S(1)} %add_rsqrt_fusion, bf16[1,256,1024]{2,1,0:T(8,128)(2,1)} %param.20), kind=kOutput, calls=%fused_computation.5 | convolution fusion | flops 2150891520 | bytes 12063744 | tf_op jit(solution)/shard_map/dot_general | solution.py:468
  95.6 0.0 reduce-scatter.2.cloned.1.call-update
  95.6 0.0 copy-done.4
  95.7 0.0 copy-done.5
  95.7 0.0 copy-done.6
  95.7 0.1 convert_reduce_fusion
  95.8 29.3 %reduce-scatter.2.cloned.1.call-done = bf16[64,4096]{1,0:T(8,128)(2,1)} async-done(((bf16[256,4096]{1,0:T(8,128)(2,1)}), bf16[64,4096]{1,0:T(8,128)(2,1)}) %reduce-scatter.2.cloned.1.call-update) | async-done | bytes 524304 | tf_op jit(solution)/shard_map/reduce_scatter | solution.py:467
  125.0 0.0 copy-done.1
  125.0 1.5 convolution_convert_fusion.1
  126.5 18.8 %all_to_all.10 = bf16[8,16,4096]{2,1,0:T(8,128)(2,1)} all-to-all(bf16[8,16,4096]{2,1,0:T(8,128)(2,1)S(1)} %bitcast.124), channel_id=1, replica_groups=mesh['ctx'=16,'exp'=4,'dp'=2] {'exp','dp'}, dimensions={0} | all-to-all | bytes 2097152 | tf_op jit(solution)/shard_map/all_to_all | solution.py:496
  145.3 201.2 %shard_map.163 = bf16[128,4096]{1,0:T(8,128)(2,1)} custom-call(bf16[128,4096]{1,0:T(8,128)(2,1)} %bitcast.132, bf16[4096,512]{1,0:T(8,128)(2,1)} %bitcast.135, bf16[4096,512]{1,0:T(8,128)(2,1)} %bitcast.136, bf16[4096,512]{1,0:T(8,128)(2,1)} %bitcast.137), custom_call_target="tpu_custom_call" | custom-call | flops 25769803776 | bytes 14680064 | tf_op jit(solution)/shard_map/pallas_call | solution.py:355
  346.5 15.2 %all-to-all-start.1 = ((bf16[8,16,4096]{2,1,0:T(8,128)(2,1)}), bf16[8,16,4096]{2,1,0:T(8,128)(2,1)S(1)}, u32[]{:S(2)}, u32[]{:S(2)}) async-start(bf16[8,16,4096]{2,1,0:T(8,128)(2,1)} %bitcast.130), calls=%async_computation.2 | async-start | bytes 2097152 | tf_op jit(solution)/shard_map/all_to_all | solution.py:498
  361.7 0.2 fusion.49
  362.0 0.1 select_reduce_fusion
  362.1 14.7 %all-to-all-done.1 = bf16[8,16,4096]{2,1,0:T(8,128)(2,1)S(1)} async-done(((bf16[8,16,4096]{2,1,0:T(8,128)(2,1)}), bf16[8,16,4096]{2,1,0:T(8,128)(2,1)S(1)}, u32[]{:S(2)}, u32[]{:S(2)}) %all-to-all-start.1) | async-done | bytes 1048608 | tf_op jit(solution)/shard_map/all_to_all | solution.py:498
  376.8 1.4 fusion.2
  (33 shorter events, 0.5 us)
Async XLA Ops:
  6.5 44.6 %copy-start = (bf16[1,256,1,128]{3,1,2,0:T(8,128)(2,1)S(1)}, bf16[1,256,1,128]{3,1,2,0:T(8,128)(2,1)}, u32[]{:S(2)}) copy-start(bf16[1,256,1,128]{3,1,2,0:T(8,128)(2,1)} %param.22) | copy-start | bytes 196612
  6.5 60.6 %all-gather.4.cloned.1.call-start = ((), (), s32[]{:S(2)}) async-start(), calls=%async_computation.4 | async-start | bytes 4456448 | tf_op jit(solution)/shard_map/all_gather | solution.py:388
  11.9 113.1 %reduce-scatter.2.cloned.1.call-start = ((), (), s32[]{:S(2)}) async-start(), calls=%async_computation.3 | async-start | bytes 2621440 | tf_op jit(solution)/shard_map/reduce_scatter | solution.py:467
  56.7 28.7 %copy-start.8 = (f32[16]{0:T(128)S(1)}, f32[16]{0:T(128)}, u32[]{:S(2)}) copy-start(f32[16]{0:T(128)} %param.24) | copy-start | bytes 196
  85.4 2.7 copy-start.7
  88.0 7.6 %copy-start.4 = (s32[1,64,2]{1,2,0:T(2,128)S(1)}, s32[1,64,2]{1,2,0:T(2,128)}, u32[]{:S(2)}) copy-start(s32[1,64,2]{1,2,0:T(2,128)} %param.30) | copy-start | bytes 1540
  88.0 7.6 %copy-start.5 = (s32[1,64,2]{1,2,0:T(2,128)S(1)}, s32[1,64,2]{1,2,0:T(2,128)}, u32[]{:S(2)}) copy-start(s32[1,64,2]{1,2,0:T(2,128)} %param.32) | copy-start | bytes 1540
  88.0 7.6 %copy-start.6 = (s32[1,64,2]{1,2,0:T(2,128)S(1)}, s32[1,64,2]{1,2,0:T(2,128)}, u32[]{:S(2)}) copy-start(s32[1,64,2]{1,2,0:T(2,128)} %param.31) | copy-start | bytes 1540
  88.1 37.0 %copy-start.1 = (bf16[1,64,4096]{2,1,0:T(8,128)(2,1)S(1)}, bf16[1,64,4096]{2,1,0:T(8,128)(2,1)}, u32[]{:S(2)}) copy-start(bf16[1,64,4096]{2,1,0:T(8,128)(2,1)} %param.28) | copy-start | bytes 1572868
  145.3 216.4 %copy-start.2 = (bf16[64,4096]{1,0:T(8,128)(2,1)S(1)}, bf16[64,4096]{1,0:T(8,128)(2,1)}, u32[]{:S(2)}) copy-start(bf16[64,4096]{1,0:T(8,128)(2,1)} %reduce-scatter.2.cloned.1.call-done) | copy-start | bytes 1572868
  145.3 216.4 %copy-start.3 = (bf16[4096,8]{0,1:T(8,128)(2,1)S(1)}, bf16[4096,8]{0,1:T(8,128)(2,1)}, u32[]{:S(2)}) copy-start(bf16[4096,8]{0,1:T(8,128)(2,1)} %param.29) | copy-start | bytes 196612
  346.5 30.3 %all-to-all-start.1 = ((bf16[8,16,4096]{2,1,0:T(8,128)(2,1)}), bf16[8,16,4096]{2,1,0:T(8,128)(2,1)S(1)}, u32[]{:S(2)}, u32[]{:S(2)}) async-start(bf16[8,16,4096]{2,1,0:T(8,128)(2,1)} %bitcast.130), calls=%async_computation.2 | async-start | bytes 2097152 | tf_op jit(solution)/shard_map/all_to_all | solution.py:498
Sparse Core Ops, SparseCore 0:
  12.1 55.0 all-gather.3
  95.8 29.2 reduce-scatter.1

commit v2 on v1

--- a/solution.py
+++ b/solution.py
@@ -12,18 +12,37 @@
 BLOCK = 16
 SIDE = 4
 ROWS = EXPERTS * BLOCK
-WIDTH = 512
+WIDTH = 256
 PAIRS = D // WIDTH // 2
 HALF = ROWS // 2
+TOKENS = 64
+GROUPS = 4
 MESH = pl.DeviceIdType.MESH
 
 
-def experts_kernel(
-    rows_ref,
+def layer_kernel(
+    normed_ref,
+    mix_ref,
+    residual_ref,
+    router_ref,
+    chosen_ref,
+    slot_ref,
+    spill_ref,
     gate_ref,
     up_ref,
     down_ref,
     out_ref,
+    normed,
+    w_mix,
+    mixed,
+    terms,
+    hidden,
+    placing,
+    shares,
+    logits,
+    leaving,
+    sums,
+    returned,
     xg,
     acc,
     act,
@@ -36,8 +55,15 @@
     ag_recv,
     rs_send,
     rs_recv,
+    mix_send,
+    mix_recv,
+    row_send,
+    row_recv,
+    back_send,
+    back_recv,
     load_sem,
-    own_sem,
+    mix_sem,
+    normed_sem,
 ):
     here = lax.axis_index("ctx")
     my = {"x": lax.rem(here, SIDE), "z": lax.div(here, SIDE)}
@@ -56,20 +82,29 @@
             return ref.at[place, at]
         return ref.at[at, place]
 
+    f32, bf16 = jnp.float32, jnp.bfloat16
+    my_exp, my_dp = lax.axis_index("exp"), lax.axis_index("dp")
+    owner = my_exp * 2 + my_dp
+
+    fetch = pltpu.make_async_copy(normed_ref, normed, normed_sem)
+    fetch.start()
+
+    def mix_load(j):
+        columns = pl.ds(pl.multiple_of(j * 2 * WIDTH, 2 * WIDTH), 2 * WIDTH)
+        return pltpu.make_async_copy(mix_ref.at[:, columns], w_mix.at[:, columns], mix_sem.at[j])
+
+    for j in range(PAIRS):
+        mix_load(j).start()
     loads = [
         pltpu.make_async_copy(src, dst, load_sem.at[i])
         for i, (src, dst) in enumerate(((gate_ref, w_gate), (up_ref, w_up), (down_ref, w_down)))
     ]
     for load in loads:
         load.start()
-    own = [
-        pltpu.make_async_copy(
-            rows_ref.at[:, pl.ds(k * WIDTH, WIDTH)], xg.at[k, my["z"], my["x"]], own_sem.at[k]
-        )
-        for k in range(2 * PAIRS)
-    ]
-    for copy in own:
-        copy.start()
+
+    def partner(o):
+        other = lax.rem(owner + o, EXPERTS)
+        return other, {"exp": lax.div(other, 2), "dp": lax.rem(other, 2)}
 
     barrier = pltpu.get_barrier_semaphore()
     for axis in ("x", "z"):
@@ -77,9 +112,107 @@
             pl.semaphore_signal(
                 barrier, inc=1, device_id=neighbour(axis, step), device_id_type=MESH
             )
-    pl.semaphore_wait(barrier, 4)
-    for copy in own:
-        copy.wait()
+    for o in range(1, EXPERTS):
+        pl.semaphore_signal(barrier, inc=1, device_id=partner(o)[1], device_id_type=MESH)
+
+    row_id = lax.broadcasted_iota(jnp.int32, (ROWS, TOKENS), 0)
+    expert_ids, slot_ids, spill_ids = chosen_ref[...], slot_ref[...], spill_ref[...]
+    target = jnp.where(
+        slot_ids >= 0,
+        expert_ids * BLOCK + slot_ids,
+        jnp.where(
+            spill_ids >= 0,
+            jnp.right_shift(spill_ids, 1) * BLOCK + CAP + jnp.bitwise_and(spill_ids, 1),
+            -1,
+        ),
+    )
+    places = [row_id == target[i : i + 1, :] for i in range(2)]
+    placing[...] = (places[0].astype(f32) + places[1].astype(f32)).astype(bf16)
+    logits[...] = jnp.zeros_like(logits)
+    pl.semaphore_wait(barrier, 4 + EXPERTS - 1)
+
+    def columns_of(k):
+        return pl.ds(pl.multiple_of(k * WIDTH, WIDTH), WIDTH)
+
+    def term_copy(j, t, i):
+        other = lax.rem(my_exp + i, GROUPS)
+        return pltpu.make_async_remote_copy(
+            src_ref=mixed.at[lax.rem(j, 2), t, other],
+            dst_ref=terms.at[2 * j + t, i - 1],
+            send_sem=mix_send.at[2 * j + t, i - 1],
+            recv_sem=mix_recv.at[2 * j + t, i - 1],
+            device_id={"exp": other},
+            device_id_type=MESH,
+        )
+
+    def mix(j):
+        mix_load(j).wait()
+        for t in range(2):
+            term = jnp.dot(
+                normed[...], w_mix[:, columns_of(2 * j + t)], preferred_element_type=f32
+            )
+            mixed[lax.rem(j, 2), t] = term.astype(bf16).reshape(GROUPS, TOKENS, WIDTH)
+            for i in range(1, GROUPS):
+                term_copy(j, t, i).start()
+
+    def row_copy(j, t, o):
+        other, place = partner(o)
+        return pltpu.make_async_remote_copy(
+            src_ref=leaving.at[lax.rem(j, 2), t, other],
+            dst_ref=xg.at[
+                2 * j + t, my["z"], my["x"], pl.ds(pl.multiple_of(owner * BLOCK, BLOCK), BLOCK)
+            ],
+            send_sem=row_send.at[2 * j + t],
+            recv_sem=row_recv.at[2 * j + t],
+            device_id=place,
+            device_id_type=MESH,
+        )
+
+    def rows_wait(j, t):
+        ref = xg.at[2 * j + t, my["z"], my["x"], pl.ds(0, ROWS - BLOCK)]
+        return pltpu.make_async_remote_copy(
+            src_ref=ref,
+            dst_ref=ref,
+            send_sem=row_send.at[2 * j + t],
+            recv_sem=row_recv.at[2 * j + t],
+            device_id=partner(1)[1],
+            device_id_type=MESH,
+        )
+
+    def tokens(j):
+        for t in range(2):
+            k = 2 * j + t
+            columns = columns_of(k)
+            for i in range(1, GROUPS):
+                term_copy(j, t, i).wait_recv()
+            total = mixed[lax.rem(j, 2), t, my_exp].astype(f32)
+            for i in range(1, GROUPS):
+                total = total + terms[k, i - 1].astype(f32)
+            value = (residual_ref[:, columns].astype(f32) + total).astype(bf16)
+            hidden[:, columns] = value
+            rows = jnp.dot(placing[...], value, preferred_element_type=f32).astype(bf16)
+            leaving[lax.rem(j, 2), t] = rows.reshape(EXPERTS, BLOCK, WIDTH)
+            for o in range(1, EXPERTS):
+                row_copy(j, t, o).start()
+            xg[k, my["z"], my["x"], pl.ds(pl.multiple_of(owner * BLOCK, BLOCK), BLOCK)] = leaving[
+                lax.rem(j, 2), t, owner
+            ]
+            logits[...] += lax.dot_general(
+                router_ref[:, columns],
+                value,
+                (((1,), (1,)), ((), ())),
+                preferred_element_type=f32,
+            )
+
+    def rows_arrive(j):
+        for t in range(2):
+            rows_wait(j, t).wait_recv()
+
+    def tokens_sent(j):
+        for t in range(2):
+            for i in range(1, GROUPS):
+                term_copy(j, t, i).wait_send()
+            rows_wait(j, t).wait_send()
 
     every = pl.ds(0, SIDE)
     halves = {1: pl.ds(0, SIDE // 2), -1: pl.ds(SIDE // 2, SIDE // 2)}
@@ -145,23 +278,32 @@
                 else:
                     acc[n, rows, :] += total
 
+    fetch.wait()
+    mix(0)
+    mix(1)
+    tokens(0)
+    rows_arrive(0)
     ag_start(0, 0)
+    tokens(1)
     ag_arrive(0, 0)
     ag_start(0, 1)
+    tokens_sent(0)
+    mix(2)
     ag_arrive(0, 1)
     ag_start(0, 2)
     for load in loads:
         load.wait()
 
     def ag_round(j, first):
-        last = j == PAIRS - 1 if isinstance(j, int) else False
+        near_end = isinstance(j, int) and j > 1
+        last = near_end and j == PAIRS - 1
         if not last:
+            rows_arrive(j + 1)
             ag_start(j + 1, 0)
+            if not (near_end and j + 2 >= PAIRS):
+                tokens(j + 2)
         if not first:
-            if isinstance(j, int) and j == 1:
-                gate_up(0, True)
-            else:
-                gate_up(j - 1, False)
+            gate_up(j - 1, isinstance(j, int) and j == 1)
         if not last:
             ag_arrive(j + 1, 0)
             ag_start(j + 1, 1)
@@ -170,6 +312,9 @@
             ag_sent(j - 1)
         ag_start(j, 3)
         if not last:
+            tokens_sent(j + 1)
+            if not (near_end and j + 3 >= PAIRS):
+                mix(j + 3)
             ag_arrive(j + 1, 1)
             ag_start(j + 1, 2)
         ag_arrive(j, 3)
@@ -177,11 +322,12 @@
     ag_round(0, True)
     ag_round(1, False)
 
-    @pl.loop(2, PAIRS - 1)
+    @pl.loop(2, PAIRS - 3)
     def _(j):
         ag_round(j, False)
 
-    ag_round(PAIRS - 1, False)
+    for j in range(PAIRS - 3, PAIRS):
+        ag_round(j, False)
     gate_up(PAIRS - 1, False)
 
     @pl.loop(0, SIDE * SIDE)
@@ -247,7 +393,45 @@
                     2, ROWS, WIDTH
                 )
 
-    f32 = jnp.float32
+    def back_copy(j, t, o):
+        other, place = partner(o)
+        return pltpu.make_async_remote_copy(
+            src_ref=sums.at[lax.rem(j, 2), t, other],
+            dst_ref=returned.at[2 * j + t, pl.ds(pl.multiple_of(owner * BLOCK, BLOCK), BLOCK)],
+            send_sem=back_send.at[2 * j + t],
+            recv_sem=back_recv.at[2 * j + t],
+            device_id=place,
+            device_id_type=MESH,
+        )
+
+    def back_wait(j, t):
+        ref = returned.at[2 * j + t, pl.ds(0, ROWS - BLOCK)]
+        return pltpu.make_async_remote_copy(
+            src_ref=ref,
+            dst_ref=ref,
+            send_sem=back_send.at[2 * j + t],
+            recv_sem=back_recv.at[2 * j + t],
+            device_id=partner(1)[1],
+            device_id_type=MESH,
+        )
+
+    def finish(j):
+        for t in range(2):
+            back_wait(j, t).wait_recv()
+            columns = columns_of(2 * j + t)
+            total = hidden[:, columns].astype(f32)
+            for n in range(2):
+                total = total + lax.dot_general(
+                    shares[n],
+                    returned[2 * j + t],
+                    (((0,), (0,)), ((), ())),
+                    preferred_element_type=f32,
+                )
+            out_ref[:, columns] = total.astype(bf16)
+
+    def sums_sent(j):
+        for t in range(2):
+            back_wait(j, t).wait_send()
 
     def add_first(j, t):
         far, near = axes[t][1], axes[t][0]
@@ -294,8 +478,10 @@
             + xg[2 * j + t, 3, 1].astype(f32)
             + xg[2 * j + t, 3, 2].astype(f32)
         )
-        start = (2 * j + t) * WIDTH
-        out_ref[:, pl.ds(pl.multiple_of(start, WIDTH), WIDTH)] = total.astype(jnp.bfloat16)
+        sums[s, t] = total.astype(bf16).reshape(EXPERTS, BLOCK, WIDTH)
+        for o in range(1, EXPERTS):
+            back_copy(j, t, o).start()
+        returned[2 * j + t, pl.ds(pl.multiple_of(owner * BLOCK, BLOCK), BLOCK)] = sums[s, t, owner]
 
     def rs_second(j):
         for t in range(2):
@@ -328,38 +514,74 @@
     down(0)
     both(0)
     down(1)
+
+    match = [
+        lax.broadcasted_iota(jnp.int32, (EXPERTS, TOKENS), 0) == chosen_ref[i : i + 1, :]
+        for i in range(2)
+    ]
+    picked = [jnp.sum(jnp.where(m, logits[...], 0.0), axis=0, keepdims=True) for m in match]
+    weights = jnp.zeros((ROWS, TOKENS), f32)
+    for i in range(2):
+        share = 1.0 / (1.0 + jnp.exp(picked[1 - i] - picked[i]))
+        weights = weights + jnp.where(row_id == target[i : i + 1, :], share, 0.0)
+    coarse = weights.astype(bf16)
+    shares[0] = coarse
+    shares[1] = (weights - coarse.astype(f32)).astype(bf16)
+
     rs_begin(0)
     both(1)
 
-    @pl.loop(0, PAIRS - 1)
+    def rs_round(j, first, last):
+        rs_second(j)
+        if not last:
+            rs_begin(j + 1)
+        rs_third(j)
+        if not first:
+            sums_sent(j - 1)
+            finish(j - 1)
+        rs_end(j)
+
+    rs_round(0, True, False)
+    down(2)
+    both(2)
+
+    @pl.loop(1, PAIRS - 2)
     def _(j):
-        rs_second(j)
-        rs_begin(j + 1)
-        rs_third(j)
-        rs_end(j)
-
-        @pl.when(j + 2 < PAIRS)
-        def _():
-            down(j + 2)
-            both(j + 2)
-
-    rs_second(PAIRS - 1)
-    rs_third(PAIRS - 1)
-    rs_end(PAIRS - 1)
-
-
-def experts(rows, gate_w, up_w, down_w):
+        rs_round(j, False, False)
+        down(j + 2)
+        both(j + 2)
+
+    rs_round(PAIRS - 2, False, False)
+    rs_round(PAIRS - 1, False, True)
+    sums_sent(PAIRS - 1)
+    finish(PAIRS - 1)
+
+
+def layer(normed, mix_w, residual, router, chosen, slots, spills, gate_w, up_w, down_w):
     hidden = gate_w.shape[1]
-    bf16 = jnp.bfloat16
+    length, inner = normed.shape
+    bf16, f32 = jnp.bfloat16, jnp.float32
     any_space = pl.BlockSpec(memory_space=pl.ANY)
+    vmem = pl.BlockSpec(memory_space=pltpu.VMEM)
     return pl.pallas_call(
-        experts_kernel,
-        out_shape=jax.ShapeDtypeStruct((ROWS, D), bf16),
-        in_specs=[any_space] * 4,
-        out_specs=pl.BlockSpec(memory_space=pltpu.VMEM),
+        layer_kernel,
+        out_shape=jax.ShapeDtypeStruct((TOKENS, D), bf16),
+        in_specs=[any_space] * 2 + [vmem] * 5 + [any_space] * 3,
+        out_specs=vmem,
         scratch_shapes=[
+            pltpu.VMEM((length, inner), bf16),
+            pltpu.VMEM((inner, D), bf16),
+            pltpu.VMEM((2, 2, GROUPS, TOKENS, WIDTH), bf16),
+            pltpu.VMEM((2 * PAIRS, GROUPS - 1, TOKENS, WIDTH), bf16),
+            pltpu.VMEM((TOKENS, D), bf16),
+            pltpu.VMEM((ROWS, TOKENS), bf16),
+            pltpu.VMEM((2, ROWS, TOKENS), bf16),
+            pltpu.VMEM((EXPERTS, TOKENS), f32),
+            pltpu.VMEM((2, 2, EXPERTS, BLOCK, WIDTH), bf16),
+            pltpu.VMEM((2, 2, EXPERTS, BLOCK, WIDTH), bf16),
+            pltpu.VMEM((2 * PAIRS, ROWS, WIDTH), bf16),
             pltpu.VMEM((2 * PAIRS, SIDE, SIDE, ROWS, WIDTH), bf16),
-            pltpu.VMEM((2, SIDE * SIDE * ROWS, hidden), jnp.float32),
+            pltpu.VMEM((2, SIDE * SIDE * ROWS, hidden), f32),
             pltpu.VMEM((SIDE * SIDE * ROWS, hidden), bf16),
             pltpu.VMEM((D, hidden), bf16),
             pltpu.VMEM((D, hidden), bf16),
@@ -370,43 +592,227 @@
             pltpu.SemaphoreType.DMA((PAIRS, 2, 8)),
             pltpu.SemaphoreType.DMA((PAIRS, 2, 8)),
             pltpu.SemaphoreType.DMA((PAIRS, 2, 8)),
+            pltpu.SemaphoreType.DMA((2 * PAIRS, GROUPS - 1)),
+            pltpu.SemaphoreType.DMA((2 * PAIRS, GROUPS - 1)),
+            pltpu.SemaphoreType.DMA((2 * PAIRS,)),
+            pltpu.SemaphoreType.DMA((2 * PAIRS,)),
+            pltpu.SemaphoreType.DMA((2 * PAIRS,)),
+            pltpu.SemaphoreType.DMA((2 * PAIRS,)),
             pltpu.SemaphoreType.DMA((3,)),
-            pltpu.SemaphoreType.DMA((2 * PAIRS,)),
+            pltpu.SemaphoreType.DMA((PAIRS,)),
+            pltpu.SemaphoreType.DMA,
         ],
         compiler_params=pltpu.CompilerParams(
-            collective_id=0, has_side_effects=True, vmem_limit_bytes=60 << 20
+            collective_id=0, has_side_effects=True, vmem_limit_bytes=62 << 20
         ),
         cost_estimate=pl.CostEstimate(
-            flops=6 * 2048 * D * 512, bytes_accessed=14 << 20, transcendentals=1 << 20
+            flops=6 * 2048 * D * 512, bytes_accessed=24 << 20, transcendentals=1 << 20
         ),
-    )(rows, gate_w, up_w, down_w)
-
-
-def entering_2(value, axis, combine, identity):
-    length, here = (lax.axis_size(axis), lax.axis_index(axis))
-    everything = jax.tree.map(
-        lambda part, kind: lax.all_gather(part.astype(kind), axis),
-        value,
-        (jnp.bfloat16, jnp.bfloat16),
+    )(normed, mix_w, residual, router, chosen, slots, spills, gate_w, up_w, down_w)
+
+
+HEADS = 16
+SIZE = 64
+STATE = 128
+CTX = SIDE * SIDE
+MESSAGE = SIZE + 16
+
+
+def scan_kernel(
+    mixer_ref,
+    gate_ref,
+    write_ref,
+    read_ref,
+    decay_ref,
+    skip_ref,
+    gain_ref,
+    start_ref,
+    out_ref,
+    leaving,
+    gathered,
+    entering,
+    returned,
+    start,
+    acc,
+    out_send,
+    out_recv,
+    back_send,
+    back_recv,
+    start_sem,
+):
+    here = lax.axis_index("ctx")
+    f32, bf16 = jnp.float32, jnp.bfloat16
+    length = mixer_ref.shape[0]
+    mine = pltpu.make_async_copy(
+        start_ref.at[pl.ds(pl.multiple_of(here * SIZE, SIZE), SIZE), :], start, start_sem
     )
-    start = jax.tree.map(
-        lambda part, zero: jnp.broadcast_to(jnp.asarray(zero, part.dtype), part.shape),
-        value,
-        identity,
+    mine.start()
+
+    barrier = pltpu.get_barrier_semaphore()
+
+    def greet(k, _):
+        other = lax.rem(here + k, CTX)
+        pl.semaphore_signal(barrier, inc=1, device_id={"ctx": other}, device_id_type=MESH)
+        return 0
+
+    lax.fori_loop(1, CTX, greet, 0)
+
+    row_id = lax.broadcasted_iota(jnp.int32, (length, length), 0)
+    col_id = lax.broadcasted_iota(jnp.int32, (length, length), 1)
+    causal = row_id >= col_id
+    upper = jnp.where(row_id <= col_id, 1.0, 0.0).astype(f32)
+    levels = jnp.dot(
+        decay_ref[...], upper, precision=lax.Precision.HIGHEST, preferred_element_type=f32
     )
-
-    def hop(k, before):
-        reached = k < here
-        new = combine(
-            before, jax.tree.map(lambda part, own: part[k].astype(own.dtype), everything, value)
-        )
-        return jax.tree.map(lambda a, b: jnp.where(reached, a, b), new, before)
-
-    return lax.fori_loop(0, length, hop, start)
-
-
-def chain_combine(earlier, later):
-    return (earlier[0] * later[0], later[0][:, None, None] * earlier[1] + later[1])
+    last = levels[:, length - 1 : length]
+    to_end = jnp.exp(levels - last).T
+    total = jnp.exp(-last)
+    levels_t = levels.T
+    from_start = jnp.exp(-levels_t)
+    low = lax.broadcasted_iota(jnp.int32, (length, 2 * SIZE), 1) < SIZE
+    top = lax.broadcasted_iota(jnp.int32, (16, STATE), 0) < 8
+
+    def spread(columns, q):
+        return jnp.where(low, columns[:, 2 * q : 2 * q + 1], columns[:, 2 * q + 1 : 2 * q + 2])
+
+    for q in range(HEADS // 2):
+        lanes = pl.ds(q * 2 * SIZE, 2 * SIZE)
+        scaled = (spread(to_end, q) * mixer_ref[:, lanes].astype(f32)).astype(bf16)
+        local = lax.dot_general(
+            scaled, write_ref[...], (((0,), (0,)), ((), ())), preferred_element_type=f32
+        )
+        for i in range(2):
+            h = 2 * q + i
+            leaving[h, 0:SIZE] = local[i * SIZE : (i + 1) * SIZE].astype(bf16)
+            value = jnp.broadcast_to(total[h : h + 1, :], (16, STATE))
+            coarse = value.astype(bf16)
+            rest = (value - coarse.astype(f32)).astype(bf16)
+            leaving[h, SIZE:MESSAGE] = jnp.where(top, coarse, rest)
+
+    pl.semaphore_wait(barrier, CTX - 1)
+
+    def out_copy(k):
+        other = lax.rem(here + k, CTX)
+        return pltpu.make_async_remote_copy(
+            src_ref=leaving.at[other],
+            dst_ref=gathered.at[here],
+            send_sem=out_send.at[k],
+            recv_sem=out_recv.at[k],
+            device_id={"ctx": other},
+            device_id_type=MESH,
+        )
+
+    def back_copy(k):
+        other = lax.rem(here + k, CTX)
+        return pltpu.make_async_remote_copy(
+            src_ref=entering.at[other],
+            dst_ref=returned.at[here],
+            send_sem=back_send.at[k],
+            recv_sem=back_recv.at[k],
+            device_id={"ctx": other},
+            device_id_type=MESH,
+        )
+
+    def each(action):
+        def step(k, _):
+            action(k)
+            return 0
+
+        lax.fori_loop(1, CTX, step, 0)
+
+    each(lambda k: out_copy(k).start())
+    gathered[here] = leaving[here]
+
+    meet = lax.dot_general(
+        read_ref[...], write_ref[...], (((1,), (1,)), ((), ())), preferred_element_type=f32
+    )
+
+    def within(q):
+        lanes = pl.ds(q * 2 * SIZE, 2 * SIZE)
+        pair = mixer_ref[:, lanes]
+        halves = []
+        for i in range(2):
+            h = 2 * q + i
+            span = levels[h : h + 1, :] - levels_t[:, h : h + 1]
+            weight = jnp.exp(jnp.where(causal, span, -1e30)) * meet
+            halves.append(jnp.dot(weight.astype(bf16), pair, preferred_element_type=f32))
+        skip = jnp.where(low, skip_ref[2 * q], skip_ref[2 * q + 1])
+        acc[:, lanes] = jnp.where(low, halves[0], halves[1]) + skip * pair.astype(f32)
+
+    EARLY = 3
+    for q in range(EARLY):
+        within(q)
+
+    mine.wait()
+    each(lambda k: out_copy(k).wait_recv())
+    state = start[...]
+    for k in range(CTX):
+        entering[k] = state.astype(bf16)
+        if k < CTX - 1:
+            factor = gathered[k, SIZE:MESSAGE].astype(f32)
+            factor = factor[0:1, :] + factor[8:9, :]
+            state = factor * state + gathered[k, 0:SIZE].astype(f32)
+    each(lambda k: back_copy(k).start())
+    returned[here] = entering[here]
+
+    for q in range(EARLY, HEADS // 2):
+        within(q)
+
+    each(lambda k: back_copy(k).wait_recv())
+    square = jnp.zeros((length, 1), f32)
+    for q in range(HEADS // 2):
+        lanes = pl.ds(q * 2 * SIZE, 2 * SIZE)
+        entered = returned[2 * q : 2 * q + 2].reshape(2 * SIZE, STATE)
+        carried = lax.dot_general(
+            read_ref[...], entered, (((1,), (1,)), ((), ())), preferred_element_type=f32
+        )
+        gate = gate_ref[:, lanes].astype(f32)
+        gated = (acc[:, lanes] + carried * spread(from_start, q)) * (gate / (1.0 + jnp.exp(-gate)))
+        acc[:, lanes] = gated
+        square = square + jnp.sum(gated * gated, axis=1, keepdims=True)
+    scale = lax.rsqrt(square / (HEADS * SIZE) + 1e-05)
+    for q in range(HEADS // 2):
+        lanes = pl.ds(q * 2 * SIZE, 2 * SIZE)
+        out_ref[:, lanes] = (acc[:, lanes] * scale * gain_ref[:, lanes]).astype(bf16)
+
+    each(lambda k: out_copy(k).wait_send())
+    each(lambda k: back_copy(k).wait_send())
+
+
+def scan(mixer, gate, write, read, decay, skip, gain, start_state):
+    length, inner = mixer.shape
+    f32, bf16 = jnp.float32, jnp.bfloat16
+    vmem = pl.BlockSpec(memory_space=pltpu.VMEM)
+    return pl.pallas_call(
+        scan_kernel,
+        out_shape=jax.ShapeDtypeStruct((length, inner), bf16),
+        in_specs=[vmem] * 5
+        + [
+            pl.BlockSpec(memory_space=pltpu.SMEM),
+            vmem,
+            pl.BlockSpec(memory_space=pl.ANY),
+        ],
+        out_specs=vmem,
+        scratch_shapes=[
+            pltpu.VMEM((CTX, MESSAGE, STATE), bf16),
+            pltpu.VMEM((CTX, MESSAGE, STATE), bf16),
+            pltpu.VMEM((CTX, SIZE, STATE), bf16),
+            pltpu.VMEM((CTX, SIZE, STATE), bf16),
+            pltpu.VMEM((SIZE, STATE), f32),
+            pltpu.VMEM((length, inner), f32),
+            pltpu.SemaphoreType.DMA((CTX,)),
+            pltpu.SemaphoreType.DMA((CTX,)),
+            pltpu.SemaphoreType.DMA((CTX,)),
+            pltpu.SemaphoreType.DMA((CTX,)),
+            pltpu.SemaphoreType.DMA,
+        ],
+        compiler_params=pltpu.CompilerParams(
+            collective_id=1, has_side_effects=True, vmem_limit_bytes=60 << 20
+        ),
+        cost_estimate=pl.CostEstimate(
+            flops=1 << 29, bytes_accessed=4 << 20, transcendentals=1 << 20
+        ),
+    )(mixer, gate, write, read, decay, skip, gain, start_state)
 
 
 def shards(
@@ -428,81 +834,28 @@
     up_weight,
     down_weight,
 ):
-    exact = lax.Precision.HIGHEST
-    length = mixer_in.shape[1]
-    head_count = skip_gain.shape[0]
-    inner_width = mixer_in.shape[2]
-    head_size = inner_width // head_count
-    inputs = mixer_in[0].astype(jnp.float32).reshape(length, head_count, head_size)
-    write_rows = state_write[0, :, 0].astype(jnp.float32)
-    read_rows = state_read[0, :, 0].astype(jnp.float32)
-    levels = jnp.cumsum(decay_rate[0], axis=1)
-    locations = jnp.arange(length)
-    causal = locations[:, None] >= locations[None, :]
-    span_levels = levels[:, :, None] - levels[:, None, :]
-    decay_pairs = jnp.where(causal[None], jnp.exp(-jnp.where(causal[None], span_levels, 0.0)), 0.0)
-    intersections = jnp.dot(read_rows, write_rows.T, precision=exact)
-    within = jnp.einsum("hts,shp->thp", decay_pairs * intersections[None], inputs, precision=exact)
-    to_end = jnp.exp(levels - levels[:, -1:])
-    local_state = jnp.einsum("hs,shp,sn->hpn", to_end, inputs, write_rows, precision=exact)
-    totals = jnp.exp(-levels[:, -1])
-    before_decay, before_state = entering_2(
-        (totals, local_state),
-        "ctx",
-        chain_combine,
-        (jnp.ones_like(totals), jnp.zeros_like(local_state)),
+    normed = scan(
+        mixer_in[0],
+        gate_in[0],
+        state_write[0, :, 0],
+        state_read[0, :, 0],
+        decay_rate[0],
+        skip_gain,
+        norm_gain[None],
+        start_state[0].reshape(HEADS * SIZE, STATE),
     )
-    entering = before_decay[:, None, None] * start_state[0] + before_state
-    carried = (
-        jnp.einsum("tn,hpn->thp", read_rows, entering, precision=exact)
-        * jnp.exp(-levels).T[:, :, None]
-    )
-    head_out = within + carried + skip_gain[None, :, None] * inputs
-    gated_out = head_out.reshape(length, inner_width) * jax.nn.silu(gate_in[0].astype(jnp.float32))
-    normed = (
-        gated_out
-        * lax.rsqrt(jnp.mean(gated_out * gated_out, axis=1, keepdims=True) + 1e-05)
-        * norm_gain
-    ).astype(jnp.bfloat16)
-    mixer_out = lax.psum_scatter(
-        jnp.dot(normed, out_weight, preferred_element_type=jnp.float32).astype(jnp.bfloat16),
-        "exp",
-        scatter_dimension=0,
-        tiled=True,
-    ).astype(jnp.float32)
-    hidden = (residual[0].astype(jnp.float32) + mixer_out).astype(jnp.bfloat16)
-    logits = jnp.dot(hidden, router_weight, preferred_element_type=jnp.float32)
-    expert_ids = chosen[0]
-    matches = expert_ids[:, :, None] == jnp.arange(EXPERTS)[None, None, :]
-    picked = jnp.sum(jnp.where(matches, logits[:, None, :], 0.0), axis=2)
-    shares = jax.nn.sigmoid(picked - picked[:, ::-1])
-    slot_ids = slot_index[0]
-    spill_ids = spill_index[0]
-    target_row = jnp.where(
-        slot_ids >= 0,
-        expert_ids * BLOCK + slot_ids,
-        jnp.where(spill_ids >= 0, spill_ids // SPILL * BLOCK + CAP + spill_ids % SPILL, -1),
-    )
-    onehot = target_row[:, :, None] == jnp.arange(EXPERTS * BLOCK)[None, None, :]
-    placing = jnp.sum(onehot, axis=1).astype(jnp.bfloat16)
-    outgoing = lax.dot_general(
-        placing, hidden, (((0,), (0,)), ((), ())), preferred_element_type=jnp.float32
-    )
-    outgoing = outgoing.astype(jnp.bfloat16).reshape(EXPERTS, BLOCK, D)
-    own_gate = gate_weight[0]
-    own_up = up_weight[0]
-    own_down = down_weight[0]
-
-    arrived = lax.all_to_all(outgoing, ("exp", "dp"), split_axis=0, concat_axis=0, tiled=True)
-    summed = experts(arrived.reshape(ROWS, D), own_gate, own_up, own_down)
-    returned = lax.all_to_all(
-        summed.reshape(EXPERTS, BLOCK, D), ("exp", "dp"), split_axis=0, concat_axis=0, tiled=True
-    )
-    weighting = jnp.sum(jnp.where(onehot, shares[:, :, None], 0.0), axis=1)
-    expert_sum = jnp.dot(
-        weighting, returned.reshape(EXPERTS * BLOCK, D).astype(jnp.float32), precision=exact
-    )
-    return (hidden.astype(jnp.float32) + expert_sum).astype(jnp.bfloat16)[None]
+    return layer(
+        normed,
+        out_weight,
+        residual[0],
+        router_weight.T,
+        chosen[0].T,
+        slot_index[0].T,
+        spill_index[0].T,
+        gate_weight[0],
+        up_weight[0],
+        down_weight[0],
+    )[None]
 
 
 def solution(mesh):

time: 386 us -> 289 us (0.75)
  Pallas kernels: 201 us -> 287 us
  waiting for transfers between devices: 54.4 us -> 0 us
  blocking collectives: 54.2 us -> 0 us
  matrix products: 20.8 us -> 0 us
  other arithmetic: 19.1 us -> 0 us
  starting transfers between devices: 15.2 us -> 0 us
  between operations: 14.3 us -> 0.02 us
    pallas_call x1 -> x2, Pallas kernels: 201 us -> 287 us  [the longest x1 265 us: layer(): pl.pallas_call(layer_kernel, out_shape=jax.ShapeDtypeStruct((TOKENS, D),...]
    unnamed x1 -> x0, blocking collectives: 35.4 us -> none
    reduce_scatter x1 -> x0, waiting for transfers between devices: 29.3 us -> none  [shards(): lax.psum_scatter(jnp.dot(normed, out_weight, preferred_element_type=jnp.f...]
    dot_general x8 -> x0, matrix products: 20.8 us -> none  [the longest x1 7.55 us: shards(): jnp.dot(normed, out_weight, preferred_element_type=jnp.float32)]
    all_to_all x1 -> x0, blocking collectives: 18.8 us -> none  [shards(): lax.all_to_all(outgoing, ('exp', 'dp'), split_axis=0, concat_axis=0, tile...]
    select_n x33 -> x0, other arithmetic: 17.8 us -> none  [the longest x32 17.8 us: hop(): return jax.tree.map(lambda a, b: jnp.where(reached, a, b), new, before)]
    all_to_all x1 -> x0, starting transfers between devices: 15.2 us -> none  [shards(): lax.all_to_all(summed.reshape(EXPERTS, BLOCK, D), ('exp', 'dp'), split_ax...]
    all_to_all x1 -> x0, waiting for transfers between devices: 14.7 us -> none  [shards(): lax.all_to_all(summed.reshape(EXPERTS, BLOCK, D), ('exp', 'dp'), split_ax...]
  transfers between devices with their start and end apart: 3 -> 0, of which waited for: 3 -> 0; matrix products, arithmetic and copies ran while one was open for 2% -> 0% of each run, Pallas kernels for 0% -> 0%
where the time goes in v2:
time: 289 us
  Pallas kernels  287 us (99%)
    pallas_call x1, Pallas kernels, layer(): pl.pallas_call(layer_kernel, out_shape=jax.ShapeDtypeStruct((TOKENS, D),...  265 us
    pallas_call x1, Pallas kernels, scan(): pl.pallas_call(scan_kernel, out_shape=jax.ShapeDtypeStruct((length, inner...  22 us

profile of v2, /device:TPU:1, one launch (start us, length us, event | category | flops | bytes accessed | tf_op | source)
XLA Modules:
  0.0 289.1 jit_solution(6919507266429559468)
XLA Ops:
  0.0 22.0 %shard_map.163.normed_ref = bf16[256,1024]{1,0:T(8,128)(2,1)} custom-call(bf16[256,1024]{1,0:T(8,128)(2,1)} %bitcast.22, bf16[256,1024]{1,0:T(8,128)(2,1)} %bitcast.23, bf16[256,128]{1,0:T(8,128)(2,1)} %bitcast.26, bf16[256,128]{1,0:T(8,128)(2,1)} %bitcast.27, f32[16,256]{1,0:T(8,128)} %bitcast.28, f32[16]{0:T(128)} %skip_ref.1, f32[1,1024]{1,0:T(1,128)} %bitcast.29, ...), custom_call_target="tpu_custom_call" | custom-call | flops 536870912 | bytes 4194304 | tf_op jit(solution)/shard_map/pallas_call | solution.py:786
  22.0 265.2 %shard_map.164 = bf16[64,4096]{1,0:T(8,128)(2,1)} custom-call(bf16[256,1024]{1,0:T(8,128)(2,1)} %shard_map.163.normed_ref, bf16[1024,4096]{1,0:T(8,128)(2,1)} %mix_ref.1, bf16[64,4096]{1,0:T(8,128)(2,1)} %bitcast.33, bf16[8,4096]{1,0:T(8,128)(2,1)} %bitcast.34, s32[2,64]{1,0:T(2,128)} %bitcast.35, s32[2,64]{1,0:T(2,128)} %bitcast.36, s32[2,64]{1,0:T(2,128)} %bitcast.37, ...), custom_call_target="tpu_custom_call" | custom-call | flops 25769803776 | bytes 25165824 | tf_op jit(solution)/shard_map/pallas_call | solution.py:566
  287.2 1.9 copy.19

commit v3 on v2

--- a/solution.py
+++ b/solution.py
@@ -1,3 +1,5 @@
+import functools
+
 import jax
 import jax.numpy as jnp
 from jax import lax
@@ -33,7 +35,6 @@
     down_ref,
     out_ref,
     normed,
-    w_mix,
     mixed,
     terms,
     hidden,
@@ -86,15 +87,26 @@
     my_exp, my_dp = lax.axis_index("exp"), lax.axis_index("dp")
     owner = my_exp * 2 + my_dp
 
+    def columns_of(k):
+        return pl.ds(pl.multiple_of(k * WIDTH, WIDTH), WIDTH)
+
     fetch = pltpu.make_async_copy(normed_ref, normed, normed_sem)
     fetch.start()
 
-    def mix_load(j):
-        columns = pl.ds(pl.multiple_of(j * 2 * WIDTH, 2 * WIDTH), 2 * WIDTH)
-        return pltpu.make_async_copy(mix_ref.at[:, columns], w_mix.at[:, columns], mix_sem.at[j])
-
-    for j in range(PAIRS):
-        mix_load(j).start()
+    def mix_room(k):
+        slot, rest = lax.div(k, 4), lax.rem(k, 4)
+        return part.at[slot, lax.div(rest, 2), pl.ds(lax.rem(rest, 2) * 2, 2)]
+
+    def mix_load(k):
+        return pltpu.make_async_copy(
+            mix_ref.at[:, :, :, columns_of(k)], mix_room(k), mix_sem.at[k]
+        )
+
+    def load_mix(k, _):
+        mix_load(k).start()
+        return 0
+
+    lax.fori_loop(0, 2 * PAIRS, load_mix, 0)
     loads = [
         pltpu.make_async_copy(src, dst, load_sem.at[i])
         for i, (src, dst) in enumerate(((gate_ref, w_gate), (up_ref, w_up), (down_ref, w_down)))
@@ -131,9 +143,6 @@
     logits[...] = jnp.zeros_like(logits)
     pl.semaphore_wait(barrier, 4 + EXPERTS - 1)
 
-    def columns_of(k):
-        return pl.ds(pl.multiple_of(k * WIDTH, WIDTH), WIDTH)
-
     def term_copy(j, t, i):
         other = lax.rem(my_exp + i, GROUPS)
         return pltpu.make_async_remote_copy(
@@ -146,10 +155,12 @@
         )
 
     def mix(j):
-        mix_load(j).wait()
-        for t in range(2):
+        for t in range(2):
+            mix_load(2 * j + t).wait()
             term = jnp.dot(
-                normed[...], w_mix[:, columns_of(2 * j + t)], preferred_element_type=f32
+                normed[...],
+                mix_room(2 * j + t)[...].reshape(normed.shape[1], WIDTH),
+                preferred_element_type=f32,
             )
             mixed[lax.rem(j, 2), t] = term.astype(bf16).reshape(GROUPS, TOKENS, WIDTH)
             for i in range(1, GROUPS):
@@ -208,10 +219,13 @@
         for t in range(2):
             rows_wait(j, t).wait_recv()
 
-    def tokens_sent(j):
+    def terms_sent(j):
         for t in range(2):
             for i in range(1, GROUPS):
                 term_copy(j, t, i).wait_send()
+
+    def rows_sent(j):
+        for t in range(2):
             rows_wait(j, t).wait_send()
 
     every = pl.ds(0, SIDE)
@@ -260,75 +274,71 @@
                 for d in (1, -1):
                     ag_copy(j, t, step, d, False).wait_send()
 
-    def gate_up(j, first):
-        @pl.loop(0, SIDE * SIDE // 2)
-        def _(b):
-            zz, x0 = lax.div(b, 2), lax.rem(b, 2) * 2
-            rows = pl.ds(pl.multiple_of(b * 2 * ROWS, 2 * ROWS), 2 * ROWS)
+    def gate_up(j):
+        @pl.loop(0, SIDE)
+        def _(zz):
+            rows = pl.ds(pl.multiple_of(zz * SIDE * ROWS, SIDE * ROWS), SIDE * ROWS)
             for n, weight in enumerate((w_gate, w_up)):
-                total = None
+                total = acc[n, rows, :]
                 for t in range(2):
                     k = 2 * j + t
-                    left = xg[k, zz, pl.ds(x0, 2)].reshape(2 * ROWS, WIDTH)
-                    right = weight[pl.ds(pl.multiple_of(k * WIDTH, WIDTH), WIDTH), :]
-                    term = jnp.dot(left, right, preferred_element_type=jnp.float32)
-                    total = term if total is None else total + term
-                if first:
-                    acc[n, rows, :] = total
-                else:
-                    acc[n, rows, :] += total
-
+                    total += jnp.dot(
+                        xg[k, zz].reshape(SIDE * ROWS, WIDTH),
+                        weight[columns_of(k), :],
+                        preferred_element_type=f32,
+                    )
+                acc[n, rows, :] = total
+
+    def stages(tick, count, steps):
+        for lag, action in steps:
+            pl.when(jnp.logical_and(tick >= lag, tick < count + lag))(
+                functools.partial(action, tick - lag)
+            )
+
+    def gather_first(j):
+        rows_arrive(j)
+        ag_start(j, 0)
+        terms_sent(j)
+
+    def gather_second(j):
+        ag_arrive(j, 0)
+        ag_start(j, 1)
+        rows_sent(j)
+
+    def gather_third(j):
+        ag_arrive(j, 1)
+        ag_start(j, 2)
+
+    def gather_last(j):
+        ag_arrive(j, 2)
+        ag_start(j, 3)
+
+    def gathered(j):
+        ag_arrive(j, 3)
+        ag_sent(j)
+        gate_up(j)
+
+    acc[...] = jnp.zeros_like(acc)
     fetch.wait()
     mix(0)
-    mix(1)
-    tokens(0)
-    rows_arrive(0)
-    ag_start(0, 0)
-    tokens(1)
-    ag_arrive(0, 0)
-    ag_start(0, 1)
-    tokens_sent(0)
-    mix(2)
-    ag_arrive(0, 1)
-    ag_start(0, 2)
     for load in loads:
         load.wait()
 
-    def ag_round(j, first):
-        near_end = isinstance(j, int) and j > 1
-        last = near_end and j == PAIRS - 1
-        if not last:
-            rows_arrive(j + 1)
-            ag_start(j + 1, 0)
-            if not (near_end and j + 2 >= PAIRS):
-                tokens(j + 2)
-        if not first:
-            gate_up(j - 1, isinstance(j, int) and j == 1)
-        if not last:
-            ag_arrive(j + 1, 0)
-            ag_start(j + 1, 1)
-        ag_arrive(j, 2)
-        if not first:
-            ag_sent(j - 1)
-        ag_start(j, 3)
-        if not last:
-            tokens_sent(j + 1)
-            if not (near_end and j + 3 >= PAIRS):
-                mix(j + 3)
-            ag_arrive(j + 1, 1)
-            ag_start(j + 1, 2)
-        ag_arrive(j, 3)
-
-    ag_round(0, True)
-    ag_round(1, False)
-
-    @pl.loop(2, PAIRS - 3)
-    def _(j):
-        ag_round(j, False)
-
-    for j in range(PAIRS - 3, PAIRS):
-        ag_round(j, False)
-    gate_up(PAIRS - 1, False)
+    @pl.loop(1, PAIRS + 7)
+    def _(tick):
+        stages(
+            tick,
+            PAIRS,
+            (
+                (6, gather_last),
+                (4, gather_third),
+                (3, gather_second),
+                (2, gather_first),
+                (1, tokens),
+                (0, mix),
+                (7, gathered),
+            ),
+        )
 
     @pl.loop(0, SIDE * SIDE)
     def _(b):
@@ -336,11 +346,9 @@
         gate_val = acc[0, rows, :]
         act[rows, :] = (gate_val / (1.0 + jnp.exp(-gate_val)) * acc[1, rows, :]).astype(jnp.bfloat16)
 
-    ag_sent(PAIRS - 1)
-
     def rs_copy(j, t, step, d):
         near, far = axes[t]
-        p = part.at[lax.rem(j, 2), t]
+        p = part.at[lax.rem(j, 4), t]
         room = xg.at[2 * j + t]
         if step == 0:
             src = along(far, p, around(far, 2), halves[d])
@@ -349,10 +357,10 @@
             src = along(far, p, around(far, d), every)
             dst, to = room.at[1 + slot[d]], far
         elif step == 2:
-            src = line.at[lax.rem(j, 2), t, around(near, 2), half_rows[d]]
+            src = line.at[lax.rem(j, 4), t, around(near, 2), half_rows[d]]
             dst, to = room.at[3, 0, half_rows[d]], near
         else:
-            src = line.at[lax.rem(j, 2), t, around(near, d)]
+            src = line.at[lax.rem(j, 4), t, around(near, d)]
             dst, to = room.at[3, 1 + slot[d]], near
         m = step * 2 + slot[d]
         return pltpu.make_async_remote_copy(
@@ -372,26 +380,24 @@
         for d in (1, -1):
             rs_copy(j, t, step, d).wait_recv()
 
-    def rs_sent(j):
-        for step in range(4):
+    def rs_sent(j, steps):
+        for step in steps:
             for t in range(2):
                 for d in (1, -1):
                     rs_copy(j, t, step, d).wait_send()
 
     def down(j):
-        @pl.loop(0, SIDE * SIDE // 2)
-        def _(b):
-            zz, x0 = lax.div(b, 2), lax.rem(b, 2) * 2
-            rows = pl.ds(pl.multiple_of(b * 2 * ROWS, 2 * ROWS), 2 * ROWS)
+        @pl.loop(0, SIDE)
+        def _(zz):
+            rows = pl.ds(pl.multiple_of(zz * SIDE * ROWS, SIDE * ROWS), SIDE * ROWS)
             for t in range(2):
-                k = 2 * j + t
-                right = w_down[pl.ds(pl.multiple_of(k * WIDTH, WIDTH), WIDTH), :]
                 term = lax.dot_general(
-                    act[rows, :], right, (((1,), (1,)), ((), ())), preferred_element_type=jnp.float32
+                    act[rows, :],
+                    w_down[columns_of(2 * j + t), :],
+                    (((1,), (1,)), ((), ())),
+                    preferred_element_type=f32,
                 )
-                part[lax.rem(j, 2), t, zz, pl.ds(x0, 2)] = term.astype(jnp.bfloat16).reshape(
-                    2, ROWS, WIDTH
-                )
+                part[lax.rem(j, 4), t, zz] = term.astype(bf16).reshape(SIDE, ROWS, WIDTH)
 
     def back_copy(j, t, o):
         other, place = partner(o)
@@ -435,7 +441,7 @@
 
     def add_first(j, t):
         far, near = axes[t][1], axes[t][0]
-        s = lax.rem(j, 2)
+        s = lax.rem(j, 4)
         for d in (1, -1):
             base = 0 if d == 1 else SIDE // 2
             place = around(far, d)
@@ -449,7 +455,7 @@
 
     def add_line(j, t):
         far = axes[t][1]
-        s = lax.rem(j, 2)
+        s = lax.rem(j, 4)
 
         @pl.loop(0, SIDE)
         def _(i):
@@ -462,7 +468,7 @@
 
     def add_second(j, t):
         near = axes[t][0]
-        s = lax.rem(j, 2)
+        s = lax.rem(j, 4)
         for d in (1, -1):
             at = around(near, d)
             line[s, t, at, half_rows[d]] = (
@@ -472,89 +478,83 @@
 
     def add_last(j, t):
         near = axes[t][0]
-        s = lax.rem(j, 2)
+        s = lax.rem(j, 4)
         total = (
             line[s, t, my[near]].astype(f32)
             + xg[2 * j + t, 3, 1].astype(f32)
             + xg[2 * j + t, 3, 2].astype(f32)
         )
+        s = lax.rem(j, 2)
         sums[s, t] = total.astype(bf16).reshape(EXPERTS, BLOCK, WIDTH)
         for o in range(1, EXPERTS):
             back_copy(j, t, o).start()
         returned[2 * j + t, pl.ds(pl.multiple_of(owner * BLOCK, BLOCK), BLOCK)] = sums[s, t, owner]
 
-    def rs_second(j):
+    def sum_start(j):
+        down(j)
+        for t in range(2):
+            rs_start(j, 0, t)
+
+    def sum_first(j):
+        for t in range(2):
+            rs_arrive(j, 0, t)
+            add_first(j, t)
+            rs_start(j, 1, t)
+
+    def sum_second(j):
         for t in range(2):
             rs_arrive(j, 1, t)
             add_line(j, t)
             rs_start(j, 2, t)
-
-    def rs_third(j):
+        rs_sent(j, (0, 1))
+
+    def sum_third(j):
         for t in range(2):
             rs_arrive(j, 2, t)
             add_second(j, t)
             rs_start(j, 3, t)
 
-    def rs_begin(j):
-        for t in range(2):
-            rs_arrive(j, 0, t)
-            add_first(j, t)
-            rs_start(j, 1, t)
-
-    def rs_end(j):
+    def sum_last(j):
         for t in range(2):
             rs_arrive(j, 3, t)
             add_last(j, t)
-        rs_sent(j)
-
-    def both(j):
-        for t in range(2):
-            rs_start(j, 0, t)
-
-    down(0)
-    both(0)
-    down(1)
-
-    match = [
-        lax.broadcasted_iota(jnp.int32, (EXPERTS, TOKENS), 0) == chosen_ref[i : i + 1, :]
-        for i in range(2)
-    ]
-    picked = [jnp.sum(jnp.where(m, logits[...], 0.0), axis=0, keepdims=True) for m in match]
-    weights = jnp.zeros((ROWS, TOKENS), f32)
-    for i in range(2):
-        share = 1.0 / (1.0 + jnp.exp(picked[1 - i] - picked[i]))
-        weights = weights + jnp.where(row_id == target[i : i + 1, :], share, 0.0)
-    coarse = weights.astype(bf16)
-    shares[0] = coarse
-    shares[1] = (weights - coarse.astype(f32)).astype(bf16)
-
-    rs_begin(0)
-    both(1)
-
-    def rs_round(j, first, last):
-        rs_second(j)
-        if not last:
-            rs_begin(j + 1)
-        rs_third(j)
-        if not first:
-            sums_sent(j - 1)
-            finish(j - 1)
-        rs_end(j)
-
-    rs_round(0, True, False)
-    down(2)
-    both(2)
-
-    @pl.loop(1, PAIRS - 2)
-    def _(j):
-        rs_round(j, False, False)
-        down(j + 2)
-        both(j + 2)
-
-    rs_round(PAIRS - 2, False, False)
-    rs_round(PAIRS - 1, False, True)
-    sums_sent(PAIRS - 1)
-    finish(PAIRS - 1)
+        rs_sent(j, (2, 3))
+
+    def sum_back(j):
+        finish(j)
+        sums_sent(j)
+
+    def weigh():
+        match = [
+            lax.broadcasted_iota(jnp.int32, (EXPERTS, TOKENS), 0) == chosen_ref[i : i + 1, :]
+            for i in range(2)
+        ]
+        picked = [jnp.sum(jnp.where(m, logits[...], 0.0), axis=0, keepdims=True) for m in match]
+        weights = jnp.zeros((ROWS, TOKENS), f32)
+        for i in range(2):
+            share = 1.0 / (1.0 + jnp.exp(picked[1 - i] - picked[i]))
+            weights = weights + jnp.where(row_id == target[i : i + 1, :], share, 0.0)
+        coarse = weights.astype(bf16)
+        shares[0] = coarse
+        shares[1] = (weights - coarse.astype(f32)).astype(bf16)
+
+    sum_start(0)
+    weigh()
+
+    @pl.loop(1, PAIRS + 7)
+    def _(tick):
+        stages(
+            tick,
+            PAIRS,
+            (
+                (4, sum_second),
+                (2, sum_first),
+                (0, sum_start),
+                (5, sum_third),
+                (6, sum_last),
+                (7, sum_back),
+            ),
+        )
 
 
 def layer(normed, mix_w, residual, router, chosen, slots, spills, gate_w, up_w, down_w):
@@ -570,7 +570,6 @@
         out_specs=vmem,
         scratch_shapes=[
             pltpu.VMEM((length, inner), bf16),
-            pltpu.VMEM((inner, D), bf16),
             pltpu.VMEM((2, 2, GROUPS, TOKENS, WIDTH), bf16),
             pltpu.VMEM((2 * PAIRS, GROUPS - 1, TOKENS, WIDTH), bf16),
             pltpu.VMEM((TOKENS, D), bf16),
@@ -586,8 +585,8 @@
             pltpu.VMEM((D, hidden), bf16),
             pltpu.VMEM((D, hidden), bf16),
             pltpu.VMEM((D, hidden), bf16),
-            pltpu.VMEM((2, 2, SIDE, SIDE, ROWS, WIDTH), bf16),
-            pltpu.VMEM((2, 2, SIDE, ROWS, WIDTH), bf16),
+            pltpu.VMEM((4, 2, SIDE, SIDE, ROWS, WIDTH), bf16),
+            pltpu.VMEM((4, 2, SIDE, ROWS, WIDTH), bf16),
             pltpu.SemaphoreType.DMA((PAIRS, 2, 8)),
             pltpu.SemaphoreType.DMA((PAIRS, 2, 8)),
             pltpu.SemaphoreType.DMA((PAIRS, 2, 8)),
@@ -599,7 +598,7 @@
             pltpu.SemaphoreType.DMA((2 * PAIRS,)),
             pltpu.SemaphoreType.DMA((2 * PAIRS,)),
             pltpu.SemaphoreType.DMA((3,)),
-            pltpu.SemaphoreType.DMA((PAIRS,)),
+            pltpu.SemaphoreType.DMA((2 * PAIRS,)),
             pltpu.SemaphoreType.DMA,
         ],
         compiler_params=pltpu.CompilerParams(
@@ -846,7 +845,7 @@
     )
     return layer(
         normed,
-        out_weight,
+        out_weight.reshape(2, SIDE, ROWS, D),
         residual[0],
         router_weight.T,
         chosen[0].T,

time: 289 us -> 240 us (0.83)
  Pallas kernels: 287 us -> 238 us
    pallas_call x1, Pallas kernels: 265 us -> 216 us  [layer(): pl.pallas_call(layer_kernel, out_shape=jax.ShapeDtypeStruct((TOKENS, D),...]
where the time goes in v3:
time: 240 us; the launch traced here: 239 us
  Pallas kernels  238 us (99%)
    pallas_call x1, Pallas kernels, layer(): pl.pallas_call(layer_kernel, out_shape=jax.ShapeDtypeStruct((TOKENS, D),...  216 us
    pallas_call x1, Pallas kernels, scan(): pl.pallas_call(scan_kernel, out_shape=jax.ShapeDtypeStruct((length, inner...  22 us

profile of v3, /device:TPU:1, one launch (start us, length us, event | category | flops | bytes accessed | tf_op | source)
XLA Modules:
  0.0 239.4 jit_solution(13940581895000910004)
XLA Ops:
  0.0 22.0 %shard_map.163.normed_ref = bf16[256,1024]{1,0:T(8,128)(2,1)} custom-call(bf16[256,1024]{1,0:T(8,128)(2,1)} %bitcast.23, bf16[256,1024]{1,0:T(8,128)(2,1)} %bitcast.24, bf16[256,128]{1,0:T(8,128)(2,1)} %bitcast.27, bf16[256,128]{1,0:T(8,128)(2,1)} %bitcast.28, f32[16,256]{1,0:T(8,128)} %bitcast.29, f32[16]{0:T(128)} %skip_ref.1, f32[1,1024]{1,0:T(1,128)} %bitcast.30, ...), custom_call_target="tpu_custom_call" | custom-call | flops 536870912 | bytes 4194304 | tf_op jit(solution)/shard_map/pallas_call | solution.py:785
  22.0 215.5 %shard_map.164 = bf16[64,4096]{1,0:T(8,128)(2,1)} custom-call(bf16[256,1024]{1,0:T(8,128)(2,1)} %shard_map.163.normed_ref, bf16[2,4,128,4096]{3,2,1,0:T(8,128)(2,1)} %bitcast.31, bf16[64,4096]{1,0:T(8,128)(2,1)} %bitcast.35, bf16[8,4096]{1,0:T(8,128)(2,1)} %bitcast.36, s32[2,64]{1,0:T(2,128)} %bitcast.37, s32[2,64]{1,0:T(2,128)} %bitcast.38, ...), custom_call_target="tpu_custom_call" | custom-call | flops 25769803776 | bytes 25165824 | tf_op jit(solution)/shard_map/pallas_call | solution.py:566
  237.5 1.9 copy.19

commit v4 on v3

v4 whole, which is shorter than its diff:
```python
import functools

import jax
import jax.numpy as jnp
from jax import lax
from jax.experimental import pallas as pl
from jax.experimental.pallas import tpu as pltpu
from jax.sharding import PartitionSpec as P

D = 4096
EXPERTS = 8
CAP = 14
BLOCK = 16
TOKENS = 64
GROUPS = 4
SIDE = 4
WIDTH = 512
QUADS = D // WIDTH // 2
PAIRS = 2 * QUADS
PIECE = GROUPS * BLOCK
HALF = PIECE // 2
PLANE = SIDE * SIDE * PIECE
SUMS = 10
LAST = 7
MESH = pl.DeviceIdType.MESH


def layer_kernel(
    normed_ref,
    mix_ref,
    residual_ref,
    router_ref,
    chosen_ref,
    slot_ref,
    spill_ref,
    gate_ref,
    up_ref,
    down_ref,
    out_ref,
    normed,
    mixed,
    terms,
    hidden,
    placing,
    shares,
    logits,
    leaving,
    sums,
    returned,
    xg,
    acc,
    act,
    w_gate,
    w_up,
    w_down,
    part,
    line,
    ag_send,
    ag_recv,
    rs_send,
    rs_recv,
    mix_send,
    mix_recv,
    row_send,
    row_recv,
    back_send,
    back_recv,
    load_sem,
    mix_sem,
    normed_sem,
):
    f32, bf16 = jnp.float32, jnp.bfloat16
    here = lax.axis_index("ctx")
    my = {"x": lax.rem(here, SIDE), "z": lax.div(here, SIDE)}
    my_exp, my_dp = lax.axis_index("exp"), lax.axis_index("dp")
    owner = my_exp * 2 + my_dp

    def around(axis, step):
        return lax.rem(my[axis] + step + SIDE, SIDE)

    def neighbour(axis, step):
        other = around(axis, step)
        if axis == "x":
            return {"ctx": my["z"] * SIDE + other}
        return {"ctx": other * SIDE + my["x"]}

    def along(axis, ref, place, at):
        if axis == "z":
            return ref.at[place, at]
        return ref.at[at, place]

    def partner(o):
        other = lax.rem(owner + o, EXPERTS)
        return other, {"exp": lax.div(other, 2), "dp": lax.rem(other, 2)}

    def remote(src, dst, send, recv, place):
        return pltpu.make_async_remote_copy(
            src_ref=src,
            dst_ref=dst,
            send_sem=send,
            recv_sem=recv,
            device_id=place,
            device_id_type=MESH,
        )

    def columns_of(q):
        return pl.ds(pl.multiple_of(q * WIDTH, WIDTH), WIDTH)

    def rows_of(index, count):
        return pl.ds(pl.multiple_of(index * count, count), count)

    def mix_room(q):
        return part.at[lax.div(q, 2), lax.rem(q, 2)]

    def mix_load(q):
        return pltpu.make_async_copy(
            mix_ref.at[:, :, :, columns_of(q)], mix_room(q), mix_sem.at[q]
        )

    fetch = pltpu.make_async_copy(normed_ref, normed, normed_sem)
    fetch.start()
    loads = [
        pltpu.make_async_copy(src, dst, load_sem.at[i])
        for i, (src, dst) in enumerate(((gate_ref, w_gate), (up_ref, w_up), (down_ref, w_down)))
    ]

    def load_mix(q, _):
        mix_load(q).start()
        return 0

    lax.fori_loop(0, 2 * QUADS, load_mix, 0)

    barrier = pltpu.get_barrier_semaphore()
    for axis in ("x", "z"):
        for step in (1, -1):
            pl.semaphore_signal(
                barrier, inc=1, device_id=neighbour(axis, step), device_id_type=MESH
            )
    for o in range(1, EXPERTS):
        pl.semaphore_signal(barrier, inc=1, device_id=partner(o)[1], device_id_type=MESH)

    row_id = lax.broadcasted_iota(jnp.int32, (EXPERTS * BLOCK, TOKENS), 0)
    expert_ids, slot_ids, spill_ids = chosen_ref[...], slot_ref[...], spill_ref[...]
    target = jnp.where(
        slot_ids >= 0,
        expert_ids * BLOCK + slot_ids,
        jnp.where(
            spill_ids >= 0,
            jnp.right_shift(spill_ids, 1) * BLOCK + CAP + jnp.bitwise_and(spill_ids, 1),
            -1,
        ),
    )
    places = [row_id == target[i : i + 1, :] for i in range(2)]
    placing[...] = (places[0].astype(f32) + places[1].astype(f32)).astype(bf16)
    logits[...] = jnp.zeros_like(logits)
    fetch.wait()
    pl.semaphore_wait(barrier, 4 + EXPERTS - 1)

    every = pl.ds(0, SIDE)
    halves = {1: pl.ds(0, SIDE // 2), -1: pl.ds(SIDE // 2, SIDE // 2)}
    half_rows = {1: pl.ds(0, HALF), -1: pl.ds(HALF, HALF)}
    axes = (("x", "z"), ("z", "x"))
    slot = {1: 0, -1: 1}
    both = [(t, d) for t in range(2) for d in (1, -1)]


    def term_copy(c, t, i):
        other = lax.rem(my_exp + i, GROUPS)
        q = 2 * c + t
        return remote(
            mixed.at[lax.rem(c, 2), t, other],
            terms.at[q, i - 1],
            mix_send.at[q, i - 1],
            mix_recv.at[q, i - 1],
            {"exp": other},
        )

    def mix(c):
        for t in range(2):
            q = 2 * c + t
            mix_load(q).wait()
            term = jnp.dot(
                normed[...],
                mix_room(q)[...].reshape(normed.shape[1], WIDTH),
                preferred_element_type=f32,
            )
            mixed[lax.rem(c, 2), t] = term.astype(bf16).reshape(GROUPS, TOKENS, WIDTH)
            for i in range(1, GROUPS):
                term_copy(c, t, i).start()


    def row_copy(c, t, o):
        other, place = partner(o)
        k = 2 * (my_dp * QUADS + c) + t
        return remote(
            leaving.at[lax.rem(c, 2), t, other],
            xg.at[k, my["z"], my["x"], rows_of(my_exp, BLOCK)],
            row_send.at[2 * c + t],
            row_recv.at[k],
            place,
        )

    def tokens(c):
        for t in range(2):
            q = 2 * c + t
            columns = columns_of(q)
            for i in range(1, GROUPS):
                term_copy(c, t, i).wait_recv()
            total = mixed[lax.rem(c, 2), t, my_exp].astype(f32)
            for i in range(1, GROUPS):
                total = total + terms[q, i - 1].astype(f32)
            value = (residual_ref[:, columns].astype(f32) + total).astype(bf16)
            hidden[:, columns] = value
            rows = jnp.dot(placing[...], value, preferred_element_type=f32).astype(bf16)
            leaving[lax.rem(c, 2), t] = rows.reshape(EXPERTS, BLOCK, WIDTH)
            for o in range(1, EXPERTS):
                row_copy(c, t, o).start()
            k = 2 * (my_dp * QUADS + c) + t
            xg[k, my["z"], my["x"], rows_of(my_exp, BLOCK)] = leaving[lax.rem(c, 2), t, owner]
            logits[...] += lax.dot_general(
                router_ref[:, columns],
                value,
                (((1,), (1,)), ((), ())),
                preferred_element_type=f32,
            )
        for t in range(2):
            for i in range(1, GROUPS):
                term_copy(c, t, i).wait_send()

    def rows_sent(c):
        for t in range(2):
            ref = leaving.at[lax.rem(c, 2), t, pl.ds(0, EXPERTS - 1)]
            remote(ref, ref, row_send.at[2 * c + t], row_recv.at[0], partner(1)[1]).wait_send()


    def ag_copy(j, t, step, d, landing, off=0):
        near, far = axes[t]
        chunk = xg.at[2 * j + t]
        back = -d if landing else 0
        if step == 0:
            ref, to = along(near, chunk, around(near, back), my[far]), near
        elif step == 1:
            ref = along(near, chunk, around(near, -2 * d if landing else -d), my[far])
            ref, to = ref.at[half_rows[d]], near
        elif step == 2 and off is None:
            ref, to = along(far, chunk, around(far, back), every), far
        elif step == 2:
            ref, to = along(near, chunk, around(near, off), my[far]), far
        else:
            ref = along(far, chunk, around(far, -2 * d if landing else -d), halves[d])
            to = far
        m = step * 2 + slot[d]
        return remote(ref, ref, ag_send.at[j, t, m], ag_recv.at[j, t, m], neighbour(to, d))

    def ag_arrive(j, step):
        for t, d in both:
            ag_copy(j, t, step, d, True, None).wait_recv()

    def gather_first(j):
        mine = my_dp == lax.div(j, QUADS)
        for t in range(2):
            k = 2 * j + t

            def arrive(count):
                ref = xg.at[k, my["z"], my["x"], pl.ds(0, count)]
                remote(ref, ref, row_send.at[0], row_recv.at[k], partner(1)[1]).wait_recv()

            pl.when(mine)(functools.partial(arrive, PIECE - BLOCK))
            pl.when(jnp.logical_not(mine))(functools.partial(arrive, PIECE))
            for d in (1, -1):
                ag_copy(j, t, 0, d, False).start()
        for t, d in both:
            ag_copy(j, t, 2, d, False, 0).start()

    def gather_second(j):
        ag_arrive(j, 0)
        for t, d in both:
            ag_copy(j, t, 1, d, False).start()
        for t, d in both:
            for off in (1, -1):
                ag_copy(j, t, 2, d, False, off).start()

    def gather_third(j):
        ag_arrive(j, 1)
        for t, d in both:
            ag_copy(j, t, 2, d, False, 2).start()

    def gather_last(j):
        ag_arrive(j, 2)
        for t, d in both:
            ag_copy(j, t, 3, d, False).start()

    def gathered(j):
        h = lax.div(j, QUADS)
        c = lax.rem(j, QUADS)
        ag_arrive(j, 3)
        for step in range(4):
            for t, d in both:
                ag_copy(j, t, step, d, False, None).wait_send()

        @pl.when(j == 0)
        def _():
            for load in loads:
                load.wait()

        @pl.loop(0, 2)
        def _(b):
            rows = rows_of(h * 2 + b, PLANE // 2)
            for n, weight in enumerate((w_gate, w_up)):
                total = acc[n, rows, :]
                for t in range(2):
                    total += jnp.dot(
                        xg[2 * j + t, pl.ds(b * 2, 2)].reshape(PLANE // 2, WIDTH),
                        weight[columns_of(2 * c + t), :],
                        preferred_element_type=f32,
                    )
                acc[n, rows, :] = total

        @pl.when(c == QUADS - 1)
        def _():
            @pl.loop(0, 8)
            def _(b):
                rows = rows_of(h * 8 + b, PLANE // 8)
                gate = acc[0, rows, :]
                act[rows, :] = (gate / (1.0 + jnp.exp(-gate)) * acc[1, rows, :]).astype(bf16)


    def rs_copy(j, t, step, d):
        near, far = axes[t]
        p = part.at[lax.rem(j, 4), t]
        room = xg.at[2 * j + t]
        if step == 0:
            src = along(far, p, around(far, 2), halves[d])
            dst, to = room.at[0, halves[d]], far
        elif step == 1:
            src = along(far, p, around(far, d), every)
            dst, to = room.at[1 + slot[d]], far
        elif step == 2:
            src = line.at[lax.rem(j, 4), t, around(near, 2), half_rows[d]]
            dst, to = room.at[3, 0, half_rows[d]], near
        else:
            src = line.at[lax.rem(j, 4), t, around(near, d)]
            dst, to = room.at[3, 1 + slot[d]], near
        m = step * 2 + slot[d]
        return remote(src, dst, rs_send.at[j, t, m], rs_recv.at[j, t, m], neighbour(to, d))

    def rs_start(j, step, t):
        for d in (1, -1):
            rs_copy(j, t, step, d).start()

    def rs_arrive(j, step, t):
        for d in (1, -1):
            rs_copy(j, t, step, d).wait_recv()

    def rs_sent(j, steps):
        for step in steps:
            for t, d in both:
                rs_copy(j, t, step, d).wait_send()

    def sum_start(j):
        h = lax.div(j, QUADS)
        c = lax.rem(j, QUADS)

        @pl.loop(0, 2)
        def _(b):
            rows = rows_of(h * 2 + b, PLANE // 2)
            for t in range(2):
                term = lax.dot_general(
                    act[rows, :],
                    w_down[columns_of(2 * c + t), :],
                    (((1,), (1,)), ((), ())),
                    preferred_element_type=f32,
                )
                part[lax.rem(j, 4), t, pl.ds(b * 2, 2)] = term.astype(bf16).reshape(
                    2, SIDE, PIECE, WIDTH
                )

        for t in range(2):
            rs_start(j, 0, t)

    def sum_first(j):
        s = lax.rem(j, 4)
        for t in range(2):
            far = axes[t][1]
            rs_arrive(j, 0, t)
            for d in (1, -1):
                base = 0 if d == 1 else SIDE // 2
                place = around(far, d)

                @pl.loop(0, SIDE // 2)
                def _(i):
                    at = (place, base + i) if far == "z" else (base + i, place)
                    part[s, t, at[0], at[1]] = (
                        part[s, t, at[0], at[1]].astype(f32)
                        + xg[2 * j + t, 0, base + i].astype(f32)
                    ).astype(bf16)

            rs_start(j, 1, t)

    def sum_second(j):
        s = lax.rem(j, 4)
        for t in range(2):
            far = axes[t][1]
            rs_arrive(j, 1, t)

            @pl.loop(0, SIDE)
            def _(i):
                at = (my[far], i) if far == "z" else (i, my[far])
                line[s, t, i] = (
                    part[s, t, at[0], at[1]].astype(f32)
                    + xg[2 * j + t, 1, i].astype(f32)
                    + xg[2 * j + t, 2, i].astype(f32)
                ).astype(bf16)

            rs_start(j, 2, t)
        rs_sent(j, (0, 1))

    def sum_third(j):
        s = lax.rem(j, 4)
        for t in range(2):
            rs_arrive(j, 2, t)
            for d in (1, -1):
                at = around(axes[t][0], d)
                line[s, t, at, half_rows[d]] = (
                    line[s, t, at, half_rows[d]].astype(f32)
                    + xg[2 * j + t, 3, 0, half_rows[d]].astype(f32)
                ).astype(bf16)
            rs_start(j, 3, t)


    def back_copy(j, t, o):
        other = lax.rem(my_exp + o, GROUPS)
        k = 2 * lax.rem(j, QUADS) + t
        return remote(
            sums.at[lax.rem(j, 2), t, other],
            returned.at[k, rows_of(owner, BLOCK)],
            back_send.at[2 * j + t],
            back_recv.at[k],
            {"exp": other, "dp": lax.div(j, QUADS)},
        )

    def sum_last(j):
        mine = my_dp == lax.div(j, QUADS)
        for t in range(2):
            rs_arrive(j, 3, t)
            total = (
                line[lax.rem(j, 4), t, my[axes[t][0]]].astype(f32)
                + xg[2 * j + t, 3, 1].astype(f32)
                + xg[2 * j + t, 3, 2].astype(f32)
            )
            s = lax.rem(j, 2)
            sums[s, t] = total.astype(bf16).reshape(GROUPS, BLOCK, WIDTH)
            for o in range(1, GROUPS):
                back_copy(j, t, o).start()

            @pl.when(mine)
            def _():
                k = 2 * lax.rem(j, QUADS) + t
                returned[k, rows_of(owner, BLOCK)] = sums[s, t, my_exp]

            @pl.when(jnp.logical_not(mine))
            def _():
                back_copy(j, t, 0).start()

        rs_sent(j, (2, 3))

    def sum_back(j):
        mine = my_dp == lax.div(j, QUADS)
        for t in range(2):
            q = 2 * lax.rem(j, QUADS) + t

            def sent(count):
                ref = sums.at[lax.rem(j, 2), t, pl.ds(0, count)]
                remote(
                    ref, ref, back_send.at[2 * j + t], back_recv.at[0], partner(1)[1]
                ).wait_send()

            @pl.when(mine)
            def _():
                ref = returned.at[q, pl.ds(0, (EXPERTS - 1) * BLOCK)]
                remote(ref, ref, back_send.at[0], back_recv.at[q], partner(1)[1]).wait_recv()
                columns = columns_of(q)
                total = hidden[:, columns].astype(f32)
                for n in range(2):
                    total = total + lax.dot_general(
                        shares[n],
                        returned[q],
                        (((0,), (0,)), ((), ())),
                        preferred_element_type=f32,
                    )
                out_ref[:, columns] = total.astype(bf16)
                sent(GROUPS - 1)

            pl.when(jnp.logical_not(mine))(functools.partial(sent, GROUPS))

    def weigh():
        match = [
            lax.broadcasted_iota(jnp.int32, (EXPERTS, TOKENS), 0) == chosen_ref[i : i + 1, :]
            for i in range(2)
        ]
        picked = [jnp.sum(jnp.where(m, logits[...], 0.0), axis=0, keepdims=True) for m in match]
        weights = jnp.zeros((EXPERTS * BLOCK, TOKENS), f32)
        for i in range(2):
            share = 1.0 / (1.0 + jnp.exp(picked[1 - i] - picked[i]))
            weights = weights + jnp.where(row_id == target[i : i + 1, :], share, 0.0)
        coarse = weights.astype(bf16)
        shares[0] = coarse
        shares[1] = (weights - coarse.astype(f32)).astype(bf16)

    def stages(tick, count, steps):
        for lag, action in steps:
            pl.when(jnp.logical_and(tick >= lag, tick < count + lag))(
                functools.partial(action, tick - lag)
            )

    for load in loads:
        load.start()
    acc[...] = jnp.zeros_like(acc)

    @pl.loop(0, 1 + SUMS + PAIRS + LAST)
    def _(turn):
        tick = turn - 1
        own = tick - my_dp * QUADS
        stages(
            tick,
            PAIRS,
            ((5, gather_last), (4, gather_third), (3, gather_second), (2, gather_first)),
        )
        stages(tick - SUMS, PAIRS, ((4, sum_second), (2, sum_first)))
        stages(own, QUADS, ((3, rows_sent), (1, tokens), (-1, mix)))
        stages(tick, PAIRS, ((6, gathered),))
        pl.when(tick == SUMS)(weigh)
        stages(
            tick - SUMS,
            PAIRS,
            ((0, sum_start), (5, sum_third), (6, sum_last), (7, sum_back)),
        )


def layer(normed, mix_w, residual, router, chosen, slots, spills, gate_w, up_w, down_w):
    units = gate_w.shape[1]
    length, inner = normed.shape
    bf16, f32 = jnp.bfloat16, jnp.float32
    any_space = pl.BlockSpec(memory_space=pl.ANY)
    vmem = pl.BlockSpec(memory_space=pltpu.VMEM)
    return pl.pallas_call(
        layer_kernel,
        out_shape=jax.ShapeDtypeStruct((TOKENS, D), bf16),
        in_specs=[any_space] * 2 + [vmem] * 5 + [any_space] * 3,
        out_specs=vmem,
        scratch_shapes=[
            pltpu.VMEM((length, inner), bf16),
            pltpu.VMEM((2, 2, GROUPS, TOKENS, WIDTH), bf16),
            pltpu.VMEM((2 * QUADS, GROUPS - 1, TOKENS, WIDTH), bf16),
            pltpu.VMEM((TOKENS, D), bf16),
            pltpu.VMEM((EXPERTS * BLOCK, TOKENS), bf16),
            pltpu.VMEM((2, EXPERTS * BLOCK, TOKENS), bf16),
            pltpu.VMEM((EXPERTS, TOKENS), f32),
            pltpu.VMEM((2, 2, EXPERTS, BLOCK, WIDTH), bf16),
            pltpu.VMEM((2, 2, GROUPS, BLOCK, WIDTH), bf16),
            pltpu.VMEM((2 * QUADS, EXPERTS * BLOCK, WIDTH), bf16),
            pltpu.VMEM((2 * PAIRS, SIDE, SIDE, PIECE, WIDTH), bf16),
            pltpu.VMEM((2, 2 * PLANE, units), f32),
            pltpu.VMEM((2 * PLANE, units), bf16),
            pltpu.VMEM((D, units), bf16),
            pltpu.VMEM((D, units), bf16),
            pltpu.VMEM((D, units), bf16),
            pltpu.VMEM((4, 2, SIDE, SIDE, PIECE, WIDTH), bf16),
            pltpu.VMEM((4, 2, SIDE, PIECE, WIDTH), bf16),
            pltpu.SemaphoreType.DMA((PAIRS, 2, 8)),
            pltpu.SemaphoreType.DMA((PAIRS, 2, 8)),
            pltpu.SemaphoreType.DMA((PAIRS, 2, 8)),
            pltpu.SemaphoreType.DMA((PAIRS, 2, 8)),
            pltpu.SemaphoreType.DMA((2 * QUADS, GROUPS - 1)),
            pltpu.SemaphoreType.DMA((2 * QUADS, GROUPS - 1)),
            pltpu.SemaphoreType.DMA((2 * QUADS,)),
            pltpu.SemaphoreType.DMA((2 * PAIRS,)),
            pltpu.SemaphoreType.DMA((2 * PAIRS,)),
            pltpu.SemaphoreType.DMA((2 * QUADS,)),
            pltpu.SemaphoreType.DMA((3,)),
            pltpu.SemaphoreType.DMA((2 * QUADS,)),
            pltpu.SemaphoreType.DMA,
        ],
        compiler_params=pltpu.CompilerParams(
            collective_id=0, has_side_effects=True, vmem_limit_bytes=62 << 20
        ),
        cost_estimate=pl.CostEstimate(
            flops=6 * 2048 * D * 512, bytes_accessed=24 << 20, transcendentals=1 << 20
        ),
    )(normed, mix_w, residual, router, chosen, slots, spills, gate_w, up_w, down_w)


HEADS = 16
SIZE = 64
STATE = 128
CTX = SIDE * SIDE
MESSAGE = SIZE + 16


def scan_kernel(
    mixer_ref,
    gate_ref,
    write_ref,
    read_ref,
    decay_ref,
    skip_ref,
    gain_ref,
    start_ref,
    out_ref,
    leaving,
    gathered,
    entering,
    returned,
    start,
    acc,
    out_send,
    out_recv,
    back_send,
    back_recv,
    start_sem,
):
    here = lax.axis_index("ctx")
    f32, bf16 = jnp.float32, jnp.bfloat16
    length = mixer_ref.shape[0]
    mine = pltpu.make_async_copy(
        start_ref.at[pl.ds(pl.multiple_of(here * SIZE, SIZE), SIZE), :], start, start_sem
    )
    mine.start()

    barrier = pltpu.get_barrier_semaphore()

    def greet(k, _):
        other = lax.rem(here + k, CTX)
        pl.semaphore_signal(barrier, inc=1, device_id={"ctx": other}, device_id_type=MESH)
        return 0

    lax.fori_loop(1, CTX, greet, 0)

    row_id = lax.broadcasted_iota(jnp.int32, (length, length), 0)
    col_id = lax.broadcasted_iota(jnp.int32, (length, length), 1)
    causal = row_id >= col_id
    upper = jnp.where(row_id <= col_id, 1.0, 0.0).astype(f32)
    levels = jnp.dot(
        decay_ref[...], upper, precision=lax.Precision.HIGHEST, preferred_element_type=f32
    )
    last = levels[:, length - 1 : length]
    to_end = jnp.exp(levels - last).T
    total = jnp.exp(-last)
    levels_t = levels.T
    from_start = jnp.exp(-levels_t)
    low = lax.broadcasted_iota(jnp.int32, (length, 2 * SIZE), 1) < SIZE
    top = lax.broadcasted_iota(jnp.int32, (16, STATE), 0) < 8

    def spread(columns, q):
        return jnp.where(low, columns[:, 2 * q : 2 * q + 1], columns[:, 2 * q + 1 : 2 * q + 2])

    for q in range(HEADS // 2):
        lanes = pl.ds(q * 2 * SIZE, 2 * SIZE)
        scaled = (spread(to_end, q) * mixer_ref[:, lanes].astype(f32)).astype(bf16)
        local = lax.dot_general(
            scaled, write_ref[...], (((0,), (0,)), ((), ())), preferred_element_type=f32
        )
        for i in range(2):
            h = 2 * q + i
            leaving[h, 0:SIZE] = local[i * SIZE : (i + 1) * SIZE].astype(bf16)
            value = jnp.broadcast_to(total[h : h + 1, :], (16, STATE))
            coarse = value.astype(bf16)
            rest = (value - coarse.astype(f32)).astype(bf16)
            leaving[h, SIZE:MESSAGE] = jnp.where(top, coarse, rest)

    pl.semaphore_wait(barrier, CTX - 1)

    def out_copy(k):
        other = lax.rem(here + k, CTX)
        return pltpu.make_async_remote_copy(
            src_ref=leaving.at[other],
            dst_ref=gathered.at[here],
            send_sem=out_send.at[k],
            recv_sem=out_recv.at[k],
            device_id={"ctx": other},
            device_id_type=MESH,
        )

    def back_copy(k):
        other = lax.rem(here + k, CTX)
        return pltpu.make_async_remote_copy(
            src_ref=entering.at[other],
            dst_ref=returned.at[here],
            send_sem=back_send.at[k],
            recv_sem=back_recv.at[k],
            device_id={"ctx": other},
            device_id_type=MESH,
        )

    def each(action):
        def step(k, _):
            action(k)
            return 0

        lax.fori_loop(1, CTX, step, 0)

    each(lambda k: out_copy(k).start())
    gathered[here] = leaving[here]

    meet = lax.dot_general(
        read_ref[...], write_ref[...], (((1,), (1,)), ((), ())), preferred_element_type=f32
    )

    def within(q):
        lanes = pl.ds(q * 2 * SIZE, 2 * SIZE)
        pair = mixer_ref[:, lanes]
        halves = []
        for i in range(2):
            h = 2 * q + i
            span = levels[h : h + 1, :] - levels_t[:, h : h + 1]
            weight = jnp.exp(jnp.where(causal, span, -1e30)) * meet
            halves.append(jnp.dot(weight.astype(bf16), pair, preferred_element_type=f32))
        skip = jnp.where(low, skip_ref[2 * q], skip_ref[2 * q + 1])
        acc[:, lanes] = jnp.where(low, halves[0], halves[1]) + skip * pair.astype(f32)

    EARLY = 3
    for q in range(EARLY):
        within(q)

    mine.wait()
    each(lambda k: out_copy(k).wait_recv())
    state = start[...]
    for k in range(CTX):
        entering[k] = state.astype(bf16)
        if k < CTX - 1:
            factor = gathered[k, SIZE:MESSAGE].astype(f32)
            factor = factor[0:1, :] + factor[8:9, :]
            state = factor * state + gathered[k, 0:SIZE].astype(f32)
    each(lambda k: back_copy(k).start())
    returned[here] = entering[here]

    for q in range(EARLY, HEADS // 2):
        within(q)

    each(lambda k: back_copy(k).wait_recv())
    square = jnp.zeros((length, 1), f32)
    for q in range(HEADS // 2):
        lanes = pl.ds(q * 2 * SIZE, 2 * SIZE)
        entered = returned[2 * q : 2 * q + 2].reshape(2 * SIZE, STATE)
        carried = lax.dot_general(
            read_ref[...], entered, (((1,), (1,)), ((), ())), preferred_element_type=f32
        )
        gate = gate_ref[:, lanes].astype(f32)
        gated = (acc[:, lanes] + carried * spread(from_start, q)) * (gate / (1.0 + jnp.exp(-gate)))
        acc[:, lanes] = gated
        square = square + jnp.sum(gated * gated, axis=1, keepdims=True)
    scale = lax.rsqrt(square / (HEADS * SIZE) + 1e-05)
    for q in range(HEADS // 2):
        lanes = pl.ds(q * 2 * SIZE, 2 * SIZE)
        out_ref[:, lanes] = (acc[:, lanes] * scale * gain_ref[:, lanes]).astype(bf16)

    each(lambda k: out_copy(k).wait_send())
    each(lambda k: back_copy(k).wait_send())


def scan(mixer, gate, write, read, decay, skip, gain, start_state):
    length, inner = mixer.shape
    f32, bf16 = jnp.float32, jnp.bfloat16
    vmem = pl.BlockSpec(memory_space=pltpu.VMEM)
    return pl.pallas_call(
        scan_kernel,
        out_shape=jax.ShapeDtypeStruct((length, inner), bf16),
        in_specs=[vmem] * 5
        + [
            pl.BlockSpec(memory_space=pltpu.SMEM),
            vmem,
            pl.BlockSpec(memory_space=pl.ANY),
        ],
        out_specs=vmem,
        scratch_shapes=[
            pltpu.VMEM((CTX, MESSAGE, STATE), bf16),
            pltpu.VMEM((CTX, MESSAGE, STATE), bf16),
            pltpu.VMEM((CTX, SIZE, STATE), bf16),
            pltpu.VMEM((CTX, SIZE, STATE), bf16),
            pltpu.VMEM((SIZE, STATE), f32),
            pltpu.VMEM((length, inner), f32),
            pltpu.SemaphoreType.DMA((CTX,)),
            pltpu.SemaphoreType.DMA((CTX,)),
            pltpu.SemaphoreType.DMA((CTX,)),
            pltpu.SemaphoreType.DMA((CTX,)),
            pltpu.SemaphoreType.DMA,
        ],
        compiler_params=pltpu.CompilerParams(
            collective_id=1, has_side_effects=True, vmem_limit_bytes=60 << 20
        ),
        cost_estimate=pl.CostEstimate(
            flops=1 << 29, bytes_accessed=4 << 20, transcendentals=1 << 20
        ),
    )(mixer, gate, write, read, decay, skip, gain, start_state)


def shards(
    mixer_in,
    gate_in,
    state_write,
    state_read,
    decay_rate,
    skip_gain,
    norm_gain,
    start_state,
    out_weight,
    residual,
    router_weight,
    chosen,
    slot_index,
    spill_index,
    gate_weight,
    up_weight,
    down_weight,
):
    normed = scan(
        mixer_in[0],
        gate_in[0],
        state_write[0, :, 0],
        state_read[0, :, 0],
        decay_rate[0],
        skip_gain,
        norm_gain[None],
        start_state[0].reshape(HEADS * SIZE, STATE),
    )
    return layer(
        normed,
        out_weight.reshape(SIDE, SIDE, PIECE, D),
        residual[0],
        router_weight.T,
        chosen[0].T,
        slot_index[0].T,
        spill_index[0].T,
        gate_weight[0],
        up_weight[0],
        down_weight[0],
    )[None]


def solution(mesh):
    placed = (
        P("dp", "ctx", "exp"),
        P("dp", "ctx", "exp"),
        P("dp", "ctx", "exp", None),
        P("dp", "ctx", "exp", None),
        P("dp", "exp", "ctx"),
        P("exp"),
        P("exp"),
        P("dp", "exp", None, None),
        P("exp", None),
        P("dp", ("ctx", "exp"), None),
        P(),
        P("dp", ("ctx", "exp"), None),
        P("dp", ("ctx", "exp"), None),
        P("dp", ("ctx", "exp"), None),
        P(("exp", "dp"), None, "ctx"),
        P(("exp", "dp"), None, "ctx"),
        P(("exp", "dp"), None, "ctx"),
    )
    return jax.shard_map(
        shards, mesh=mesh, in_specs=placed, out_specs=P("dp", ("ctx", "exp"), None), check_vma=False
    )
```

time: 240 us -> 228 us (0.950)
  Pallas kernels: 238 us -> 226 us
    pallas_call x1, Pallas kernels: 216 us -> 204 us  [layer(): pl.pallas_call(layer_kernel, out_shape=jax.ShapeDtypeStruct((TOKENS, D),...]
where the time goes in v4:
time: 228 us
  Pallas kernels  226 us (99%)
    pallas_call x1, Pallas kernels, layer(): pl.pallas_call(layer_kernel, out_shape=jax.ShapeDtypeStruct((TOKENS, D),...  204 us
    pallas_call x1, Pallas kernels, scan(): pl.pallas_call(scan_kernel, out_shape=jax.ShapeDtypeStruct((length, inner...  22 us

profile of v4, /device:TPU:1, one launch (start us, length us, event | category | flops | bytes accessed | tf_op | source)
XLA Modules:
  0.0 227.8 jit_solution(837860800422120697)
XLA Ops:
  0.0 22.0 %shard_map.163.normed_ref = bf16[256,1024]{1,0:T(8,128)(2,1)} custom-call(bf16[256,1024]{1,0:T(8,128)(2,1)} %bitcast.23, bf16[256,1024]{1,0:T(8,128)(2,1)} %bitcast.24, bf16[256,128]{1,0:T(8,128)(2,1)} %bitcast.27, bf16[256,128]{1,0:T(8,128)(2,1)} %bitcast.28, f32[16,256]{1,0:T(8,128)} %bitcast.29, f32[16]{0:T(128)} %skip_ref.1, f32[1,1024]{1,0:T(1,128)} %bitcast.30, ...), custom_call_target="tpu_custom_call" | custom-call | flops 536870912 | bytes 4194304 | tf_op jit(solution)/shard_map/pallas_call | solution.py:765
  22.0 203.9 %shard_map.164 = bf16[64,4096]{1,0:T(8,128)(2,1)} custom-call(bf16[256,1024]{1,0:T(8,128)(2,1)} %shard_map.163.normed_ref, bf16[4,4,64,4096]{3,2,1,0:T(8,128)(2,1)} %bitcast.31, bf16[64,4096]{1,0:T(8,128)(2,1)} %bitcast.35, bf16[8,4096]{1,0:T(8,128)(2,1)} %bitcast.36, s32[2,64]{1,0:T(2,128)} %bitcast.37, s32[2,64]{1,0:T(2,128)} %bitcast.38, ...), custom_call_target="tpu_custom_call" | custom-call | flops 25769803776 | bytes 25165824 | tf_op jit(solution)/shard_map/pallas_call | solution.py:546
  225.9 1.9 copy.19

commit v5 on v4

--- a/solution.py
+++ b/solution.py
@@ -20,13 +20,28 @@
 PIECE = GROUPS * BLOCK
 HALF = PIECE // 2
 PLANE = SIDE * SIDE * PIECE
+HEADS = 16
+SIZE = 64
+STATE = 128
+CTX = SIDE * SIDE
+LENGTH = 256
+INNER = HEADS * SIZE
+MESSAGE = SIZE + 16
+EARLY = 3
 SUMS = 10
 LAST = 7
 MESH = pl.DeviceIdType.MESH
 
 
 def layer_kernel(
-    normed_ref,
+    mixer_ref,
+    switch_ref,
+    write_ref,
+    read_ref,
+    decay_ref,
+    skip_ref,
+    gain_ref,
+    start_ref,
     mix_ref,
     residual_ref,
     router_ref,
@@ -37,6 +52,19 @@
     up_ref,
     down_ref,
     out_ref,
+    mixer,
+    switch,
+    write,
+    read,
+    decay,
+    start,
+    residual,
+    router,
+    inner,
+    states,
+    gathered_states,
+    entering,
+    entered,
     normed,
     mixed,
     terms,
@@ -67,7 +95,11 @@
     back_recv,
     load_sem,
     mix_sem,
-    normed_sem,
+    input_sem,
+    out_send,
+    out_recv,
+    in_send,
+    in_recv,
 ):
     f32, bf16 = jnp.float32, jnp.bfloat16
     here = lax.axis_index("ctx")
@@ -117,29 +149,149 @@
             mix_ref.at[:, :, :, columns_of(q)], mix_room(q), mix_sem.at[q]
         )
 
-    fetch = pltpu.make_async_copy(normed_ref, normed, normed_sem)
-    fetch.start()
+    inputs = {
+        name: pltpu.make_async_copy(src, dst, input_sem.at[i])
+        for i, (name, src, dst) in enumerate(
+            (
+                ("decay", decay_ref, decay),
+                ("mixer", mixer_ref, mixer),
+                ("write", write_ref, write),
+                ("read", read_ref, read),
+                ("start", start_ref.at[rows_of(here, SIZE), :], start),
+                ("switch", switch_ref, switch),
+                ("residual", residual_ref, residual),
+                ("router", router_ref, router),
+            )
+        )
+    }
+    for copy in inputs.values():
+        copy.start()
     loads = [
         pltpu.make_async_copy(src, dst, load_sem.at[i])
         for i, (src, dst) in enumerate(((gate_ref, w_gate), (up_ref, w_up), (down_ref, w_down)))
     ]
 
+    barrier = pltpu.get_barrier_semaphore()
+
+    def greet(k, _):
+        other = lax.rem(here + k, CTX)
+        pl.semaphore_signal(barrier, inc=1, device_id={"ctx": other}, device_id_type=MESH)
+        return 0
+
+    lax.fori_loop(1, CTX, greet, 0)
+    for o in range(1, EXPERTS):
+        pl.semaphore_signal(barrier, inc=1, device_id=partner(o)[1], device_id_type=MESH)
+
+
+    row_id = lax.broadcasted_iota(jnp.int32, (LENGTH, LENGTH), 0)
+    col_id = lax.broadcasted_iota(jnp.int32, (LENGTH, LENGTH), 1)
+    causal = row_id >= col_id
+    upper = jnp.where(row_id <= col_id, 1.0, 0.0).astype(f32)
+    inputs["decay"].wait()
+    levels = jnp.dot(
+        decay[...], upper, precision=lax.Precision.HIGHEST, preferred_element_type=f32
+    )
+    last = levels[:, LENGTH - 1 : LENGTH]
+    to_end = jnp.exp(levels - last).T
+    total_decay = jnp.exp(-last)
+    levels_t = levels.T
+    from_start = jnp.exp(-levels_t)
+    low = lax.broadcasted_iota(jnp.int32, (LENGTH, 2 * SIZE), 1) < SIZE
+    top = lax.broadcasted_iota(jnp.int32, (16, STATE), 0) < 8
+
+    def spread(columns, q):
+        return jnp.where(low, columns[:, 2 * q : 2 * q + 1], columns[:, 2 * q + 1 : 2 * q + 2])
+
+    inputs["mixer"].wait()
+    inputs["write"].wait()
+    for q in range(HEADS // 2):
+        lanes = pl.ds(q * 2 * SIZE, 2 * SIZE)
+        scaled = (spread(to_end, q) * mixer[:, lanes].astype(f32)).astype(bf16)
+        local = lax.dot_general(
+            scaled, write[...], (((0,), (0,)), ((), ())), preferred_element_type=f32
+        )
+        for i in range(2):
+            h = 2 * q + i
+            states[h, 0:SIZE] = local[i * SIZE : (i + 1) * SIZE].astype(bf16)
+            value = jnp.broadcast_to(total_decay[h : h + 1, :], (16, STATE))
+            coarse = value.astype(bf16)
+            rest = (value - coarse.astype(f32)).astype(bf16)
+            states[h, SIZE:MESSAGE] = jnp.where(top, coarse, rest)
+
+    pl.semaphore_wait(barrier, CTX - 1 + EXPERTS - 1)
+
+    def out_copy(k):
+        other = lax.rem(here + k, CTX)
+        return remote(
+            states.at[other],
+            gathered_states.at[here],
+            out_send.at[k],
+            out_recv.at[k],
+            {"ctx": other},
+        )
+
+    def in_copy(k):
+        other = lax.rem(here + k, CTX)
+        return remote(
+            entering.at[other], entered.at[here], in_send.at[k], in_recv.at[k], {"ctx": other}
+        )
+
+    def each(action):
+        def step(k, _):
+            action(k)
+            return 0
+
+        lax.fori_loop(1, CTX, step, 0)
+
+    each(lambda k: out_copy(k).start())
+    gathered_states[here] = states[here]
+
     def load_mix(q, _):
         mix_load(q).start()
         return 0
 
     lax.fori_loop(0, 2 * QUADS, load_mix, 0)
-
-    barrier = pltpu.get_barrier_semaphore()
-    for axis in ("x", "z"):
-        for step in (1, -1):
-            pl.semaphore_signal(
-                barrier, inc=1, device_id=neighbour(axis, step), device_id_type=MESH
-            )
-    for o in range(1, EXPERTS):
-        pl.semaphore_signal(barrier, inc=1, device_id=partner(o)[1], device_id_type=MESH)
-
-    row_id = lax.broadcasted_iota(jnp.int32, (EXPERTS * BLOCK, TOKENS), 0)
+    for load in loads:
+        load.start()
+
+
+    inputs["read"].wait()
+    meet = lax.dot_general(
+        read[...], write[...], (((1,), (1,)), ((), ())), preferred_element_type=f32
+    )
+
+    def within(q):
+        lanes = pl.ds(q * 2 * SIZE, 2 * SIZE)
+        pair = mixer[:, lanes]
+        heads = []
+        for i in range(2):
+            h = 2 * q + i
+            span = levels[h : h + 1, :] - levels_t[:, h : h + 1]
+            weight = jnp.exp(jnp.where(causal, span, -1e30)) * meet
+            heads.append(jnp.dot(weight.astype(bf16), pair, preferred_element_type=f32))
+        skip = jnp.where(low, skip_ref[2 * q], skip_ref[2 * q + 1])
+        inner[:, lanes] = jnp.where(low, heads[0], heads[1]) + skip * pair.astype(f32)
+
+    for q in range(EARLY):
+        within(q)
+
+
+    inputs["start"].wait()
+    each(lambda k: out_copy(k).wait_recv())
+    state = start[...]
+    for k in range(CTX):
+        entering[k] = state.astype(bf16)
+        if k < CTX - 1:
+            factor = gathered_states[k, SIZE:MESSAGE].astype(f32)
+            factor = factor[0:1, :] + factor[8:9, :]
+            state = factor * state + gathered_states[k, 0:SIZE].astype(f32)
+    each(lambda k: in_copy(k).start())
+    entered[here] = entering[here]
+
+    for q in range(EARLY, HEADS // 2):
+        within(q)
+
+    place_id = lax.broadcasted_iota(jnp.int32, (EXPERTS * BLOCK, TOKENS), 0)
     expert_ids, slot_ids, spill_ids = chosen_ref[...], slot_ref[...], spill_ref[...]
     target = jnp.where(
         slot_ids >= 0,
@@ -150,11 +302,37 @@
             -1,
         ),
     )
-    places = [row_id == target[i : i + 1, :] for i in range(2)]
+    places = [place_id == target[i : i + 1, :] for i in range(2)]
     placing[...] = (places[0].astype(f32) + places[1].astype(f32)).astype(bf16)
     logits[...] = jnp.zeros_like(logits)
-    fetch.wait()
-    pl.semaphore_wait(barrier, 4 + EXPERTS - 1)
+    acc[...] = jnp.zeros_like(acc)
+
+    inputs["switch"].wait()
+    each(lambda k: in_copy(k).wait_recv())
+    square = jnp.zeros((LENGTH, 1), f32)
+    for q in range(HEADS // 2):
+        lanes = pl.ds(q * 2 * SIZE, 2 * SIZE)
+        carried = lax.dot_general(
+            read[...],
+            entered[2 * q : 2 * q + 2].reshape(2 * SIZE, STATE),
+            (((1,), (1,)), ((), ())),
+            preferred_element_type=f32,
+        )
+        gate = switch[:, lanes].astype(f32)
+        gated = (inner[:, lanes] + carried * spread(from_start, q)) * (
+            gate / (1.0 + jnp.exp(-gate))
+        )
+        inner[:, lanes] = gated
+        square = square + jnp.sum(gated * gated, axis=1, keepdims=True)
+    scale = lax.rsqrt(square / INNER + 1e-05)
+    for q in range(HEADS // 2):
+        lanes = pl.ds(q * 2 * SIZE, 2 * SIZE)
+        normed[:, lanes] = (inner[:, lanes] * scale * gain_ref[:, lanes]).astype(bf16)
+
+    inputs["residual"].wait()
+    inputs["router"].wait()
+    each(lambda k: out_copy(k).wait_send())
+    each(lambda k: in_copy(k).wait_send())
 
     every = pl.ds(0, SIDE)
     halves = {1: pl.ds(0, SIDE // 2), -1: pl.ds(SIDE // 2, SIDE // 2)}
@@ -181,7 +359,7 @@
             mix_load(q).wait()
             term = jnp.dot(
                 normed[...],
-                mix_room(q)[...].reshape(normed.shape[1], WIDTH),
+                mix_room(q)[...].reshape(INNER, WIDTH),
                 preferred_element_type=f32,
             )
             mixed[lax.rem(c, 2), t] = term.astype(bf16).reshape(GROUPS, TOKENS, WIDTH)
@@ -209,7 +387,7 @@
             total = mixed[lax.rem(c, 2), t, my_exp].astype(f32)
             for i in range(1, GROUPS):
                 total = total + terms[q, i - 1].astype(f32)
-            value = (residual_ref[:, columns].astype(f32) + total).astype(bf16)
+            value = (residual[:, columns].astype(f32) + total).astype(bf16)
             hidden[:, columns] = value
             rows = jnp.dot(placing[...], value, preferred_element_type=f32).astype(bf16)
             leaving[lax.rem(c, 2), t] = rows.reshape(EXPERTS, BLOCK, WIDTH)
@@ -218,7 +396,7 @@
             k = 2 * (my_dp * QUADS + c) + t
             xg[k, my["z"], my["x"], rows_of(my_exp, BLOCK)] = leaving[lax.rem(c, 2), t, owner]
             logits[...] += lax.dot_general(
-                router_ref[:, columns],
+                router[:, columns],
                 value,
                 (((1,), (1,)), ((), ())),
                 preferred_element_type=f32,
@@ -502,7 +680,7 @@
         weights = jnp.zeros((EXPERTS * BLOCK, TOKENS), f32)
         for i in range(2):
             share = 1.0 / (1.0 + jnp.exp(picked[1 - i] - picked[i]))
-            weights = weights + jnp.where(row_id == target[i : i + 1, :], share, 0.0)
+            weights = weights + jnp.where(place_id == target[i : i + 1, :], share, 0.0)
         coarse = weights.astype(bf16)
         shares[0] = coarse
         shares[1] = (weights - coarse.astype(f32)).astype(bf16)
@@ -512,10 +690,6 @@
             pl.when(jnp.logical_and(tick >= lag, tick < count + lag))(
                 functools.partial(action, tick - lag)
             )
-
-    for load in loads:
-        load.start()
-    acc[...] = jnp.zeros_like(acc)
 
     @pl.loop(0, 1 + SUMS + PAIRS + LAST)
     def _(turn):
@@ -537,19 +711,36 @@
         )
 
 
-def layer(normed, mix_w, residual, router, chosen, slots, spills, gate_w, up_w, down_w):
-    units = gate_w.shape[1]
-    length, inner = normed.shape
+def layer(*args):
+    units = args[-1].shape[1]
     bf16, f32 = jnp.bfloat16, jnp.float32
     any_space = pl.BlockSpec(memory_space=pl.ANY)
     vmem = pl.BlockSpec(memory_space=pltpu.VMEM)
+    smem = pl.BlockSpec(memory_space=pltpu.SMEM)
     return pl.pallas_call(
         layer_kernel,
         out_shape=jax.ShapeDtypeStruct((TOKENS, D), bf16),
-        in_specs=[any_space] * 2 + [vmem] * 5 + [any_space] * 3,
+        in_specs=[any_space] * 5
+        + [smem, vmem]
+        + [any_space] * 4
+        + [vmem] * 3
+        + [any_space] * 3,
         out_specs=vmem,
         scratch_shapes=[
-            pltpu.VMEM((length, inner), bf16),
+            pltpu.VMEM((LENGTH, INNER), bf16),
+            pltpu.VMEM((LENGTH, INNER), bf16),
+            pltpu.VMEM((LENGTH, STATE), bf16),
+            pltpu.VMEM((LENGTH, STATE), bf16),
+            pltpu.VMEM((HEADS, LENGTH), f32),
+            pltpu.VMEM((SIZE, STATE), f32),
+            pltpu.VMEM((TOKENS, D), bf16),
+            pltpu.VMEM((EXPERTS, D), bf16),
+            pltpu.VMEM((LENGTH, INNER), f32),
+            pltpu.VMEM((CTX, MESSAGE, STATE), bf16),
+            pltpu.VMEM((CTX, MESSAGE, STATE), bf16),
+            pltpu.VMEM((CTX, SIZE, STATE), bf16),
+            pltpu.VMEM((CTX, SIZE, STATE), bf16),
+            pltpu.VMEM((LENGTH, INNER), bf16),
             pltpu.VMEM((2, 2, GROUPS, TOKENS, WIDTH), bf16),
             pltpu.VMEM((2 * QUADS, GROUPS - 1, TOKENS, WIDTH), bf16),
             pltpu.VMEM((TOKENS, D), bf16),
@@ -579,7 +770,11 @@
             pltpu.SemaphoreType.DMA((2 * QUADS,)),
             pltpu.SemaphoreType.DMA((3,)),
             pltpu.SemaphoreType.DMA((2 * QUADS,)),
-            pltpu.SemaphoreType.DMA,
+            pltpu.SemaphoreType.DMA((8,)),
+            pltpu.SemaphoreType.DMA((CTX,)),
+            pltpu.SemaphoreType.DMA((CTX,)),
+            pltpu.SemaphoreType.DMA((CTX,)),
+            pltpu.SemaphoreType.DMA((CTX,)),
         ],
         compiler_params=pltpu.CompilerParams(
             collective_id=0, has_side_effects=True, vmem_limit_bytes=62 << 20
@@ -587,211 +782,7 @@
         cost_estimate=pl.CostEstimate(
             flops=6 * 2048 * D * 512, bytes_accessed=24 << 20, transcendentals=1 << 20
         ),
-    )(normed, mix_w, residual, router, chosen, slots, spills, gate_w, up_w, down_w)
-
-
-HEADS = 16
-SIZE = 64
-STATE = 128
-CTX = SIDE * SIDE
-MESSAGE = SIZE + 16
-
-
-def scan_kernel(
-    mixer_ref,
-    gate_ref,
-    write_ref,
-    read_ref,
-    decay_ref,
-    skip_ref,
-    gain_ref,
-    start_ref,
-    out_ref,
-    leaving,
-    gathered,
-    entering,
-    returned,
-    start,
-    acc,
-    out_send,
-    out_recv,
-    back_send,
-    back_recv,
-    start_sem,
-):
-    here = lax.axis_index("ctx")
-    f32, bf16 = jnp.float32, jnp.bfloat16
-    length = mixer_ref.shape[0]
-    mine = pltpu.make_async_copy(
-        start_ref.at[pl.ds(pl.multiple_of(here * SIZE, SIZE), SIZE), :], start, start_sem
-    )
-    mine.start()
-
-    barrier = pltpu.get_barrier_semaphore()
-
-    def greet(k, _):
-        other = lax.rem(here + k, CTX)
-        pl.semaphore_signal(barrier, inc=1, device_id={"ctx": other}, device_id_type=MESH)
-        return 0
-
-    lax.fori_loop(1, CTX, greet, 0)
-
-    row_id = lax.broadcasted_iota(jnp.int32, (length, length), 0)
-    col_id = lax.broadcasted_iota(jnp.int32, (length, length), 1)
-    causal = row_id >= col_id
-    upper = jnp.where(row_id <= col_id, 1.0, 0.0).astype(f32)
-    levels = jnp.dot(
-        decay_ref[...], upper, precision=lax.Precision.HIGHEST, preferred_element_type=f32
-    )
-    last = levels[:, length - 1 : length]
-    to_end = jnp.exp(levels - last).T
-    total = jnp.exp(-last)
-    levels_t = levels.T
-    from_start = jnp.exp(-levels_t)
-    low = lax.broadcasted_iota(jnp.int32, (length, 2 * SIZE), 1) < SIZE
-    top = lax.broadcasted_iota(jnp.int32, (16, STATE), 0) < 8
-
-    def spread(columns, q):
-        return jnp.where(low, columns[:, 2 * q : 2 * q + 1], columns[:, 2 * q + 1 : 2 * q + 2])
-
-    for q in range(HEADS // 2):
-        lanes = pl.ds(q * 2 * SIZE, 2 * SIZE)
-        scaled = (spread(to_end, q) * mixer_ref[:, lanes].astype(f32)).astype(bf16)
-        local = lax.dot_general(
-            scaled, write_ref[...], (((0,), (0,)), ((), ())), preferred_element_type=f32
-        )
-        for i in range(2):
-            h = 2 * q + i
-            leaving[h, 0:SIZE] = local[i * SIZE : (i + 1) * SIZE].astype(bf16)
-            value = jnp.broadcast_to(total[h : h + 1, :], (16, STATE))
-            coarse = value.astype(bf16)
-            rest = (value - coarse.astype(f32)).astype(bf16)
-            leaving[h, SIZE:MESSAGE] = jnp.where(top, coarse, rest)
-
-    pl.semaphore_wait(barrier, CTX - 1)
-
-    def out_copy(k):
-        other = lax.rem(here + k, CTX)
-        return pltpu.make_async_remote_copy(
-            src_ref=leaving.at[other],
-            dst_ref=gathered.at[here],
-            send_sem=out_send.at[k],
-            recv_sem=out_recv.at[k],
-            device_id={"ctx": other},
-            device_id_type=MESH,
-        )
-
-    def back_copy(k):
-        other = lax.rem(here + k, CTX)
-        return pltpu.make_async_remote_copy(
-            src_ref=entering.at[other],
-            dst_ref=returned.at[here],
-            send_sem=back_send.at[k],
-            recv_sem=back_recv.at[k],
-            device_id={"ctx": other},
-            device_id_type=MESH,
-        )
-
-    def each(action):
-        def step(k, _):
-            action(k)
-            return 0
-
-        lax.fori_loop(1, CTX, step, 0)
-
-    each(lambda k: out_copy(k).start())
-    gathered[here] = leaving[here]
-
-    meet = lax.dot_general(
-        read_ref[...], write_ref[...], (((1,), (1,)), ((), ())), preferred_element_type=f32
-    )
-
-    def within(q):
-        lanes = pl.ds(q * 2 * SIZE, 2 * SIZE)
-        pair = mixer_ref[:, lanes]
-        halves = []
-        for i in range(2):
-            h = 2 * q + i
-            span = levels[h : h + 1, :] - levels_t[:, h : h + 1]
-            weight = jnp.exp(jnp.where(causal, span, -1e30)) * meet
-            halves.append(jnp.dot(weight.astype(bf16), pair, preferred_element_type=f32))
-        skip = jnp.where(low, skip_ref[2 * q], skip_ref[2 * q + 1])
-        acc[:, lanes] = jnp.where(low, halves[0], halves[1]) + skip * pair.astype(f32)
-
-    EARLY = 3
-    for q in range(EARLY):
-        within(q)
-
-    mine.wait()
-    each(lambda k: out_copy(k).wait_recv())
-    state = start[...]
-    for k in range(CTX):
-        entering[k] = state.astype(bf16)
-        if k < CTX - 1:
-            factor = gathered[k, SIZE:MESSAGE].astype(f32)
-            factor = factor[0:1, :] + factor[8:9, :]
-            state = factor * state + gathered[k, 0:SIZE].astype(f32)
-    each(lambda k: back_copy(k).start())
-    returned[here] = entering[here]
-
-    for q in range(EARLY, HEADS // 2):
-        within(q)
-
-    each(lambda k: back_copy(k).wait_recv())
-    square = jnp.zeros((length, 1), f32)
-    for q in range(HEADS // 2):
-        lanes = pl.ds(q * 2 * SIZE, 2 * SIZE)
-        entered = returned[2 * q : 2 * q + 2].reshape(2 * SIZE, STATE)
-        carried = lax.dot_general(
-            read_ref[...], entered, (((1,), (1,)), ((), ())), preferred_element_type=f32
-        )
-        gate = gate_ref[:, lanes].astype(f32)
-        gated = (acc[:, lanes] + carried * spread(from_start, q)) * (gate / (1.0 + jnp.exp(-gate)))
-        acc[:, lanes] = gated
-        square = square + jnp.sum(gated * gated, axis=1, keepdims=True)
-    scale = lax.rsqrt(square / (HEADS * SIZE) + 1e-05)
-    for q in range(HEADS // 2):
-        lanes = pl.ds(q * 2 * SIZE, 2 * SIZE)
-        out_ref[:, lanes] = (acc[:, lanes] * scale * gain_ref[:, lanes]).astype(bf16)
-
-    each(lambda k: out_copy(k).wait_send())
-    each(lambda k: back_copy(k).wait_send())
-
-
-def scan(mixer, gate, write, read, decay, skip, gain, start_state):
-    length, inner = mixer.shape
-    f32, bf16 = jnp.float32, jnp.bfloat16
-    vmem = pl.BlockSpec(memory_space=pltpu.VMEM)
-    return pl.pallas_call(
-        scan_kernel,
-        out_shape=jax.ShapeDtypeStruct((length, inner), bf16),
-        in_specs=[vmem] * 5
-        + [
-            pl.BlockSpec(memory_space=pltpu.SMEM),
-            vmem,
-            pl.BlockSpec(memory_space=pl.ANY),
-        ],
-        out_specs=vmem,
-        scratch_shapes=[
-            pltpu.VMEM((CTX, MESSAGE, STATE), bf16),
-            pltpu.VMEM((CTX, MESSAGE, STATE), bf16),
-            pltpu.VMEM((CTX, SIZE, STATE), bf16),
-            pltpu.VMEM((CTX, SIZE, STATE), bf16),
-            pltpu.VMEM((SIZE, STATE), f32),
-            pltpu.VMEM((length, inner), f32),
-            pltpu.SemaphoreType.DMA((CTX,)),
-            pltpu.SemaphoreType.DMA((CTX,)),
-            pltpu.SemaphoreType.DMA((CTX,)),
-            pltpu.SemaphoreType.DMA((CTX,)),
-            pltpu.SemaphoreType.DMA,
-        ],
-        compiler_params=pltpu.CompilerParams(
-            collective_id=1, has_side_effects=True, vmem_limit_bytes=60 << 20
-        ),
-        cost_estimate=pl.CostEstimate(
-            flops=1 << 29, bytes_accessed=4 << 20, transcendentals=1 << 20
-        ),
-    )(mixer, gate, write, read, decay, skip, gain, start_state)
+    )(*args)
 
 
 def shards(
@@ -813,7 +804,7 @@
     up_weight,
     down_weight,
 ):
-    normed = scan(
+    return layer(
         mixer_in[0],
         gate_in[0],
         state_write[0, :, 0],
@@ -822,9 +813,6 @@
         skip_gain,
         norm_gain[None],
         start_state[0].reshape(HEADS * SIZE, STATE),
-    )
-    return layer(
-        normed,
         out_weight.reshape(SIDE, SIDE, PIECE, D),
         residual[0],
         router_weight.T,

time: 228 us -> 223 us (0.978)
  Pallas kernels: 226 us -> 221 us
    pallas_call x1 -> x0, Pallas kernels: 22 us -> none  [scan(): pl.pallas_call(scan_kernel, out_shape=jax.ShapeDtypeStruct((length, inner...]
    pallas_call x1, Pallas kernels: 204 us -> 221 us  [layer(): pl.pallas_call(layer_kernel, out_shape=jax.ShapeDtypeStruct((TOKENS, D),...]
where the time goes in v5:
time: 223 us
  Pallas kernels  221 us (99%)
    pallas_call x1, Pallas kernels, layer(): pl.pallas_call(layer_kernel, out_shape=jax.ShapeDtypeStruct((TOKENS, D),...  221 us

profile of v5, /device:TPU:1, one launch (start us, length us, event | category | flops | bytes accessed | tf_op | source)
XLA Modules:
  0.0 222.8 jit_solution(7932774574700244325)
XLA Ops:
  0.0 221.0 %shard_map.163 = bf16[64,4096]{1,0:T(8,128)(2,1)} custom-call(bf16[256,1024]{1,0:T(8,128)(2,1)} %bitcast.28, bf16[256,1024]{1,0:T(8,128)(2,1)} %bitcast.29, bf16[256,128]{1,0:T(8,128)(2,1)} %bitcast.32, bf16[256,128]{1,0:T(8,128)(2,1)} %bitcast.33, f32[16,256]{1,0:T(8,128)} %bitcast.35, f32[16]{0:T(128)} %skip_ref.1, f32[1,1024]{1,0:T(1,128)} %bitcast.36, ...), custom_call_target="tpu_custom_call" | custom-call | flops 25769803776 | bytes 25165824 | tf_op jit(solution)/shard_map/pallas_call | solution.py:720
  221.0 1.9 copy.19

commit v6 on v5

--- a/solution.py
+++ b/solution.py
@@ -28,6 +28,8 @@
 INNER = HEADS * SIZE
 MESSAGE = SIZE + 16
 EARLY = 3
+APART = QUADS - 1
+ROUNDS = 2 * APART + 1
 SUMS = 10
 LAST = 7
 MESH = pl.DeviceIdType.MESH
@@ -60,14 +62,19 @@
     start,
     residual,
     router,
+    chosen,
+    slots,
+    spills,
+    skips,
+    gains,
+    out,
     inner,
     states,
     gathered_states,
     entering,
     entered,
     normed,
-    mixed,
-    terms,
+    pool,
     hidden,
     placing,
     shares,
@@ -83,6 +90,8 @@
     w_down,
     part,
     line,
+    apart,
+    weights,
     ag_send,
     ag_recv,
     rs_send,
@@ -93,9 +102,15 @@
     row_recv,
     back_send,
     back_recv,
+    apart_send,
+    apart_recv,
+    weight_send,
+    weight_recv,
+    ready,
     load_sem,
     mix_sem,
     input_sem,
+    done_sem,
     out_send,
     out_recv,
     in_send,
@@ -148,6 +163,17 @@
         return pltpu.make_async_copy(
             mix_ref.at[:, :, :, columns_of(q)], mix_room(q), mix_sem.at[q]
         )
+
+    barrier = pltpu.get_barrier_semaphore()
+
+    def greet(k, _):
+        other = lax.rem(here + k, CTX)
+        pl.semaphore_signal(barrier, inc=1, device_id={"ctx": other}, device_id_type=MESH)
+        return 0
+
+    lax.fori_loop(1, CTX, greet, 0)
+    for o in range(1, EXPERTS):
+        pl.semaphore_signal(barrier, inc=1, device_id=partner(o)[1], device_id_type=MESH)
 
     inputs = {
         name: pltpu.make_async_copy(src, dst, input_sem.at[i])
@@ -161,6 +187,11 @@
                 ("switch", switch_ref, switch),
                 ("residual", residual_ref, residual),
                 ("router", router_ref, router),
+                ("skip", skip_ref, skips),
+                ("gain", gain_ref, gains),
+                ("chosen", chosen_ref, chosen),
+                ("slots", slot_ref, slots),
+                ("spills", spill_ref, spills),
             )
         )
     }
@@ -170,17 +201,6 @@
         pltpu.make_async_copy(src, dst, load_sem.at[i])
         for i, (src, dst) in enumerate(((gate_ref, w_gate), (up_ref, w_up), (down_ref, w_down)))
     ]
-
-    barrier = pltpu.get_barrier_semaphore()
-
-    def greet(k, _):
-        other = lax.rem(here + k, CTX)
-        pl.semaphore_signal(barrier, inc=1, device_id={"ctx": other}, device_id_type=MESH)
-        return 0
-
-    lax.fori_loop(1, CTX, greet, 0)
-    for o in range(1, EXPERTS):
-        pl.semaphore_signal(barrier, inc=1, device_id=partner(o)[1], device_id_type=MESH)
 
 
     row_id = lax.broadcasted_iota(jnp.int32, (LENGTH, LENGTH), 0)
@@ -256,6 +276,7 @@
 
 
     inputs["read"].wait()
+    inputs["skip"].wait()
     meet = lax.dot_general(
         read[...], write[...], (((1,), (1,)), ((), ())), preferred_element_type=f32
     )
@@ -269,7 +290,7 @@
             span = levels[h : h + 1, :] - levels_t[:, h : h + 1]
             weight = jnp.exp(jnp.where(causal, span, -1e30)) * meet
             heads.append(jnp.dot(weight.astype(bf16), pair, preferred_element_type=f32))
-        skip = jnp.where(low, skip_ref[2 * q], skip_ref[2 * q + 1])
+        skip = spread(skips[...], q)
         inner[:, lanes] = jnp.where(low, heads[0], heads[1]) + skip * pair.astype(f32)
 
     for q in range(EARLY):
@@ -291,8 +312,11 @@
     for q in range(EARLY, HEADS // 2):
         within(q)
 
+    for name in ("chosen", "slots", "spills", "gain"):
+        inputs[name].wait()
+
     place_id = lax.broadcasted_iota(jnp.int32, (EXPERTS * BLOCK, TOKENS), 0)
-    expert_ids, slot_ids, spill_ids = chosen_ref[...], slot_ref[...], spill_ref[...]
+    expert_ids, slot_ids, spill_ids = chosen[...], slots[...], spills[...]
     target = jnp.where(
         slot_ids >= 0,
         expert_ids * BLOCK + slot_ids,
@@ -327,7 +351,7 @@
     scale = lax.rsqrt(square / INNER + 1e-05)
     for q in range(HEADS // 2):
         lanes = pl.ds(q * 2 * SIZE, 2 * SIZE)
-        normed[:, lanes] = (inner[:, lanes] * scale * gain_ref[:, lanes]).astype(bf16)
+        normed[:, lanes] = (inner[:, lanes] * scale * gains[:, lanes]).astype(bf16)
 
     inputs["residual"].wait()
     inputs["router"].wait()
@@ -342,12 +366,19 @@
     both = [(t, d) for t in range(2) for d in (1, -1)]
 
 
+    def mixed(c, t):
+        return pool.at[lax.rem(c, 2) * 2 + t]
+
+    def term(q, i):
+        b = q * (GROUPS - 1) + i - 1
+        return pool.at[4 + lax.div(b, GROUPS), lax.rem(b, GROUPS)]
+
     def term_copy(c, t, i):
         other = lax.rem(my_exp + i, GROUPS)
         q = 2 * c + t
         return remote(
-            mixed.at[lax.rem(c, 2), t, other],
-            terms.at[q, i - 1],
+            mixed(c, t).at[other],
+            term(q, i),
             mix_send.at[q, i - 1],
             mix_recv.at[q, i - 1],
             {"exp": other},
@@ -357,12 +388,12 @@
         for t in range(2):
             q = 2 * c + t
             mix_load(q).wait()
-            term = jnp.dot(
+            value = jnp.dot(
                 normed[...],
                 mix_room(q)[...].reshape(INNER, WIDTH),
                 preferred_element_type=f32,
             )
-            mixed[lax.rem(c, 2), t] = term.astype(bf16).reshape(GROUPS, TOKENS, WIDTH)
+            mixed(c, t)[...] = value.astype(bf16).reshape(GROUPS, TOKENS, WIDTH)
             for i in range(1, GROUPS):
                 term_copy(c, t, i).start()
 
@@ -384,9 +415,9 @@
             columns = columns_of(q)
             for i in range(1, GROUPS):
                 term_copy(c, t, i).wait_recv()
-            total = mixed[lax.rem(c, 2), t, my_exp].astype(f32)
+            total = mixed(c, t)[my_exp].astype(f32)
             for i in range(1, GROUPS):
-                total = total + terms[q, i - 1].astype(f32)
+                total = total + term(q, i)[...].astype(f32)
             value = (residual[:, columns].astype(f32) + total).astype(bf16)
             hidden[:, columns] = value
             rows = jnp.dot(placing[...], value, preferred_element_type=f32).astype(bf16)
@@ -494,6 +525,11 @@
                     )
                 acc[n, rows, :] = total
 
+        @pl.when(j == QUADS - 1)
+        def _():
+            for o in range(1, EXPERTS):
+                pl.semaphore_signal(ready, inc=1, device_id=partner(o)[1], device_id_type=MESH)
+
         @pl.when(c == QUADS - 1)
         def _():
             @pl.loop(0, 8)
@@ -503,10 +539,14 @@
                 act[rows, :] = (gate / (1.0 + jnp.exp(-gate)) * acc[1, rows, :]).astype(bf16)
 
 
+    def room_of(j, t):
+        pair = j + lax.div(j, APART) - lax.div(j, 2 * APART)
+        return xg.at[2 * pair + t]
+
     def rs_copy(j, t, step, d):
         near, far = axes[t]
         p = part.at[lax.rem(j, 4), t]
-        room = xg.at[2 * j + t]
+        room = room_of(j, t)
         if step == 0:
             src = along(far, p, around(far, 2), halves[d])
             dst, to = room.at[0, halves[d]], far
@@ -535,24 +575,118 @@
             for t, d in both:
                 rs_copy(j, t, step, d).wait_send()
 
-    def sum_start(j):
-        h = lax.div(j, QUADS)
-        c = lax.rem(j, QUADS)
+    def down(h, b, q):
+        rows = rows_of(h * 2 + b, PLANE // 2)
+        value = lax.dot_general(
+            act[rows, :],
+            w_down[columns_of(q), :],
+            (((1,), (1,)), ((), ())),
+            preferred_element_type=f32,
+        )
+        return value.astype(bf16)
+
+    def by_rows(j):
+        h = lax.div(j, APART)
+        c = lax.rem(j, APART)
 
         @pl.loop(0, 2)
         def _(b):
-            rows = rows_of(h * 2 + b, PLANE // 2)
             for t in range(2):
-                term = lax.dot_general(
-                    act[rows, :],
-                    w_down[columns_of(2 * c + t), :],
-                    (((1,), (1,)), ((), ())),
-                    preferred_element_type=f32,
-                )
-                part[lax.rem(j, 4), t, pl.ds(b * 2, 2)] = term.astype(bf16).reshape(
+                part[lax.rem(j, 4), t, pl.ds(b * 2, 2)] = down(h, b, 2 * c + t).reshape(
                     2, SIDE, PIECE, WIDTH
                 )
 
+
+    def apart_room(t, e):
+        if t == 0:
+            return xg.at[2 * APART + lax.div(e, SIDE), lax.rem(e, SIDE)]
+        return pool.at[e]
+
+    def apart_copy(h, t, o):
+        other = lax.rem(my_exp + o, GROUPS)
+        return remote(
+            apart.at[t, other],
+            apart_room(t, owner),
+            apart_send.at[h, t],
+            apart_recv.at[t],
+            {"exp": other, "dp": h},
+        )
+
+    def apart_sent(h):
+        for t in range(2):
+
+            def sent(count):
+                ref = pool.at[pl.ds(0, count)]
+                remote(
+                    ref, ref, apart_send.at[h, t], apart_recv.at[0], partner(1)[1]
+                ).wait_send()
+
+            pl.when(my_dp == h)(functools.partial(sent, GROUPS - 1))
+            pl.when(my_dp != h)(functools.partial(sent, GROUPS))
+
+    def apart_start(h):
+        if h == 0:
+            pl.semaphore_wait(ready, EXPERTS - 1)
+        else:
+            apart_sent(0)
+        for t in range(2):
+
+            @pl.loop(0, 2)
+            def _(b):
+                value = down(h, b, 2 * APART + t)
+                for i in range(2):
+                    for x in range(SIDE):
+                        for y in range(GROUPS):
+                            low_row = (i * SIDE + x) * PIECE + y * BLOCK
+                            apart[t, y, 2 * b + i, x * BLOCK : (x + 1) * BLOCK] = value[
+                                low_row : low_row + BLOCK
+                            ]
+
+            for o in range(1, GROUPS):
+                apart_copy(h, t, o).start()
+
+            @pl.when(my_dp == h)
+            def _():
+                apart_room(t, owner)[...] = apart[t, my_exp]
+
+            @pl.when(my_dp != h)
+            def _():
+                apart_copy(h, t, 0).start()
+
+    def weight_copy(k):
+        other = lax.rem(here + k, CTX)
+        return remote(
+            weights.at[here],
+            weights.at[here],
+            weight_send.at[k],
+            weight_recv.at[k],
+            {"ctx": other},
+        )
+
+    def by_tokens(j):
+        each(lambda k: weight_copy(k).wait_recv())
+        for t in range(2):
+            ref = pool.at[pl.ds(0, EXPERTS - 1)]
+            remote(ref, ref, apart_send.at[0, 0], apart_recv.at[t], partner(1)[1]).wait_recv()
+
+            @pl.loop(0, SIDE)
+            def _(z):
+                for x in range(SIDE):
+                    rows = jnp.concatenate(
+                        [
+                            apart_room(t, e)[z, x * BLOCK : (x + 1) * BLOCK]
+                            for e in range(EXPERTS)
+                        ],
+                        axis=0,
+                    )
+                    value = jnp.dot(
+                        weights[z * SIDE + x], rows, preferred_element_type=f32
+                    )
+                    part[lax.rem(j, 4), t, z, x] = value.astype(bf16)
+
+    def sum_start(j):
+        pl.when(j < 2 * APART)(functools.partial(by_rows, j))
+        pl.when(j == 2 * APART)(functools.partial(by_tokens, j))
         for t in range(2):
             rs_start(j, 0, t)
 
@@ -570,7 +704,7 @@
                     at = (place, base + i) if far == "z" else (base + i, place)
                     part[s, t, at[0], at[1]] = (
                         part[s, t, at[0], at[1]].astype(f32)
-                        + xg[2 * j + t, 0, base + i].astype(f32)
+                        + room_of(j, t)[0, base + i].astype(f32)
                     ).astype(bf16)
 
             rs_start(j, 1, t)
@@ -586,8 +720,8 @@
                 at = (my[far], i) if far == "z" else (i, my[far])
                 line[s, t, i] = (
                     part[s, t, at[0], at[1]].astype(f32)
-                    + xg[2 * j + t, 1, i].astype(f32)
-                    + xg[2 * j + t, 2, i].astype(f32)
+                    + room_of(j, t)[1, i].astype(f32)
+                    + room_of(j, t)[2, i].astype(f32)
                 ).astype(bf16)
 
             rs_start(j, 2, t)
@@ -601,51 +735,65 @@
                 at = around(axes[t][0], d)
                 line[s, t, at, half_rows[d]] = (
                     line[s, t, at, half_rows[d]].astype(f32)
-                    + xg[2 * j + t, 3, 0, half_rows[d]].astype(f32)
+                    + room_of(j, t)[3, 0, half_rows[d]].astype(f32)
                 ).astype(bf16)
             rs_start(j, 3, t)
 
 
     def back_copy(j, t, o):
         other = lax.rem(my_exp + o, GROUPS)
-        k = 2 * lax.rem(j, QUADS) + t
+        k = 2 * lax.rem(j, APART) + t
         return remote(
             sums.at[lax.rem(j, 2), t, other],
             returned.at[k, rows_of(owner, BLOCK)],
             back_send.at[2 * j + t],
             back_recv.at[k],
-            {"exp": other, "dp": lax.div(j, QUADS)},
+            {"exp": other, "dp": lax.div(j, APART)},
         )
 
     def sum_last(j):
-        mine = my_dp == lax.div(j, QUADS)
+        mine = my_dp == lax.div(j, APART)
         for t in range(2):
             rs_arrive(j, 3, t)
             total = (
                 line[lax.rem(j, 4), t, my[axes[t][0]]].astype(f32)
-                + xg[2 * j + t, 3, 1].astype(f32)
-                + xg[2 * j + t, 3, 2].astype(f32)
+                + room_of(j, t)[3, 1].astype(f32)
+                + room_of(j, t)[3, 2].astype(f32)
             )
-            s = lax.rem(j, 2)
-            sums[s, t] = total.astype(bf16).reshape(GROUPS, BLOCK, WIDTH)
-            for o in range(1, GROUPS):
-                back_copy(j, t, o).start()
-
-            @pl.when(mine)
+
+            @pl.when(j == 2 * APART)
             def _():
-                k = 2 * lax.rem(j, QUADS) + t
-                returned[k, rows_of(owner, BLOCK)] = sums[s, t, my_exp]
-
-            @pl.when(jnp.logical_not(mine))
+                q = 2 * APART + t
+                columns = columns_of(q)
+                out[:, columns] = (hidden[:, columns].astype(f32) + total).astype(bf16)
+                out_store(q).start()
+
+            @pl.when(j < 2 * APART)
             def _():
-                back_copy(j, t, 0).start()
+                s = lax.rem(j, 2)
+                sums[s, t] = total.astype(bf16).reshape(GROUPS, BLOCK, WIDTH)
+                for o in range(1, GROUPS):
+                    back_copy(j, t, o).start()
+
+                @pl.when(mine)
+                def _():
+                    k = 2 * lax.rem(j, APART) + t
+                    returned[k, rows_of(owner, BLOCK)] = sums[s, t, my_exp]
+
+                @pl.when(jnp.logical_not(mine))
+                def _():
+                    back_copy(j, t, 0).start()
 
         rs_sent(j, (2, 3))
 
+    def out_store(q):
+        columns = columns_of(q)
+        return pltpu.make_async_copy(out.at[:, columns], out_ref.at[:, columns], done_sem.at[q])
+
     def sum_back(j):
-        mine = my_dp == lax.div(j, QUADS)
-        for t in range(2):
-            q = 2 * lax.rem(j, QUADS) + t
+        mine = my_dp == lax.div(j, APART)
+        for t in range(2):
+            q = 2 * lax.rem(j, APART) + t
 
             def sent(count):
                 ref = sums.at[lax.rem(j, 2), t, pl.ds(0, count)]
@@ -666,24 +814,27 @@
                         (((0,), (0,)), ((), ())),
                         preferred_element_type=f32,
                     )
-                out_ref[:, columns] = total.astype(bf16)
+                out[:, columns] = total.astype(bf16)
+                out_store(q).start()
                 sent(GROUPS - 1)
 
             pl.when(jnp.logical_not(mine))(functools.partial(sent, GROUPS))
 
     def weigh():
         match = [
-            lax.broadcasted_iota(jnp.int32, (EXPERTS, TOKENS), 0) == chosen_ref[i : i + 1, :]
+            lax.broadcasted_iota(jnp.int32, (EXPERTS, TOKENS), 0) == chosen[i : i + 1, :]
             for i in range(2)
         ]
         picked = [jnp.sum(jnp.where(m, logits[...], 0.0), axis=0, keepdims=True) for m in match]
-        weights = jnp.zeros((EXPERTS * BLOCK, TOKENS), f32)
+        weight = jnp.zeros((EXPERTS * BLOCK, TOKENS), f32)
         for i in range(2):
             share = 1.0 / (1.0 + jnp.exp(picked[1 - i] - picked[i]))
-            weights = weights + jnp.where(place_id == target[i : i + 1, :], share, 0.0)
-        coarse = weights.astype(bf16)
+            weight = weight + jnp.where(place_id == target[i : i + 1, :], share, 0.0)
+        coarse = weight.astype(bf16)
         shares[0] = coarse
-        shares[1] = (weights - coarse.astype(f32)).astype(bf16)
+        shares[1] = (weight - coarse.astype(f32)).astype(bf16)
+        weights[here] = weight.T.astype(bf16)
+        each(lambda k: weight_copy(k).start())
 
     def stages(tick, count, steps):
         for lag, action in steps:
@@ -691,7 +842,7 @@
                 functools.partial(action, tick - lag)
             )
 
-    @pl.loop(0, 1 + SUMS + PAIRS + LAST)
+    @pl.loop(0, 1 + SUMS + ROUNDS + LAST)
     def _(turn):
         tick = turn - 1
         own = tick - my_dp * QUADS
@@ -700,32 +851,30 @@
             PAIRS,
             ((5, gather_last), (4, gather_third), (3, gather_second), (2, gather_first)),
         )
-        stages(tick - SUMS, PAIRS, ((4, sum_second), (2, sum_first)))
+        stages(tick - SUMS, ROUNDS, ((4, sum_second), (2, sum_first)))
         stages(own, QUADS, ((3, rows_sent), (1, tokens), (-1, mix)))
         stages(tick, PAIRS, ((6, gathered),))
         pl.when(tick == SUMS)(weigh)
-        stages(
-            tick - SUMS,
-            PAIRS,
-            ((0, sum_start), (5, sum_third), (6, sum_last), (7, sum_back)),
-        )
+        stages(tick - SUMS, ROUNDS, ((0, sum_start), (5, sum_third), (6, sum_last)))
+        stages(tick - SUMS, 2 * APART, ((7, sum_back),))
+        for h in range(2):
+            pl.when(tick == SUMS + APART * h)(functools.partial(apart_start, h))
+
+    apart_sent(1)
+    each(lambda k: weight_copy(k).wait_send())
+    for q in range(2 * QUADS):
+        out_store(q).wait()
 
 
 def layer(*args):
     units = args[-1].shape[1]
     bf16, f32 = jnp.bfloat16, jnp.float32
     any_space = pl.BlockSpec(memory_space=pl.ANY)
-    vmem = pl.BlockSpec(memory_space=pltpu.VMEM)
-    smem = pl.BlockSpec(memory_space=pltpu.SMEM)
     return pl.pallas_call(
         layer_kernel,
         out_shape=jax.ShapeDtypeStruct((TOKENS, D), bf16),
-        in_specs=[any_space] * 5
-        + [smem, vmem]
-        + [any_space] * 4
-        + [vmem] * 3
-        + [any_space] * 3,
-        out_specs=vmem,
+        in_specs=[any_space] * len(args),
+        out_specs=any_space,
         scratch_shapes=[
             pltpu.VMEM((LENGTH, INNER), bf16),
             pltpu.VMEM((LENGTH, INNER), bf16),
@@ -735,21 +884,26 @@
             pltpu.VMEM((SIZE, STATE), f32),
             pltpu.VMEM((TOKENS, D), bf16),
             pltpu.VMEM((EXPERTS, D), bf16),
+            pltpu.VMEM((2, TOKENS), jnp.int32),
+            pltpu.VMEM((2, TOKENS), jnp.int32),
+            pltpu.VMEM((2, TOKENS), jnp.int32),
+            pltpu.VMEM((1, HEADS), f32),
+            pltpu.VMEM((1, INNER), f32),
+            pltpu.VMEM((TOKENS, D), bf16),
             pltpu.VMEM((LENGTH, INNER), f32),
             pltpu.VMEM((CTX, MESSAGE, STATE), bf16),
             pltpu.VMEM((CTX, MESSAGE, STATE), bf16),
             pltpu.VMEM((CTX, SIZE, STATE), bf16),
             pltpu.VMEM((CTX, SIZE, STATE), bf16),
             pltpu.VMEM((LENGTH, INNER), bf16),
-            pltpu.VMEM((2, 2, GROUPS, TOKENS, WIDTH), bf16),
-            pltpu.VMEM((2 * QUADS, GROUPS - 1, TOKENS, WIDTH), bf16),
+            pltpu.VMEM((4 + 2 * QUADS * (GROUPS - 1) // GROUPS, GROUPS, TOKENS, WIDTH), bf16),
             pltpu.VMEM((TOKENS, D), bf16),
             pltpu.VMEM((EXPERTS * BLOCK, TOKENS), bf16),
             pltpu.VMEM((2, EXPERTS * BLOCK, TOKENS), bf16),
             pltpu.VMEM((EXPERTS, TOKENS), f32),
             pltpu.VMEM((2, 2, EXPERTS, BLOCK, WIDTH), bf16),
             pltpu.VMEM((2, 2, GROUPS, BLOCK, WIDTH), bf16),
-            pltpu.VMEM((2 * QUADS, EXPERTS * BLOCK, WIDTH), bf16),
+            pltpu.VMEM((2 * APART, EXPERTS * BLOCK, WIDTH), bf16),
             pltpu.VMEM((2 * PAIRS, SIDE, SIDE, PIECE, WIDTH), bf16),
             pltpu.VMEM((2, 2 * PLANE, units), f32),
             pltpu.VMEM((2 * PLANE, units), bf16),
@@ -758,6 +912,8 @@
             pltpu.VMEM((D, units), bf16),
             pltpu.VMEM((4, 2, SIDE, SIDE, PIECE, WIDTH), bf16),
             pltpu.VMEM((4, 2, SIDE, PIECE, WIDTH), bf16),
+            pltpu.VMEM((2, GROUPS, SIDE, PIECE, WIDTH), bf16),
+            pltpu.VMEM((CTX, TOKENS, EXPERTS * BLOCK), bf16),
             pltpu.SemaphoreType.DMA((PAIRS, 2, 8)),
             pltpu.SemaphoreType.DMA((PAIRS, 2, 8)),
             pltpu.SemaphoreType.DMA((PAIRS, 2, 8)),
@@ -768,16 +924,22 @@
             pltpu.SemaphoreType.DMA((2 * PAIRS,)),
             pltpu.SemaphoreType.DMA((2 * PAIRS,)),
             pltpu.SemaphoreType.DMA((2 * QUADS,)),
+            pltpu.SemaphoreType.DMA((2, 2)),
+            pltpu.SemaphoreType.DMA((2,)),
+            pltpu.SemaphoreType.DMA((CTX,)),
+            pltpu.SemaphoreType.DMA((CTX,)),
+            pltpu.SemaphoreType.REGULAR,
             pltpu.SemaphoreType.DMA((3,)),
             pltpu.SemaphoreType.DMA((2 * QUADS,)),
-            pltpu.SemaphoreType.DMA((8,)),
+            pltpu.SemaphoreType.DMA((13,)),
+            pltpu.SemaphoreType.DMA((2 * QUADS,)),
             pltpu.SemaphoreType.DMA((CTX,)),
             pltpu.SemaphoreType.DMA((CTX,)),
             pltpu.SemaphoreType.DMA((CTX,)),
             pltpu.SemaphoreType.DMA((CTX,)),
         ],
         compiler_params=pltpu.CompilerParams(
-            collective_id=0, has_side_effects=True, vmem_limit_bytes=62 << 20
+            collective_id=0, has_side_effects=True, vmem_limit_bytes=63 << 20
         ),
         cost_estimate=pl.CostEstimate(
             flops=6 * 2048 * D * 512, bytes_accessed=24 << 20, transcendentals=1 << 20
@@ -810,7 +972,7 @@
         state_write[0, :, 0],
         state_read[0, :, 0],
         decay_rate[0],
-        skip_gain,
+        skip_gain[None],
         norm_gain[None],
         start_state[0].reshape(HEADS * SIZE, STATE),
         out_weight.reshape(SIDE, SIDE, PIECE, D),

time: 223 us -> 212 us (0.951)
  Pallas kernels: 221 us -> 209 us
    pallas_call x1, Pallas kernels: 221 us -> 209 us  [layer(): pl.pallas_call(layer_kernel, out_shape=jax.ShapeDtypeStruct((TOKENS, D),...]
where the time goes in v6:
time: 212 us; the launch traced here: 211 us
  Pallas kernels  209 us (99%)
    pallas_call x1, Pallas kernels, layer(): pl.pallas_call(layer_kernel, out_shape=jax.ShapeDtypeStruct((TOKENS, D),...  209 us

profile of v6, /device:TPU:1, one launch (start us, length us, event | category | flops | bytes accessed | tf_op | source)
XLA Modules:
  0.0 211.3 jit_solution(1801711411798988399)
XLA Ops:
  0.0 209.5 %shard_map.163 = bf16[64,4096]{1,0:T(8,128)(2,1)} custom-call(bf16[256,1024]{1,0:T(8,128)(2,1)} %bitcast.29, bf16[256,1024]{1,0:T(8,128)(2,1)} %bitcast.30, bf16[256,128]{1,0:T(8,128)(2,1)} %bitcast.33, bf16[256,128]{1,0:T(8,128)(2,1)} %bitcast.34, f32[16,256]{1,0:T(8,128)} %bitcast.36, f32[1,16]{1,0:T(1,128)} %bitcast.41, f32[1,1024]{1,0:T(1,128)} %bitcast.37, ...), custom_call_target="tpu_custom_call" | custom-call | flops 25769803776 | bytes 25165824 | tf_op jit(solution)/shard_map/pallas_call | solution.py:873
  209.5 1.9 copy.19

commit v7 on v6

--- a/solution.py
+++ b/solution.py
@@ -29,8 +29,10 @@
 MESSAGE = SIZE + 16
 EARLY = 3
 APART = QUADS - 1
-ROUNDS = 2 * APART + 1
+ROUNDS = 2 * (QUADS - 1) + 1
 SUMS = 10
+SPREAD, SPREAD_LATER = 5, 2
+DONE = (9, 13)
 LAST = 7
 MESH = pl.DeviceIdType.MESH
 
@@ -92,6 +94,7 @@
     line,
     apart,
     weights,
+    placings,
     ag_send,
     ag_recv,
     rs_send,
@@ -106,6 +109,10 @@
     apart_recv,
     weight_send,
     weight_recv,
+    placing_send,
+    placing_recv,
+    spread_send,
+    spread_recv,
     ready,
     load_sem,
     mix_sem,
@@ -327,7 +334,9 @@
         ),
     )
     places = [place_id == target[i : i + 1, :] for i in range(2)]
-    placing[...] = (places[0].astype(f32) + places[1].astype(f32)).astype(bf16)
+    place = places[0].astype(f32) + places[1].astype(f32)
+    placing[...] = place.astype(bf16)
+    placings[here] = place.T.astype(bf16)
     logits[...] = jnp.zeros_like(logits)
     acc[...] = jnp.zeros_like(acc)
 
@@ -409,7 +418,7 @@
             place,
         )
 
-    def tokens(c):
+    def tokens(c, by_token=False):
         for t in range(2):
             q = 2 * c + t
             columns = columns_of(q)
@@ -420,12 +429,21 @@
                 total = total + term(q, i)[...].astype(f32)
             value = (residual[:, columns].astype(f32) + total).astype(bf16)
             hidden[:, columns] = value
-            rows = jnp.dot(placing[...], value, preferred_element_type=f32).astype(bf16)
-            leaving[lax.rem(c, 2), t] = rows.reshape(EXPERTS, BLOCK, WIDTH)
-            for o in range(1, EXPERTS):
-                row_copy(c, t, o).start()
-            k = 2 * (my_dp * QUADS + c) + t
-            xg[k, my["z"], my["x"], rows_of(my_exp, BLOCK)] = leaving[lax.rem(c, 2), t, owner]
+            if by_token:
+                apart[t, my["z"], my["x"]] = value
+                for d in (1, -1):
+                    ag_copy(c, t, 0, d, False, by_token=True).start()
+                for d in (1, -1):
+                    ag_copy(c, t, 2, d, False, by_token=True).start()
+            else:
+                rows = jnp.dot(placing[...], value, preferred_element_type=f32).astype(bf16)
+                leaving[lax.rem(c, 2), t] = rows.reshape(EXPERTS, BLOCK, WIDTH)
+                for o in range(1, EXPERTS):
+                    row_copy(c, t, o).start()
+                k = 2 * (my_dp * QUADS + c) + t
+                xg[k, my["z"], my["x"], rows_of(my_exp, BLOCK)] = leaving[
+                    lax.rem(c, 2), t, owner
+                ]
             logits[...] += lax.dot_general(
                 router[:, columns],
                 value,
@@ -442,9 +460,12 @@
             remote(ref, ref, row_send.at[2 * c + t], row_recv.at[0], partner(1)[1]).wait_send()
 
 
-    def ag_copy(j, t, step, d, landing, off=0):
+    def pair_of(j):
+        return j + lax.div(j - 1, QUADS - 1)
+
+    def ag_copy(j, t, step, d, landing, off=0, by_token=False):
         near, far = axes[t]
-        chunk = xg.at[2 * j + t]
+        chunk = apart.at[t] if by_token else xg.at[2 * pair_of(j) + t]
         back = -d if landing else 0
         if step == 0:
             ref, to = along(near, chunk, around(near, back), my[far]), near
@@ -461,14 +482,15 @@
         m = step * 2 + slot[d]
         return remote(ref, ref, ag_send.at[j, t, m], ag_recv.at[j, t, m], neighbour(to, d))
 
-    def ag_arrive(j, step):
+    def ag_arrive(j, step, by_token):
         for t, d in both:
-            ag_copy(j, t, step, d, True, None).wait_recv()
+            ag_copy(j, t, step, d, True, None, by_token).wait_recv()
 
     def gather_first(j):
-        mine = my_dp == lax.div(j, QUADS)
-        for t in range(2):
-            k = 2 * j + t
+        pair = pair_of(j)
+        mine = my_dp == lax.div(pair, QUADS)
+        for t in range(2):
+            k = 2 * pair + t
 
             def arrive(count):
                 ref = xg.at[k, my["z"], my["x"], pl.ds(0, count)]
@@ -481,37 +503,31 @@
         for t, d in both:
             ag_copy(j, t, 2, d, False, 0).start()
 
-    def gather_second(j):
-        ag_arrive(j, 0)
+    def gather_second(j, by_token=False):
+        ag_arrive(j, 0, by_token)
         for t, d in both:
-            ag_copy(j, t, 1, d, False).start()
+            ag_copy(j, t, 1, d, False, 0, by_token).start()
         for t, d in both:
             for off in (1, -1):
-                ag_copy(j, t, 2, d, False, off).start()
-
-    def gather_third(j):
-        ag_arrive(j, 1)
+                ag_copy(j, t, 2, d, False, off, by_token).start()
+
+    def gather_third(j, by_token=False):
+        ag_arrive(j, 1, by_token)
         for t, d in both:
-            ag_copy(j, t, 2, d, False, 2).start()
-
-    def gather_last(j):
-        ag_arrive(j, 2)
+            ag_copy(j, t, 2, d, False, 2, by_token).start()
+
+    def gather_last(j, by_token=False):
+        ag_arrive(j, 2, by_token)
         for t, d in both:
-            ag_copy(j, t, 3, d, False).start()
-
-    def gathered(j):
-        h = lax.div(j, QUADS)
-        c = lax.rem(j, QUADS)
-        ag_arrive(j, 3)
+            ag_copy(j, t, 3, d, False, 0, by_token).start()
+
+    def gather_done(j, by_token=False):
+        ag_arrive(j, 3, by_token)
         for step in range(4):
             for t, d in both:
-                ag_copy(j, t, step, d, False, None).wait_send()
-
-        @pl.when(j == 0)
-        def _():
-            for load in loads:
-                load.wait()
-
+                ag_copy(j, t, step, d, False, None, by_token).wait_send()
+
+    def multiply(h, c):
         @pl.loop(0, 2)
         def _(b):
             rows = rows_of(h * 2 + b, PLANE // 2)
@@ -519,28 +535,104 @@
                 total = acc[n, rows, :]
                 for t in range(2):
                     total += jnp.dot(
-                        xg[2 * j + t, pl.ds(b * 2, 2)].reshape(PLANE // 2, WIDTH),
+                        xg[2 * (h * QUADS + c) + t, pl.ds(b * 2, 2)].reshape(PLANE // 2, WIDTH),
                         weight[columns_of(2 * c + t), :],
                         preferred_element_type=f32,
                     )
                 acc[n, rows, :] = total
 
+    def gathered(j):
+        gather_done(j)
+
+        @pl.when(j == 1)
+        def _():
+            for load in loads:
+                load.wait()
+
+        multiply(lax.div(j - 1, QUADS - 1), lax.rem(j - 1, QUADS - 1) + 1)
+
         @pl.when(j == QUADS - 1)
         def _():
             for o in range(1, EXPERTS):
                 pl.semaphore_signal(ready, inc=1, device_id=partner(o)[1], device_id_type=MESH)
 
-        @pl.when(c == QUADS - 1)
-        def _():
-            @pl.loop(0, 8)
-            def _(b):
-                rows = rows_of(h * 8 + b, PLANE // 8)
-                gate = acc[0, rows, :]
-                act[rows, :] = (gate / (1.0 + jnp.exp(-gate)) * acc[1, rows, :]).astype(bf16)
+
+    def placing_copy(k):
+        other = lax.rem(here + k, CTX)
+        return remote(
+            placings.at[here],
+            placings.at[here],
+            placing_send.at[k],
+            placing_recv.at[k],
+            {"ctx": other},
+        )
+
+    def spread_room(t, e):
+        return part.at[2 + t, lax.div(e, SIDE), lax.rem(e, SIDE)]
+
+    def spread_copy(t, o, x):
+        other, place = partner(o)
+        return remote(
+            spread_room(t, other).at[:, pl.ds(x * BLOCK, BLOCK)],
+            xg.at[2 * my_dp * QUADS + t, :, x, rows_of(my_exp, BLOCK)],
+            spread_send.at[t],
+            spread_recv.at[2 * my_dp + t],
+            place,
+        )
+
+    def spread_rows():
+        each(lambda k: placing_copy(k).wait_recv())
+        for t in range(2):
+
+            @pl.loop(0, SIDE)
+            def _(z):
+                for x in range(SIDE):
+                    rows = lax.dot_general(
+                        placings[z * SIDE + x],
+                        apart[t, z, x],
+                        (((0,), (0,)), ((), ())),
+                        preferred_element_type=f32,
+                    ).astype(bf16)
+                    for e in range(EXPERTS):
+                        part[2 + t, e // SIDE, e % SIDE, z, x * BLOCK : (x + 1) * BLOCK] = rows[
+                            e * BLOCK : (e + 1) * BLOCK
+                        ]
+
+            for o in range(1, EXPERTS):
+                for x in range(SIDE):
+                    spread_copy(t, o, x).start()
+            for x in range(SIDE):
+                xg[2 * my_dp * QUADS + t, :, x, rows_of(my_exp, BLOCK)] = spread_room(t, owner)[
+                    :, x * BLOCK : (x + 1) * BLOCK
+                ]
+
+    def spread_sent():
+        for t in range(2):
+            ref = pool.at[pl.ds(0, EXPERTS - 1)]
+            remote(ref, ref, spread_send.at[t], spread_recv.at[0], partner(1)[1]).wait_send()
+
+    def rows_done(h):
+        for t in range(2):
+
+            def arrive(count):
+                ref = pool.at[pl.ds(0, count)]
+                remote(
+                    ref, ref, spread_send.at[0], spread_recv.at[2 * h + t], partner(1)[1]
+                ).wait_recv()
+
+            pl.when(my_dp == h)(functools.partial(arrive, GROUPS - 1))
+            pl.when(my_dp != h)(functools.partial(arrive, GROUPS))
+        multiply(h, 0)
+
+        @pl.loop(0, 8)
+        def _(b):
+            rows = rows_of(h * 8 + b, PLANE // 8)
+            gate = acc[0, rows, :]
+            act[rows, :] = (gate / (1.0 + jnp.exp(-gate)) * acc[1, rows, :]).astype(bf16)
 
 
     def room_of(j, t):
-        pair = j + lax.div(j, APART) - lax.div(j, 2 * APART)
+        pair = lax.div(j, APART) * QUADS + lax.rem(j + 1, APART) - 2 * lax.div(j, 2 * APART)
         return xg.at[2 * pair + t]
 
     def rs_copy(j, t, step, d):
@@ -842,18 +934,37 @@
                 functools.partial(action, tick - lag)
             )
 
+    each(lambda k: placing_copy(k).start())
+
+    def later(action):
+        return lambda j: action(j + 1)
+
     @pl.loop(0, 1 + SUMS + ROUNDS + LAST)
     def _(turn):
         tick = turn - 1
-        own = tick - my_dp * QUADS
-        stages(
-            tick,
-            PAIRS,
-            ((5, gather_last), (4, gather_third), (3, gather_second), (2, gather_first)),
-        )
+        own = tick - my_dp * (QUADS - 1)
+
+        def first(when, action):
+            pl.when(tick == when)(functools.partial(action, tick - when, True))
+
+        first(4, gather_last)
+        stages(tick - 1, 2 * QUADS - 2, ((5, later(gather_last)),))
+        first(3, gather_third)
+        stages(tick - 1, 2 * QUADS - 2, ((4, later(gather_third)),))
+        first(2, gather_second)
+        stages(tick - 1, 2 * QUADS - 2, ((3, later(gather_second)), (2, later(gather_first))))
         stages(tick - SUMS, ROUNDS, ((4, sum_second), (2, sum_first)))
-        stages(own, QUADS, ((3, rows_sent), (1, tokens), (-1, mix)))
-        stages(tick, PAIRS, ((6, gathered),))
+        stages(own - 1, QUADS - 1, ((3, later(rows_sent)),))
+        first(1, tokens)
+        stages(own - 1, QUADS - 1, ((1, later(tokens)),))
+        stages(tick, 1, ((-1, mix),))
+        stages(own - 1, QUADS - 1, ((-1, later(mix)),))
+        first(5, gather_done)
+        pl.when(tick == SPREAD + SPREAD_LATER * my_dp)(spread_rows)
+        stages(tick - 1, 2 * QUADS - 2, ((6, later(gathered)),))
+        pl.when(tick == SUMS + 2)(spread_sent)
+        for h in range(2):
+            pl.when(tick == DONE[h])(functools.partial(rows_done, h))
         pl.when(tick == SUMS)(weigh)
         stages(tick - SUMS, ROUNDS, ((0, sum_start), (5, sum_third), (6, sum_last)))
         stages(tick - SUMS, 2 * APART, ((7, sum_back),))
@@ -862,6 +973,7 @@
 
     apart_sent(1)
     each(lambda k: weight_copy(k).wait_send())
+    each(lambda k: placing_copy(k).wait_send())
     for q in range(2 * QUADS):
         out_store(q).wait()
 
@@ -914,6 +1026,7 @@
             pltpu.VMEM((4, 2, SIDE, PIECE, WIDTH), bf16),
             pltpu.VMEM((2, GROUPS, SIDE, PIECE, WIDTH), bf16),
             pltpu.VMEM((CTX, TOKENS, EXPERTS * BLOCK), bf16),
+            pltpu.VMEM((CTX, TOKENS, EXPERTS * BLOCK), bf16),
             pltpu.SemaphoreType.DMA((PAIRS, 2, 8)),
             pltpu.SemaphoreType.DMA((PAIRS, 2, 8)),
             pltpu.SemaphoreType.DMA((PAIRS, 2, 8)),
@@ -928,6 +1041,10 @@
             pltpu.SemaphoreType.DMA((2,)),
             pltpu.SemaphoreType.DMA((CTX,)),
             pltpu.SemaphoreType.DMA((CTX,)),
+            pltpu.SemaphoreType.DMA((CTX,)),
+            pltpu.SemaphoreType.DMA((CTX,)),
+            pltpu.SemaphoreType.DMA((2,)),
+            pltpu.SemaphoreType.DMA((4,)),
             pltpu.SemaphoreType.REGULAR,
             pltpu.SemaphoreType.DMA((3,)),
             pltpu.SemaphoreType.DMA((2 * QUADS,)),

time: 212 us -> 198 us (0.934)
  Pallas kernels: 209 us -> 196 us
    pallas_call x1, Pallas kernels: 209 us -> 196 us  [layer(): pl.pallas_call(layer_kernel, out_shape=jax.ShapeDtypeStruct((TOKENS, D),...]
where the time goes in v7:
time: 198 us
  Pallas kernels  196 us (99%)
    pallas_call x1, Pallas kernels, layer(): pl.pallas_call(layer_kernel, out_shape=jax.ShapeDtypeStruct((TOKENS, D),...  196 us

profile of v7, /device:TPU:1, one launch (start us, length us, event | category | flops | bytes accessed | tf_op | source)
XLA Modules:
  0.0 198.1 jit_solution(480773852577487298)
XLA Ops:
  0.0 196.2 %shard_map.163 = bf16[64,4096]{1,0:T(8,128)(2,1)} custom-call(bf16[256,1024]{1,0:T(8,128)(2,1)} %bitcast.29, bf16[256,1024]{1,0:T(8,128)(2,1)} %bitcast.30, bf16[256,128]{1,0:T(8,128)(2,1)} %bitcast.33, bf16[256,128]{1,0:T(8,128)(2,1)} %bitcast.34, f32[16,256]{1,0:T(8,128)} %bitcast.36, f32[1,16]{1,0:T(1,128)} %bitcast.41, f32[1,1024]{1,0:T(1,128)} %bitcast.37, ...), custom_call_target="tpu_custom_call" | custom-call | flops 25769803776 | bytes 25165824 | tf_op jit(solution)/shard_map/pallas_call | solution.py:985
  196.2 1.9 copy.19

commit v8 on v7

--- a/solution.py
+++ b/solution.py
@@ -305,15 +305,20 @@
 
 
     inputs["start"].wait()
-    each(lambda k: out_copy(k).wait_recv())
     state = start[...]
     for k in range(CTX):
         entering[k] = state.astype(bf16)
+        behind = lax.rem(here - k + CTX, CTX)
+
+        @pl.when(behind != 0)
+        def _():
+            in_copy(lax.rem(k - here + CTX, CTX)).start()
+            out_copy(behind).wait_recv()
+
         if k < CTX - 1:
             factor = gathered_states[k, SIZE:MESSAGE].astype(f32)
             factor = factor[0:1, :] + factor[8:9, :]
             state = factor * state + gathered_states[k, 0:SIZE].astype(f32)
-    each(lambda k: in_copy(k).start())
     entered[here] = entering[here]
 
     for q in range(EARLY, HEADS // 2):
@@ -482,10 +487,6 @@
         m = step * 2 + slot[d]
         return remote(ref, ref, ag_send.at[j, t, m], ag_recv.at[j, t, m], neighbour(to, d))
 
-    def ag_arrive(j, step, by_token):
-        for t, d in both:
-            ag_copy(j, t, step, d, True, None, by_token).wait_recv()
-
     def gather_first(j):
         pair = pair_of(j)
         mine = my_dp == lax.div(pair, QUADS)
@@ -498,31 +499,32 @@
 
             pl.when(mine)(functools.partial(arrive, PIECE - BLOCK))
             pl.when(jnp.logical_not(mine))(functools.partial(arrive, PIECE))
+            for step in (0, 2):
+                for d in (1, -1):
+                    ag_copy(j, t, step, d, False).start()
+
+    def gather_second(j, by_token=False):
+        for t, d in both:
+            ag_copy(j, t, 0, d, True, None, by_token).wait_recv()
+            ag_copy(j, t, 1, d, False, 0, by_token).start()
+            for e in (1, -1):
+                ag_copy(j, t, 2, e, False, -d, by_token).start()
+
+    def gather_third(j, by_token=False):
+        for t in range(2):
             for d in (1, -1):
-                ag_copy(j, t, 0, d, False).start()
+                ag_copy(j, t, 1, d, True, None, by_token).wait_recv()
+            for d in (1, -1):
+                ag_copy(j, t, 2, d, False, 2, by_token).start()
+
+    def gather_last(j, by_token=False):
         for t, d in both:
-            ag_copy(j, t, 2, d, False, 0).start()
-
-    def gather_second(j, by_token=False):
-        ag_arrive(j, 0, by_token)
+            ag_copy(j, t, 2, d, True, None, by_token).wait_recv()
+            ag_copy(j, t, 3, d, False, 0, by_token).start()
+
+    def gather_done(j, by_token=False):
         for t, d in both:
-            ag_copy(j, t, 1, d, False, 0, by_token).start()
-        for t, d in both:
-            for off in (1, -1):
-                ag_copy(j, t, 2, d, False, off, by_token).start()
-
-    def gather_third(j, by_token=False):
-        ag_arrive(j, 1, by_token)
-        for t, d in both:
-            ag_copy(j, t, 2, d, False, 2, by_token).start()
-
-    def gather_last(j, by_token=False):
-        ag_arrive(j, 2, by_token)
-        for t, d in both:
-            ag_copy(j, t, 3, d, False, 0, by_token).start()
-
-    def gather_done(j, by_token=False):
-        ag_arrive(j, 3, by_token)
+            ag_copy(j, t, 3, d, True, None, by_token).wait_recv()
         for step in range(4):
             for t, d in both:
                 ag_copy(j, t, step, d, False, None, by_token).wait_send()
@@ -784,22 +786,21 @@
 
     def sum_first(j):
         s = lax.rem(j, 4)
-        for t in range(2):
+        for t, d in both:
             far = axes[t][1]
-            rs_arrive(j, 0, t)
-            for d in (1, -1):
-                base = 0 if d == 1 else SIDE // 2
-                place = around(far, d)
-
-                @pl.loop(0, SIDE // 2)
-                def _(i):
-                    at = (place, base + i) if far == "z" else (base + i, place)
-                    part[s, t, at[0], at[1]] = (
-                        part[s, t, at[0], at[1]].astype(f32)
-                        + room_of(j, t)[0, base + i].astype(f32)
-                    ).astype(bf16)
-
-            rs_start(j, 1, t)
+            base = 0 if d == 1 else SIDE // 2
+            place = around(far, d)
+            rs_copy(j, t, 0, d).wait_recv()
+
+            @pl.loop(0, SIDE // 2)
+            def _(i):
+                at = (place, base + i) if far == "z" else (base + i, place)
+                part[s, t, at[0], at[1]] = (
+                    part[s, t, at[0], at[1]].astype(f32)
+                    + room_of(j, t)[0, base + i].astype(f32)
+                ).astype(bf16)
+
+            rs_copy(j, t, 1, d).start()
 
     def sum_second(j):
         s = lax.rem(j, 4)
@@ -821,15 +822,14 @@
 
     def sum_third(j):
         s = lax.rem(j, 4)
-        for t in range(2):
-            rs_arrive(j, 2, t)
-            for d in (1, -1):
-                at = around(axes[t][0], d)
-                line[s, t, at, half_rows[d]] = (
-                    line[s, t, at, half_rows[d]].astype(f32)
-                    + room_of(j, t)[3, 0, half_rows[d]].astype(f32)
-                ).astype(bf16)
-            rs_start(j, 3, t)
+        for t, d in both:
+            at = around(axes[t][0], d)
+            rs_copy(j, t, 2, d).wait_recv()
+            line[s, t, at, half_rows[d]] = (
+                line[s, t, at, half_rows[d]].astype(f32)
+                + room_of(j, t)[3, 0, half_rows[d]].astype(f32)
+            ).astype(bf16)
+            rs_copy(j, t, 3, d).start()
 
 
     def back_copy(j, t, o):

time: 198 us -> 198 us (level)
  no operation moved by 1% of the time
where the time goes in v8:
time: 198 us
  Pallas kernels  196 us (99%)
    pallas_call x1, Pallas kernels, layer(): pl.pallas_call(layer_kernel, out_shape=jax.ShapeDtypeStruct((TOKENS, D),...  196 us

profile of v8, /device:TPU:1, one launch (start us, length us, event | category | flops | bytes accessed | tf_op | source)
XLA Modules:
  0.0 197.6 jit_solution(7648179979366602056)
XLA Ops:
  0.0 195.7 %shard_map.163 = bf16[64,4096]{1,0:T(8,128)(2,1)} custom-call(bf16[256,1024]{1,0:T(8,128)(2,1)} %bitcast.29, bf16[256,1024]{1,0:T(8,128)(2,1)} %bitcast.30, bf16[256,128]{1,0:T(8,128)(2,1)} %bitcast.33, bf16[256,128]{1,0:T(8,128)(2,1)} %bitcast.34, f32[16,256]{1,0:T(8,128)} %bitcast.36, f32[1,16]{1,0:T(1,128)} %bitcast.41, f32[1,1024]{1,0:T(1,128)} %bitcast.37, ...), custom_call_target="tpu_custom_call" | custom-call | flops 25769803776 | bytes 25165824 | tf_op jit(solution)/shard_map/pallas_call | solution.py:985
  195.7 1.9 copy.19
